TPU v7x, 512 devices: a whole 4x4x16 slice. The times are simulated.
512 devices in a mesh: seq: 128 (over y, z, x_lo), head: 4 (over x_hi, core).
Axes of the slice: x: 4 (x_hi: 2, x_lo: 2; x = x_hi * 2 + x_lo), y: 4, z: 16, core: 2. Of those that a mesh axis runs over, the one named last changes fastest.
Arguments:
- self_query: bfloat16 [32768, 1536], P('seq', 'head'), may hold values from -12 to 12
- self_key: bfloat16 [32768, 1536], P('seq', 'head'), may hold values from -12 to 12
- self_value: bfloat16 [32768, 1536], P('seq', 'head'), may hold values from -6 to 6
- cross_query: bfloat16 [32768, 1536], P('seq', 'head'), may hold values from -12 to 12
- cross_key: bfloat16 [32768, 1536], P('seq', 'head'), may hold values from -12 to 12
- cross_value: bfloat16 [32768, 1536], P('seq', 'head'), may hold values from -6 to 6
- cotangent: bfloat16 [32768, 1536], P('seq', 'head'), may hold values from -6 to 6
- norm_gains: float32 [2, 4, 1536], P(None, None, 'head'), may hold values from 0.65 to 1.9
- cross_span: int32 [384, 2], replicated, may hold values from 0 to 4, as said below
Outputs:
- attention_out: bfloat16 [32768, 1536], P('seq', 'head')
- self_query_grad: bfloat16 [32768, 1536], P('seq', 'head')
- self_key_grad: bfloat16 [32768, 1536], P('seq', 'head')
- self_value_grad: bfloat16 [32768, 1536], P('seq', 'head')
- cross_query_grad: bfloat16 [32768, 1536], P('seq', 'head')
- cross_key_grad: bfloat16 [32768, 1536], P('seq', 'head')
- cross_value_grad: bfloat16 [32768, 1536], P('seq', 'head')
Inputs may be any that keep to these rules, and one draw needn't show every extreme that they name: `cross_span`: row b gives a range lo to hi of 64-token blocks inside the audio block aligned in time with video block b // 4; always lo <= b % 4 < hi.
All inputs are finite; a program needn't handle non-finite values.
Results may differ from a plain program's by a relative error of at most 0.013.
The roundings to bfloat16 on the way count: a program that leaves them out, or rounds other values in their place, can miss the bound.
Values may be sent and summed in bfloat16 or wider, within the bound.
No kernel may reach another device: no remote copies, remote signals or barrier semaphores. Data moves between devices by JAX's collectives and lax.ppermute only.
A program may use at most 64 MiB of HBM per device.

v0:
```python
import jax
import jax.numpy as jnp
from jax import lax
from jax.sharding import PartitionSpec as P

DH = 128
BLK = 64
REACH = 1
WIDTH = 1536
NSUB = 4


EPSILON = 1e-06


def shifted_2(value, axis, steps):
    count = lax.axis_size(axis)
    first, last = (max(0, -steps), min(count, count - steps))
    return lax.ppermute(value, axis, [(source, source + steps) for source in range(first, last)])


def shifted_3(block, axis, distance):
    devices = range(lax.axis_size(axis))
    route = [((i - distance) % len(devices), i) for i in devices]
    return lax.ppermute(block, axis, route)


def split_heads(tensor):
    return tensor.reshape(tensor.shape[0], tensor.shape[1] // DH, DH)


def query_side(queries, keys, values, upstream, allowed):
    tok_rows = queries.shape[0]
    scores = jnp.einsum(
        "qhd,khd->hqk", split_heads(queries), split_heads(keys), preferred_element_type=jnp.float32
    ) * DH ** (-0.5)
    scores = jnp.where(allowed[None], scores, -jnp.inf)
    row_max = jnp.max(scores, axis=2)
    shifted = jnp.exp(scores - row_max[:, :, None])
    row_total = jnp.sum(shifted, axis=2)
    soft_probs = shifted / row_total[:, :, None]
    weights = soft_probs.astype(jnp.bfloat16)
    value_heads = split_heads(values)
    grad_heads = split_heads(upstream)
    result = jnp.einsum(
        "hqk,khd->qhd", weights, value_heads, preferred_element_type=jnp.float32
    ).reshape(tok_rows, -1)
    prob_grad = jnp.einsum(
        "qhd,khd->hqk", grad_heads, value_heads, preferred_element_type=jnp.float32
    )
    row_delta = jnp.sum(soft_probs * prob_grad, axis=2)
    score_grad = (soft_probs * (prob_grad - row_delta[:, :, None]) * DH ** (-0.5)).astype(
        jnp.bfloat16
    )
    query_grad = jnp.einsum(
        "hqk,khd->qhd", score_grad, split_heads(keys), preferred_element_type=jnp.float32
    ).reshape(tok_rows, -1)
    key_grad = jnp.einsum(
        "hqk,qhd->khd", score_grad, split_heads(queries), preferred_element_type=jnp.float32
    ).reshape(keys.shape[0], -1)
    value_grad = jnp.einsum(
        "hqk,qhd->khd", weights, grad_heads, preferred_element_type=jnp.float32
    ).reshape(keys.shape[0], -1)
    return (result, query_grad, key_grad, value_grad)


def cross_mask(my_index, receipt, cross_span, quarter):
    my_group = my_index // quarter
    sender_device = (my_index - receipt * quarter) % (4 * quarter)
    own_span = lax.dynamic_slice_in_dim(
        cross_span, jnp.minimum(my_index, 3 * quarter - 1) * NSUB, NSUB, 0
    )
    their_span = lax.dynamic_slice_in_dim(
        cross_span, jnp.minimum(sender_device, 3 * quarter - 1) * NSUB, NSUB, 0
    )
    sub_index = jnp.arange(NSUB * BLK, dtype=jnp.int32) // BLK
    own_lower = jnp.repeat(own_span[:, 0], BLK)[:, None]
    own_upper = jnp.repeat(own_span[:, 1], BLK)[:, None]
    their_lower = jnp.repeat(their_span[:, 0], BLK)[None, :]
    their_upper = jnp.repeat(their_span[:, 1], BLK)[None, :]
    video_side = (
        (my_group < 3)
        & (sender_device // quarter == 3)
        & (own_lower <= sub_index[None, :])
        & (sub_index[None, :] < own_upper)
    )
    audio_side = (
        (my_group == 3)
        & (sender_device // quarter < 3)
        & (their_lower <= sub_index[:, None])
        & (sub_index[:, None] < their_upper)
    )
    return video_side | audio_side


def on_device(
    self_query,
    self_key,
    self_value,
    cross_query,
    cross_key,
    cross_value,
    cotangent,
    norm_gains,
    cross_span,
):
    seq_count = lax.axis_size("seq")
    quarter = seq_count // 4
    my_index = lax.axis_index("seq")
    my_group = my_index // quarter
    gain_rows = jnp.where(my_group == 3, norm_gains[1], norm_gains[0])
    inputs = (self_query, self_key, cross_query, cross_key)
    squares = jnp.stack(
        [jnp.sum(jnp.square(tensor.astype(jnp.float32)), axis=1) for tensor in inputs]
    )
    squares = lax.psum(squares, "head")
    inv_rms = lax.rsqrt(squares / WIDTH + EPSILON)
    normed = [
        (
            inputs[which].astype(jnp.float32) * inv_rms[which][:, None] * gain_rows[which][None, :]
        ).astype(jnp.bfloat16)
        for which in range(4)
    ]
    tok_rows = self_query.shape[0]
    columns = self_query.shape[1]
    offsets = list(range(-REACH, REACH + 1))
    local_pair = jnp.stack([normed[1], self_value])
    key_blocks = []
    value_blocks = []
    slot_valid = []
    for offset in offsets:
        if offset == 0:
            arrived = local_pair
        else:
            arrived = shifted_2(local_pair, "seq", -offset)
        key_blocks.append(arrived[0])
        value_blocks.append(arrived[1])
        receiver_device = my_index + offset
        slot_valid.append(
            (receiver_device >= 0)
            & (receiver_device < seq_count)
            & (receiver_device // quarter == my_group)
        )
    allowed = jnp.broadcast_to(
        jnp.repeat(jnp.stack(slot_valid), tok_rows)[None, :], (tok_rows, len(offsets) * tok_rows)
    )
    self_out, self_qgrad, self_kparts, self_value_pieces = query_side(
        normed[0], jnp.concatenate(key_blocks), jnp.concatenate(value_blocks), cotangent, allowed
    )
    self_kgrad = jnp.zeros((tok_rows, columns), jnp.float32)
    self_vgrad = jnp.zeros((tok_rows, columns), jnp.float32)
    for position_index, offset in enumerate(offsets):
        partial_value = jnp.stack(
            [
                self_kparts[position_index * tok_rows : (position_index + 1) * tok_rows],
                self_value_pieces[position_index * tok_rows : (position_index + 1) * tok_rows],
            ]
        )
        if offset == 0:
            returned = partial_value
        else:
            returned = shifted_2(partial_value.astype(jnp.bfloat16), "seq", offset).astype(
                partial_value.dtype
            )
        self_kgrad = self_kgrad + returned[0]
        self_vgrad = self_vgrad + returned[1]
    local_cross = jnp.stack([normed[3], cross_value])
    receipts = []
    for receipt in range(1, 4):
        receipts.append(shifted_3(local_cross, "seq", receipt * quarter))
    cross_allowed = jnp.concatenate(
        [cross_mask(my_index, receipt, cross_span, quarter) for receipt in range(1, 4)], axis=1
    )
    cross_keys = jnp.concatenate([arrived[0] for arrived in receipts])
    cross_values = jnp.concatenate([arrived[1] for arrived in receipts])
    cross_out, cross_qgrad, cross_kparts, cross_value_pieces = query_side(
        normed[2], cross_keys, cross_values, cotangent, cross_allowed
    )
    partials = [
        jnp.stack(
            [
                cross_kparts[receipt * tok_rows : (receipt + 1) * tok_rows],
                cross_value_pieces[receipt * tok_rows : (receipt + 1) * tok_rows],
            ]
        )
        for receipt in range(3)
    ]
    cross_back = jnp.zeros((2, tok_rows, columns), jnp.float32)
    for receipt in range(1, 4):
        cross_back = cross_back + shifted_3(
            partials[receipt - 1].astype(jnp.bfloat16), "seq", -receipt * quarter
        ).astype(jnp.float32)
    upstream = (self_qgrad, self_kgrad, cross_qgrad, cross_back[0])
    inner = jnp.stack(
        [
            jnp.sum(
                gain_rows[which][None, :] * upstream[which] * inputs[which].astype(jnp.float32),
                axis=1,
            )
            for which in range(4)
        ]
    )
    inner = lax.psum(inner, "head")
    results = []
    for which in range(4):
        scale_rows = inv_rms[which][:, None]
        wide = inputs[which].astype(jnp.float32)
        results.append(
            (
                scale_rows * gain_rows[which][None, :] * upstream[which]
                - wide * (inv_rms[which] ** 3 * (inner[which] / WIDTH))[:, None]
            ).astype(jnp.bfloat16)
        )
    attention_out = (self_out + cross_out).astype(jnp.bfloat16)
    return (
        attention_out,
        results[0],
        results[1],
        self_vgrad.astype(jnp.bfloat16),
        results[2],
        results[3],
        cross_back[1].astype(jnp.bfloat16),
    )


def solution(mesh):
    in_specs = (
        P("seq", "head"),
        P("seq", "head"),
        P("seq", "head"),
        P("seq", "head"),
        P("seq", "head"),
        P("seq", "head"),
        P("seq", "head"),
        P(None, None, "head"),
        P(),
    )
    out_specs = (
        P("seq", "head"),
        P("seq", "head"),
        P("seq", "head"),
        P("seq", "head"),
        P("seq", "head"),
        P("seq", "head"),
        P("seq", "head"),
    )
    return jax.shard_map(
        on_device, mesh=mesh, in_specs=in_specs, out_specs=out_specs, check_vma=False
    )
```

profile of v0, /device:TPU:8, one launch (start us, length us, event | category | flops | bytes accessed | tf_op | source)
XLA Modules:
  0.0 181.6 jit_solution(3175331343803873993)
XLA Ops:
  6.1 10.1 %psum.14 = f32[4,256]{1,0:T(4,128)S(1)} all-reduce(f32[4,256]{1,0:T(4,128)S(1)} %pad_maximum_fusion.27), channel_id=1, replica_groups=mesh['seq'=128,'head'=4] {'head'}, use_global_device_ids=true, to_apply=%region_4.5 | all-reduce | flops 1024 | bytes 8192 | tf_op jit(solution)/shard_map/psum | solution.py:116
  18.0 11.3 %collective-permute-start.1 = (bf16[2,256,384]{1,2,0:T(8,128)(2,1)}, bf16[2,256,384]{1,2,0:T(8,128)(2,1)}, u32[]{:S(2)}, u32[]{:S(2)}) collective-permute-start(bf16[2,256,384]{1,2,0:T(8,128)(2,1)} %pad_maximum_fusion.4), channel_id=1, source_target_pairs={{4,0},{8,4},{12,8},{16,12},{20,16},{24,20},{28,24},{32,28},{36,32}... | collective-permute-start | bytes 1179656 | tf_op jit(solution)/shard_map/ppermute | solution.py:19
  29.3 1.9 %collective-permute-start = (bf16[2,256,384]{1,2,0:T(8,128)(2,1)}, bf16[2,256,384]{1,2,0:T(8,128)(2,1)}, u32[]{:S(2)}, u32[]{:S(2)}) collective-permute-start(bf16[2,256,384]{1,2,0:T(8,128)(2,1)} %pad_maximum_fusion.4), channel_id=1, source_target_pairs={{0,4},{4,8},{8,12},{12,16},{16,20},{20,24},{24,28},{28,32},{32,36}... | collective-permute-start | bytes 1179656 | tf_op jit(solution)/shard_map/ppermute | solution.py:19
  31.6 1.9 %collective-permute-start.4 = (bf16[2,256,384]{1,2,0:T(8,128)(2,1)S(1)}, bf16[2,256,384]{1,2,0:T(8,128)(2,1)S(1)}, u32[]{:S(2)}, u32[]{:S(2)}) collective-permute-start(bf16[2,256,384]{1,2,0:T(8,128)(2,1)S(1)} %pad_maximum_fusion.5), channel_id=1, source_target_pairs={{128,0},{132,4},{136,8},{140,12},{144,16},{148,20},{152,24},{156,2... | collective-permute-start | bytes 1179656 | tf_op jit(solution)/shard_map/ppermute | solution.py:25
  33.5 4.9 %collective-permute-start.3 = (bf16[2,256,384]{1,2,0:T(8,128)(2,1)S(1)}, bf16[2,256,384]{1,2,0:T(8,128)(2,1)S(1)}, u32[]{:S(2)}, u32[]{:S(2)}) collective-permute-start(bf16[2,256,384]{1,2,0:T(8,128)(2,1)S(1)} %pad_maximum_fusion.5), channel_id=1, source_target_pairs={{256,0},{260,4},{264,8},{268,12},{272,16},{276,20},{280,24},{284,2... | collective-permute-start | bytes 1179656 | tf_op jit(solution)/shard_map/ppermute | solution.py:25
  38.4 4.1 %collective-permute-start.2 = (bf16[2,256,384]{1,2,0:T(8,128)(2,1)S(1)}, bf16[2,256,384]{1,2,0:T(8,128)(2,1)S(1)}, u32[]{:S(2)}, u32[]{:S(2)}) collective-permute-start(bf16[2,256,384]{1,2,0:T(8,128)(2,1)S(1)} %pad_maximum_fusion.5), channel_id=1, source_target_pairs={{384,0},{388,4},{392,8},{396,12},{400,16},{404,20},{408,24},{412,2... | collective-permute-start | bytes 1179656 | tf_op jit(solution)/shard_map/ppermute | solution.py:25
  48.6 3.0 %collective-permute-done.3 = bf16[2,256,384]{1,2,0:T(8,128)(2,1)S(1)} collective-permute-done((bf16[2,256,384]{1,2,0:T(8,128)(2,1)S(1)}, bf16[2,256,384]{1,2,0:T(8,128)(2,1)S(1)}, u32[]{:S(2)}, u32[]{:S(2)}) %collective-permute-start.3) | collective-permute-done | bytes 393248 | tf_op jit(solution)/shard_map/ppermute | solution.py:25
  53.2 7.0 %collective-permute-done.2 = bf16[2,256,384]{1,2,0:T(8,128)(2,1)S(1)} collective-permute-done((bf16[2,256,384]{1,2,0:T(8,128)(2,1)S(1)}, bf16[2,256,384]{1,2,0:T(8,128)(2,1)S(1)}, u32[]{:S(2)}, u32[]{:S(2)}) %collective-permute-start.2) | collective-permute-done | bytes 393248 | tf_op jit(solution)/shard_map/ppermute | solution.py:25
  63.2 4.3 %fusion.106 = (f32[3,256]{1,0:T(4,128)}, f32[3,256,768]{2,1,0:T(8,128)}) fusion(pred[256,768]{1,0:T(8,128)(4,1)} %pad_add_fusion, bf16[256,3,128]{0,2,1:T(8,128)(2,1)} %bitcast.225, bf16[256,3,128]{2,0,1:T(8,128)(2,1)} %copy.66, bf16[256,3,128]{2,0,1:T(8,128)(2,1)} %copy.65, bf16[256,3,128]{2,0,1:T(8,128)(2,1)} %copy.64), kind=kOutput, calls=%fused_computation.197 | convolution fusion | flops 155124480 | bytes 3345408 | tf_op jit(solution)/shard_map/sub | solution.py:39
  67.5 7.4 %fusion.12 = bf16[768,3,128]{0,2,1:T(8,128)(2,1)} fusion(bf16[256,3,128]{0,2,1:T(8,128)(2,1)} %bitcast.226, f32[3,768,256]{1,2,0:T(8,128)S(1)} %fusion.63, f32[3,256,768]{2,1,0:T(8,128)} %get-tuple-element.71, f32[3,256]{1,0:T(4,128)} %get-tuple-element.70), kind=kOutput, calls=%fused_computation.24 | convolution fusion | flops 155420160 | bytes 5508096 | tf_op jit(solution)/shard_map/hqk,qhd->khd/dot_general | solution.py:58
  74.9 3.3 %fusion.26 = f32[3,128,256]{2,1,0:T(8,128)} fusion(bf16[256,3,128]{0,2,1:T(8,128)(2,1)S(1)} %bitcast.204, bf16[256,3,128]{0,2,1:T(8,128)(2,1)} %bitcast.206, bf16[256,3,128]{0,2,1:T(8,128)(2,1)} %bitcast.210, f32[3,256,768]{2,1,0:T(8,128)} %get-tuple-element.71, f32[3,256]{1,0:T(4,128)} %get-tuple-element.70), kind=kOutput, calls=%fused_computation.63 | convolution fusion | flops 153944064 | bytes 3345408 | tf_op jit(solution)/shard_map/hqk,khd->qhd/dot_general | solution.py:45
  78.2 1.7 fusion.101
  79.9 8.1 %fusion.18 = f32[3,128,256]{2,1,0:T(8,128)} fusion(f32[3,768,256]{1,2,0:T(8,128)S(1)} %fusion.63, bf16[256,3,128]{2,0,1:T(8,128)(2,1)} %copy.66, bf16[256,3,128]{2,0,1:T(8,128)(2,1)} %copy.65, bf16[256,3,128]{2,0,1:T(8,128)(2,1)} %copy.64, f32[3,256,768]{2,1,0:T(8,128)} %get-tuple-element.71, f32[3,256]{1,0:T(4,128)} %get-tuple-element.70), kind=kOutput, calls=%fused_computation.33 | convolution fusion | flops 156894720 | bytes 5704704 | tf_op jit(solution)/shard_map/hqk,khd->qhd/dot_general | solution.py:55
  88.9 2.9 %fusion.13 = bf16[768,3,128]{0,2,1:T(8,128)(2,1)} fusion(bf16[256,3,128]{0,2,1:T(8,128)(2,1)S(1)} %bitcast.191, f32[3,256,768]{2,1,0:T(8,128)} %get-tuple-element.71, f32[3,256]{1,0:T(4,128)} %get-tuple-element.70), kind=kOutput, calls=%fused_computation.25 | convolution fusion | flops 152469504 | bytes 3148800 | tf_op jit(solution)/shard_map/hqk,qhd->khd/dot_general | solution.py:61
  91.8 1.8 fusion.100
  97.2 4.4 %collective-permute-start.8 = (bf16[2,256,384]{1,2,0:T(8,128)(2,1)}, bf16[2,256,384]{1,2,0:T(8,128)(2,1)}, u32[]{:S(2)}, u32[]{:S(2)}) collective-permute-start(bf16[2,256,384]{1,2,0:T(8,128)(2,1)} %pad_maximum_fusion.9), channel_id=1, source_target_pairs={{256,0},{260,4},{264,8},{268,12},{272,16},{276,20},{280,24},{284,2... | collective-permute-start | bytes 1179656 | tf_op jit(solution)/shard_map/ppermute | solution.py:25
  102.3 1.9 %collective-permute-start.9 = (bf16[2,256,384]{1,2,0:T(8,128)(2,1)}, bf16[2,256,384]{1,2,0:T(8,128)(2,1)}, u32[]{:S(2)}, u32[]{:S(2)}) collective-permute-start(bf16[2,256,384]{1,2,0:T(8,128)(2,1)} %pad_maximum_fusion.10), channel_id=1, source_target_pairs={{384,0},{388,4},{392,8},{396,12},{400,16},{404,20},{408,24},{412,2... | collective-permute-start | bytes 1179656 | tf_op jit(solution)/shard_map/ppermute | solution.py:25
  105.1 4.1 %collective-permute-start.7 = (bf16[2,256,384]{1,2,0:T(8,128)(2,1)}, bf16[2,256,384]{1,2,0:T(8,128)(2,1)}, u32[]{:S(2)}, u32[]{:S(2)}) collective-permute-start(bf16[2,256,384]{1,2,0:T(8,128)(2,1)} %pad_maximum_fusion.8), channel_id=1, source_target_pairs={{128,0},{132,4},{136,8},{140,12},{144,16},{148,20},{152,24},{156,2... | collective-permute-start | bytes 1179656 | tf_op jit(solution)/shard_map/ppermute | solution.py:25
  109.2 2.3 %fusion.107 = (f32[3,256]{1,0:T(4,128)S(1)}, f32[3,256,768]{2,1,0:T(8,128)}) fusion(pred[768]{0:T(1024)(128)(4,1)S(1)} %copy-done.27, bf16[256,3,128]{0,2,1:T(8,128)(2,1)S(1)} %bitcast.228, bf16[256,3,128]{2,0,1:T(8,128)(2,1)S(1)} %copy-done.14, bf16[256,3,128]{2,0,1:T(8,128)(2,1)S(1)} %copy-done.13, bf16[256,3,128]{2,0,1:T(8,128)(2,1)S(1)} %copy-done.15), kind=kOutput, calls=%fused_computation.198 | convolution fusion | flops 155124480 | bytes 3149568 | tf_op jit(solution)/shard_map/sub | solution.py:39
  111.6 3.4 %fusion.108 = (bf16[768,3,128]{0,2,1:T(8,128)(2,1)}, f32[768,3,128]{0,2,1:T(8,128)}) fusion(bf16[256,3,128]{0,2,1:T(8,128)(2,1)S(1)} %bitcast.192, f32[3,256,768]{2,1,0:T(8,128)} %get-tuple-element.73, f32[3,256]{1,0:T(4,128)S(1)} %get-tuple-element.72), kind=kOutput, calls=%fused_computation.199 | convolution fusion | flops 152469504 | bytes 4328448 | tf_op jit(solution)/shard_map/hqk,qhd->khd/dot_general | solution.py:61
  115.0 1.6 fusion.65
  117.7 7.7 %fusion.109 = (bf16[768,3,128]{0,2,1:T(8,128)(2,1)}, f32[768,3,128]{0,2,1:T(8,128)}) fusion(bf16[256,3,128]{0,2,1:T(8,128)(2,1)S(1)} %bitcast.229, f32[3,768,256]{1,2,0:T(8,128)S(1)} %fusion.65, f32[3,256,768]{2,1,0:T(8,128)} %get-tuple-element.73, f32[3,256]{1,0:T(4,128)} %copy-done.30), kind=kOutput, calls=%fused_computation.200 | convolution fusion | flops 155420160 | bytes 6687744 | tf_op jit(solution)/shard_map/hqk,qhd->khd/dot_general | solution.py:58
  125.4 1.8 fusion.97
  127.2 1.8 fusion.96
  130.9 1.8 slice.288
  132.7 1.8 pad_maximum_fusion.7
  134.5 1.9 %collective-permute-start.6 = (bf16[2,256,384]{1,2,0:T(8,128)(2,1)}, bf16[2,256,384]{1,2,0:T(8,128)(2,1)}, u32[]{:S(2)}, u32[]{:S(2)}) collective-permute-start(bf16[2,256,384]{1,2,0:T(8,128)(2,1)} %pad_maximum_fusion.7), channel_id=1, source_target_pairs={{0,4},{4,8},{8,12},{12,16},{16,20},{20,24},{24,28},{28,32},{32,36}... | collective-permute-start | bytes 1179656 | tf_op jit(solution)/shard_map/ppermute | solution.py:19
  137.2 6.9 %collective-permute-start.5 = (bf16[2,256,384]{1,2,0:T(8,128)(2,1)}, bf16[2,256,384]{1,2,0:T(8,128)(2,1)}, u32[]{:S(2)}, u32[]{:S(2)}) collective-permute-start(bf16[2,256,384]{1,2,0:T(8,128)(2,1)} %pad_maximum_fusion.6), channel_id=1, source_target_pairs={{4,0},{8,4},{12,8},{16,12},{20,16},{24,20},{28,24},{32,28},{36,32}... | collective-permute-start | bytes 1179656 | tf_op jit(solution)/shard_map/ppermute | solution.py:19
  144.1 8.1 %fusion.20 = f32[3,128,256]{2,1,0:T(8,128)} fusion(f32[3,768,256]{1,2,0:T(8,128)S(1)} %fusion.65, bf16[256,3,128]{2,0,1:T(8,128)(2,1)} %copy.61, bf16[256,3,128]{2,0,1:T(8,128)(2,1)} %copy.60, bf16[256,3,128]{2,0,1:T(8,128)(2,1)} %copy.59, f32[3,256,768]{2,1,0:T(8,128)} %get-tuple-element.73, f32[3,256]{1,0:T(4,128)} %copy-done.30), kind=kOutput, calls=%fused_computation.35 | convolution fusion | flops 156894720 | bytes 5704704 | tf_op jit(solution)/shard_map/hqk,khd->qhd/dot_general | solution.py:55
  152.3 1.7 fusion.39
  159.2 9.9 %psum.15 = f32[4,256]{1,0:T(4,128)} all-reduce(f32[4,256]{1,0:T(4,128)} %pad_maximum_fusion.28), channel_id=1, replica_groups=mesh['seq'=128,'head'=4] {'head'}, use_global_device_ids=true, to_apply=%region_15.16 | all-reduce | flops 1024 | bytes 8192 | tf_op jit(solution)/shard_map/psum | solution.py:203
  172.7 1.7 copy.82
  (159 shorter events, 43.5 us)
Async XLA Ops:
  0.6 15.5 %copy-start.10 = (bf16[256,384]{1,0:T(8,128)(2,1)S(1)}, bf16[256,384]{1,0:T(8,128)(2,1)}, u32[]{:S(2)}) copy-start(bf16[256,384]{1,0:T(8,128)(2,1)} %param.11) | copy-start | bytes 589828
  0.6 30.6 %copy-start.11 = (bf16[256,384]{1,0:T(8,128)(2,1)S(1)}, bf16[256,384]{1,0:T(8,128)(2,1)}, u32[]{:S(2)}) copy-start(bf16[256,384]{1,0:T(8,128)(2,1)} %param.14) | copy-start | bytes 589828
  4.8 38.0 %copy-start.23 = (s32[384,2]{0,1:T(2,128)S(1)}, s32[384,2]{0,1:T(2,128)}, u32[]{:S(2)}) copy-start(s32[384,2]{0,1:T(2,128)} %param.17) | copy-start | bytes 9220
  6.0 40.0 %copy-start.12 = (bf16[256,384]{1,0:T(8,128)(2,1)S(1)}, bf16[256,384]{1,0:T(8,128)(2,1)}, u32[]{:S(2)}) copy-start(bf16[256,384]{1,0:T(8,128)(2,1)} %param.15) | copy-start | bytes 589828
  16.2 13.1 %copy-start.18 = (f32[1,256]{1,0:T(1,128)}, f32[1,256]{1,0:T(1,128)S(1)}, u32[]{:S(2)}) copy-start(f32[1,256]{1,0:T(1,128)S(1)} %get-tuple-element.51) | copy-start | bytes 3076
  16.2 13.1 %copy-start.20 = (f32[1,256]{1,0:T(1,128)}, f32[1,256]{1,0:T(1,128)S(1)}, u32[]{:S(2)}) copy-start(f32[1,256]{1,0:T(1,128)S(1)} %get-tuple-element.54) | copy-start | bytes 3076
  16.2 28.0 %copy-start.21 = (f32[1,256]{1,0:T(1,128)}, f32[1,256]{1,0:T(1,128)S(1)}, u32[]{:S(2)}) copy-start(f32[1,256]{1,0:T(1,128)S(1)} %get-tuple-element.52) | copy-start | bytes 3076
  16.2 27.9 %copy-start.22 = (f32[1,256]{1,0:T(1,128)}, f32[1,256]{1,0:T(1,128)S(1)}, u32[]{:S(2)}) copy-start(f32[1,256]{1,0:T(1,128)S(1)} %get-tuple-element.53) | copy-start | bytes 3076
  16.4 30.7 %copy-start.1 = (bf16[256,384]{0,1:T(8,128)(2,1)}, bf16[256,384]{0,1:T(8,128)(2,1)S(1)}, u32[]{:S(2)}) copy-start(bf16[256,384]{0,1:T(8,128)(2,1)S(1)} %copy.57) | copy-start | bytes 589828
  18.0 60.2 %collective-permute-start.1 = (bf16[2,256,384]{1,2,0:T(8,128)(2,1)}, bf16[2,256,384]{1,2,0:T(8,128)(2,1)}, u32[]{:S(2)}, u32[]{:S(2)}) collective-permute-start(bf16[2,256,384]{1,2,0:T(8,128)(2,1)} %pad_maximum_fusion.4), channel_id=1, source_target_pairs={{4,0},{8,4},{12,8},{16,12},{20,16},{24,20},{28,24},{32,28},{36,32}... | collective-permute-start | bytes 1179656 | tf_op jit(solution)/shard_map/ppermute | solution.py:19
  29.3 62.5 %collective-permute-start = (bf16[2,256,384]{1,2,0:T(8,128)(2,1)}, bf16[2,256,384]{1,2,0:T(8,128)(2,1)}, u32[]{:S(2)}, u32[]{:S(2)}) collective-permute-start(bf16[2,256,384]{1,2,0:T(8,128)(2,1)} %pad_maximum_fusion.4), channel_id=1, source_target_pairs={{0,4},{4,8},{8,12},{12,16},{16,20},{20,24},{24,28},{28,32},{32,36}... | collective-permute-start | bytes 1179656 | tf_op jit(solution)/shard_map/ppermute | solution.py:19
  31.6 16.2 %collective-permute-start.4 = (bf16[2,256,384]{1,2,0:T(8,128)(2,1)S(1)}, bf16[2,256,384]{1,2,0:T(8,128)(2,1)S(1)}, u32[]{:S(2)}, u32[]{:S(2)}) collective-permute-start(bf16[2,256,384]{1,2,0:T(8,128)(2,1)S(1)} %pad_maximum_fusion.5), channel_id=1, source_target_pairs={{128,0},{132,4},{136,8},{140,12},{144,16},{148,20},{152,24},{156,2... | collective-permute-start | bytes 1179656 | tf_op jit(solution)/shard_map/ppermute | solution.py:25
  33.5 18.2 %collective-permute-start.3 = (bf16[2,256,384]{1,2,0:T(8,128)(2,1)S(1)}, bf16[2,256,384]{1,2,0:T(8,128)(2,1)S(1)}, u32[]{:S(2)}, u32[]{:S(2)}) collective-permute-start(bf16[2,256,384]{1,2,0:T(8,128)(2,1)S(1)} %pad_maximum_fusion.5), channel_id=1, source_target_pairs={{256,0},{260,4},{264,8},{268,12},{272,16},{276,20},{280,24},{284,2... | collective-permute-start | bytes 1179656 | tf_op jit(solution)/shard_map/ppermute | solution.py:25
  38.4 21.8 %collective-permute-start.2 = (bf16[2,256,384]{1,2,0:T(8,128)(2,1)S(1)}, bf16[2,256,384]{1,2,0:T(8,128)(2,1)S(1)}, u32[]{:S(2)}, u32[]{:S(2)}) collective-permute-start(bf16[2,256,384]{1,2,0:T(8,128)(2,1)S(1)} %pad_maximum_fusion.5), channel_id=1, source_target_pairs={{384,0},{388,4},{392,8},{396,12},{400,16},{404,20},{408,24},{412,2... | collective-permute-start | bytes 1179656 | tf_op jit(solution)/shard_map/ppermute | solution.py:25
  46.2 65.3 %copy-start = (bf16[256,384]{0,1:T(8,128)(2,1)}, bf16[256,384]{0,1:T(8,128)(2,1)S(1)}, u32[]{:S(2)}) copy-start(bf16[256,384]{0,1:T(8,128)(2,1)S(1)} %copy.68) | copy-start | bytes 589828
  91.8 3.8 %copy-start.9 = (bf16[768,3,128]{0,2,1:T(8,128)(2,1)S(1)}, bf16[768,3,128]{0,2,1:T(8,128)(2,1)}, u32[]{:S(2)}) copy-start(bf16[768,3,128]{0,2,1:T(8,128)(2,1)} %fusion.12) | copy-start | bytes 1769476
  91.8 3.9 %copy-start.3 = (f32[3,128,256]{2,1,0:T(8,128)S(1)}, f32[3,128,256]{2,1,0:T(8,128)}, u32[]{:S(2)}) copy-start(f32[3,128,256]{2,1,0:T(8,128)} %fusion.18) | copy-start | bytes 1179652
  95.6 13.6 %copy-start.13 = (bf16[256,3,128]{2,0,1:T(8,128)(2,1)S(1)}, bf16[256,3,128]{2,0,1:T(8,128)(2,1)}, u32[]{:S(2)}) copy-start(bf16[256,3,128]{2,0,1:T(8,128)(2,1)} %copy.60) | copy-start | bytes 589828
  95.6 13.6 %copy-start.14 = (bf16[256,3,128]{2,0,1:T(8,128)(2,1)S(1)}, bf16[256,3,128]{2,0,1:T(8,128)(2,1)}, u32[]{:S(2)}) copy-start(bf16[256,3,128]{2,0,1:T(8,128)(2,1)} %copy.61) | copy-start | bytes 589828
  95.6 13.6 %copy-start.15 = (bf16[256,3,128]{2,0,1:T(8,128)(2,1)S(1)}, bf16[256,3,128]{2,0,1:T(8,128)(2,1)}, u32[]{:S(2)}) copy-start(bf16[256,3,128]{2,0,1:T(8,128)(2,1)} %copy.59) | copy-start | bytes 589828
  95.7 13.6 %copy-start.16 = (bf16[256,384]{0,1:T(8,128)(2,1)S(1)}, bf16[256,384]{0,1:T(8,128)(2,1)}, u32[]{:S(2)}) copy-start(bf16[256,384]{0,1:T(8,128)(2,1)} %get-tuple-element.79) | copy-start | bytes 589828
  95.7 13.6 %copy-start.27 = (pred[768]{0:T(1024)(128)(4,1)S(1)}, pred[768]{0:T(1024)(128)(4,1)}, u32[]{:S(2)}) copy-start(pred[768]{0:T(1024)(128)(4,1)} %broadcast_in_dim_reshape.2) | copy-start | bytes 2308
  97.2 56.8 %collective-permute-start.8 = (bf16[2,256,384]{1,2,0:T(8,128)(2,1)}, bf16[2,256,384]{1,2,0:T(8,128)(2,1)}, u32[]{:S(2)}, u32[]{:S(2)}) collective-permute-start(bf16[2,256,384]{1,2,0:T(8,128)(2,1)} %pad_maximum_fusion.9), channel_id=1, source_target_pairs={{256,0},{260,4},{264,8},{268,12},{272,16},{276,20},{280,24},{284,2... | collective-permute-start | bytes 1179656 | tf_op jit(solution)/shard_map/ppermute | solution.py:25
  102.3 51.7 %collective-permute-start.9 = (bf16[2,256,384]{1,2,0:T(8,128)(2,1)}, bf16[2,256,384]{1,2,0:T(8,128)(2,1)}, u32[]{:S(2)}, u32[]{:S(2)}) collective-permute-start(bf16[2,256,384]{1,2,0:T(8,128)(2,1)} %pad_maximum_fusion.10), channel_id=1, source_target_pairs={{384,0},{388,4},{392,8},{396,12},{400,16},{404,20},{408,24},{412,2... | collective-permute-start | bytes 1179656 | tf_op jit(solution)/shard_map/ppermute | solution.py:25
  105.1 48.9 %collective-permute-start.7 = (bf16[2,256,384]{1,2,0:T(8,128)(2,1)}, bf16[2,256,384]{1,2,0:T(8,128)(2,1)}, u32[]{:S(2)}, u32[]{:S(2)}) collective-permute-start(bf16[2,256,384]{1,2,0:T(8,128)(2,1)} %pad_maximum_fusion.8), channel_id=1, source_target_pairs={{128,0},{132,4},{136,8},{140,12},{144,16},{148,20},{152,24},{156,2... | collective-permute-start | bytes 1179656 | tf_op jit(solution)/shard_map/ppermute | solution.py:25
  129.8 6.6 %copy-start.7 = (bf16[256,3,128]{0,2,1:T(8,128)(2,1)S(1)}, bf16[256,3,128]{0,2,1:T(8,128)(2,1)}, u32[]{:S(2)}) copy-start(bf16[256,3,128]{0,2,1:T(8,128)(2,1)} %get-tuple-element.29) | copy-start | bytes 589828
  129.8 6.6 %copy-start.8 = (bf16[256,3,128]{0,2,1:T(8,128)(2,1)S(1)}, bf16[256,3,128]{0,2,1:T(8,128)(2,1)}, u32[]{:S(2)}) copy-start(bf16[256,3,128]{0,2,1:T(8,128)(2,1)} %get-tuple-element.27) | copy-start | bytes 589828
  134.5 21.7 %collective-permute-start.6 = (bf16[2,256,384]{1,2,0:T(8,128)(2,1)}, bf16[2,256,384]{1,2,0:T(8,128)(2,1)}, u32[]{:S(2)}, u32[]{:S(2)}) collective-permute-start(bf16[2,256,384]{1,2,0:T(8,128)(2,1)} %pad_maximum_fusion.7), channel_id=1, source_target_pairs={{0,4},{4,8},{8,12},{12,16},{16,20},{20,24},{24,28},{28,32},{32,36}... | collective-permute-start | bytes 1179656 | tf_op jit(solution)/shard_map/ppermute | solution.py:19
  137.2 20.2 %collective-permute-start.5 = (bf16[2,256,384]{1,2,0:T(8,128)(2,1)}, bf16[2,256,384]{1,2,0:T(8,128)(2,1)}, u32[]{:S(2)}, u32[]{:S(2)}) collective-permute-start(bf16[2,256,384]{1,2,0:T(8,128)(2,1)} %pad_maximum_fusion.6), channel_id=1, source_target_pairs={{4,0},{8,4},{12,8},{16,12},{20,16},{24,20},{28,24},{32,28},{36,32}... | collective-permute-start | bytes 1179656 | tf_op jit(solution)/shard_map/ppermute | solution.py:19
  174.5 5.4 %copy-start.19 = (f32[1,256]{1,0:T(1,128)S(1)}, f32[1,256]{1,0:T(1,128)}, u32[]{:S(2)}) copy-start(f32[1,256]{1,0:T(1,128)} %copy-done.18) | copy-start | bytes 3076
  174.5 5.4 %copy-start.26 = (f32[1,256]{1,0:T(1,128)S(1)}, f32[1,256]{1,0:T(1,128)}, u32[]{:S(2)}) copy-start(f32[1,256]{1,0:T(1,128)} %get-tuple-element.50) | copy-start | bytes 3076
  174.5 5.4 %copy-start.4 = (f32[3,128,256]{2,1,0:T(8,128)S(1)}, f32[3,128,256]{2,1,0:T(8,128)}, u32[]{:S(2)}) copy-start(f32[3,128,256]{2,1,0:T(8,128)} %fusion.20) | copy-start | bytes 1179652
  (10 other events, 24.9 us)
where the time goes:
time: 183 us; the launch traced here: 182 us
  matrix products  51.3 us (28%)
  starting transfers between devices  43.4 us (24%)
  local copies, waits for them, and re-layouts  31.4 us (17%)
  other arithmetic  24 us (13%)
  blocking collectives  20 us (11%)
  waiting for transfers between devices  10.1 us (6%)
    ppermute x4, starting transfers between devices, shifted_2(): lax.ppermute(value, axis, [(source, source + steps) for source in range(f...  22.1 us
    ppermute x6, starting transfers between devices, shifted_3(): return lax.ppermute(block, axis, route)  21.3 us
    dot_general x2, matrix products, query_side(): jnp.einsum('hqk,khd->qhd', score_grad, split_heads(keys), preferred_eleme...  16.3 us
    dot_general x2, matrix products, query_side(): jnp.einsum('hqk,qhd->khd', score_grad, split_heads(queries), preferred_el...  15.1 us
    unnamed x78, local copies, waits for them, and re-layouts  11.9 us
    psum x1, blocking collectives, on_device(): squares = lax.psum(squares, 'head')  10.1 us
    ppermute x6, waiting for transfers between devices, shifted_3(): return lax.ppermute(block, axis, route)  10 us
    psum x1, blocking collectives, on_device(): inner = lax.psum(inner, 'head')  9.94 us
  transfers between devices with their start and end apart: 10, of which 2 were waited for; matrix products, arithmetic and copies ran while one was open for 44% of the time, Pallas kernels for 0%

commit v1 on v0

v1 whole, which is shorter than its diff:
```python
import functools

import jax
import jax.numpy as jnp
from jax import lax
from jax.experimental import pallas as pl
from jax.experimental.pallas import tpu as pltpu
from jax.sharding import Mesh, PartitionSpec as P

DH = 128
BLK = 64
WIDTH = 1536
NSUB = 4
HEADS = 3
TOK = 256
COLS = 384
EPSILON = 1e-06
SCALE = DH ** (-0.5)
MASKED = -1e30
F32 = jnp.float32
BF16 = jnp.bfloat16
VMEM = pltpu.VMEM
VSPEC = pl.BlockSpec(memory_space=pltpu.VMEM)
SSPEC = pl.BlockSpec(memory_space=pltpu.SMEM)


def dot(a, b, ca, cb):
    return lax.dot_general(a, b, (((ca,), (cb,)), ((), ())), preferred_element_type=F32)


def row_sums(product):
    folded = product[:, 0:128] + product[:, 128:256] + product[:, 256:384]
    return jnp.sum(jnp.transpose(folded), axis=0, keepdims=True)


def squares_kernel(*refs):
    ins, out = refs[:-1], refs[-1]
    out[...] = jnp.zeros(out.shape, F32)
    for i, ref in enumerate(ins):
        wide = ref[...].astype(F32)
        out[i : i + 1, :] = row_sums(wide * wide)


def attend(heads_q, heads_k, heads_v, heads_do, biases, masks):
    scores = []
    for kn, bias, mask in zip(heads_k, biases, masks):
        s = dot(kn, heads_q, 1, 1)
        if bias is not None:
            s = s + bias
        if mask is not None:
            s = jnp.where(mask, s, MASKED)
        scores.append(s)
    top = functools.reduce(jnp.maximum, [jnp.max(s, axis=0, keepdims=True) for s in scores])
    shifted = [jnp.exp((s - top) * SCALE) for s in scores]
    total = sum(jnp.sum(e, axis=0, keepdims=True) for e in shifted)
    inverse = 1.0 / total
    probs = [e * inverse for e in shifted]
    dprobs = [dot(v, heads_do, 1, 1) for v in heads_v]
    delta = sum(jnp.sum(p * d, axis=0, keepdims=True) for p, d in zip(probs, dprobs))
    out = dq = None
    dks, dvs = [], []
    for p, d, kn, v in zip(probs, dprobs, heads_k, heads_v):
        w = p.astype(BF16)
        ds = (p * (d - delta) * SCALE).astype(BF16)
        o_part = dot(w, v, 0, 0)
        q_part = dot(ds, kn, 0, 0)
        out = o_part if out is None else out + o_part
        dq = q_part if dq is None else dq + q_part
        dks.append(dot(ds, heads_q, 1, 0))
        dvs.append(dot(w, heads_do, 1, 0))
    return out, dq, dks, dvs


def inverse_rms(sums_ref):
    return jnp.transpose(lax.rsqrt(sums_ref[...] * (1.0 / WIDTH) + EPSILON))


def normed(raw, inv, gain):
    return (raw.astype(F32) * inv * gain).astype(BF16)


def self_kernel(
    scal, sums, gains, q_ref, k_ref, v_ref, do_ref, kb_ref, vb_ref, ka_ref, va_ref,
    out_ref, dq_ref, dk_ref, dv_ref, pb_ref, pa_ref,
):
    group, slot = scal[0], scal[1]
    tower = (group == 3).astype(jnp.int32)
    inv = inverse_rms(sums)
    bias_b = jnp.where(slot > 0, 0.0, MASKED).astype(F32)
    bias_a = jnp.where(slot < 31, 0.0, MASKED).astype(F32)
    for h in range(HEADS):
        c = slice(h * DH, (h + 1) * DH)
        gq = gains[tower, 0:1, c]
        gk = gains[tower, 1:2, c]
        qn = normed(q_ref[:, c], inv[:, 0:1], gq)
        do = do_ref[:, c]
        kn = [
            normed(k_ref[:, c], inv[:, 1:2], gk),
            normed(kb_ref[:, c], inv[:, 4:5], gk),
            normed(ka_ref[:, c], inv[:, 5:6], gk),
        ]
        vs = [v_ref[:, c], vb_ref[:, c], va_ref[:, c]]
        out, dq, dks, dvs = attend(qn, kn, vs, do, [None, bias_b, bias_a], [None] * 3)
        out_ref[:, c] = out
        dq_ref[:, c] = dq
        dk_ref[:, c] = dks[0]
        dv_ref[:, c] = dvs[0]
        for ref, i in ((pb_ref, 1), (pa_ref, 2)):
            ref[0:TOK, c] = dks[i].astype(BF16)
            ref[TOK:, c] = dvs[i].astype(BF16)


def cross_kernel(
    scal, sums, gains, q_ref, do_ref, k0, v0, k1, v1, k2, v2,
    out_ref, dq_ref, p0, p1, p2,
):
    group = scal[0]
    audio = group == 3
    inv = inverse_rms(sums)
    sub_row = lax.broadcasted_iota(jnp.int32, (1, TOK), 1) // BLK
    sub_col = lax.broadcasted_iota(jnp.int32, (TOK, 1), 0) // BLK

    def spread(base, offset, sub):
        value = jnp.zeros(sub.shape, jnp.int32)
        for b in range(NSUB):
            value = jnp.where(sub == b, scal[base + 2 * b + offset], value)
        return value

    @pl.when(audio)
    def _():
        masks = []
        for j in range(3):
            lower = spread(2 + 8 * j, 0, sub_col)
            upper = spread(2 + 8 * j, 1, sub_col)
            masks.append((sub_row >= lower) & (sub_row < upper))
        for h in range(HEADS):
            c = slice(h * DH, (h + 1) * DH)
            qn = normed(q_ref[:, c], inv[:, 2:3], gains[1, 2:3, c])
            do = do_ref[:, c]
            kn = [normed(k[:, c], inv[:, 6 + j : 7 + j], gains[0, 3:4, c]) for j, k in enumerate((k0, k1, k2))]
            vs = [v[:, c] for v in (v0, v1, v2)]
            out, dq, dks, dvs = attend(qn, kn, vs, do, [None] * 3, masks)
            out_ref[:, c] = out
            dq_ref[:, c] = dq
            for ref, dk, dv in zip((p0, p1, p2), dks, dvs):
                ref[0:TOK, c] = dk.astype(BF16)
                ref[TOK:, c] = dv.astype(BF16)

    @pl.when(jnp.logical_not(audio))
    def _():
        base = 2 + 8 * group
        lower = spread(base, 0, sub_row)
        upper = spread(base, 1, sub_row)
        mask = (sub_col >= lower) & (sub_col < upper)
        first, second = group == 0, group == 1

        def pick(a, b, c):
            return jnp.where(first, a, jnp.where(second, b, c))

        inv_k = pick(inv[:, 6:7], inv[:, 7:8], inv[:, 8:9])
        for h in range(HEADS):
            c = slice(h * DH, (h + 1) * DH)
            qn = normed(q_ref[:, c], inv[:, 2:3], gains[0, 2:3, c])
            do = do_ref[:, c]
            kn = normed(pick(k0[:, c], k1[:, c], k2[:, c]), inv_k, gains[1, 3:4, c])
            v = pick(v0[:, c], v1[:, c], v2[:, c])
            out, dq, dks, dvs = attend(qn, [kn], [v], do, [None], [mask])
            out_ref[:, c] = out
            dq_ref[:, c] = dq
            dk = dks[0].astype(BF16)
            dv = dvs[0].astype(BF16)
            for j, ref in enumerate((p0, p1, p2)):

                @pl.when(group == j)
                def _():
                    ref[0:TOK, c] = dk
                    ref[TOK:, c] = dv


def gather_kernel(
    scal, gains, sq, sk, cq, ck, so, co, sdq, cdq, sdk, sdv, rb, ra, r0, r1, r2,
    att, svg, cvg, dks_ref, dkc_ref, inner,
):
    tower = (scal[0] == 3).astype(jnp.int32)
    att[...] = (so[...] + co[...]).astype(BF16)
    dks = sdk[...] + rb[0:TOK, :].astype(F32) + ra[0:TOK, :].astype(F32)
    svg[...] = (sdv[...] + rb[TOK:, :].astype(F32) + ra[TOK:, :].astype(F32)).astype(BF16)
    dkc = r0[0:TOK, :].astype(F32) + r1[0:TOK, :].astype(F32) + r2[0:TOK, :].astype(F32)
    cvg[...] = (r0[TOK:, :].astype(F32) + r1[TOK:, :].astype(F32) + r2[TOK:, :].astype(F32)).astype(BF16)
    dks_ref[...] = dks
    dkc_ref[...] = dkc
    inner[...] = jnp.zeros(inner.shape, F32)
    for i, (x, y) in enumerate(((sq, sdq[...]), (sk, dks), (cq, cdq[...]), (ck, dkc))):
        inner[i : i + 1, :] = row_sums(gains[tower, i : i + 1, :] * y * x[...].astype(F32))


def final_kernel(scal, gains, sums, inner, sq, sk, cq, ck, y0, y1, y2, y3, o0, o1, o2, o3):
    tower = (scal[0] == 3).astype(jnp.int32)
    inv = inverse_rms(sums)
    mean = jnp.transpose(inner[...]) * (1.0 / WIDTH)
    for i, (x, y, o) in enumerate(zip((sq, sk, cq, ck), (y0, y1, y2, y3), (o0, o1, o2, o3))):
        r = inv[:, i : i + 1]
        o[...] = (
            r * gains[tower, i : i + 1, :] * y[...] - x[...].astype(F32) * (r * r * r * mean[:, i : i + 1])
        ).astype(BF16)


def shape(rows, dtype, cols=COLS):
    return jax.ShapeDtypeStruct((rows, cols), dtype)


def call(kernel, name, scalars, outs, *args, flops=0):
    nbytes = sum(a.size * a.dtype.itemsize for a in args) + sum(o.size * o.dtype.itemsize for o in outs)
    return pl.pallas_call(
        kernel,
        name=name,
        out_shape=outs,
        in_specs=[SSPEC] * scalars + [VSPEC] * (len(args) - scalars),
        out_specs=[VSPEC] * len(outs),
        compiler_params=pltpu.CompilerParams(vmem_limit_bytes=40 * 1024 * 1024),
        cost_estimate=pl.CostEstimate(flops=flops, bytes_accessed=nbytes, transcendentals=0),
    )(*args)


def on_device(sq, sk, sv, cq, ck, cv, do, gains, span):
    group = lax.axis_index("y")
    slot = lax.axis_index("t")
    slots = lax.axis_size("t")
    up = [(i, i + 1) for i in range(slots - 1)]
    down = [(i + 1, i) for i in range(slots - 1)]
    pairs = [[(3, j), (j, 3)] for j in range(3)]
    spans = lax.dynamic_slice_in_dim(span.reshape(3, NSUB * slots, 2), slot * NSUB, NSUB, 1)
    scal = jnp.concatenate([jnp.stack([group, slot]).astype(jnp.int32), spans.reshape(-1)])

    c_in = [(lax.ppermute(ck, "y", p), lax.ppermute(cv, "y", p)) for p in pairs]
    kb, vb = lax.ppermute(sk, "t", up), lax.ppermute(sv, "t", up)
    ka, va = lax.ppermute(sk, "t", down), lax.ppermute(sv, "t", down)

    sums = call(
        squares_kernel, "squares", 0, [shape(16, F32, TOK)], sq, sk, cq, ck, kb, ka, c_in[0][0], c_in[1][0], c_in[2][0]
    )[0]
    sums = lax.psum(sums, "head")

    flat = [a for pair in c_in for a in pair]
    c_out, c_dq, *c_parts = call(
        cross_kernel, "cross", 1, [shape(TOK, F32)] * 2 + [shape(2 * TOK, BF16)] * 3, scal, sums, gains, cq, do, *flat,
        flops=12 * HEADS * TOK * 3 * TOK * DH,
    )
    c_back = [lax.ppermute(part, "y", p) for part, p in zip(c_parts, pairs)]
    s_out, s_dq, s_dk, s_dv, part_b, part_a = call(
        self_kernel, "selfatt", 1, [shape(TOK, F32)] * 4 + [shape(2 * TOK, BF16)] * 2, scal, sums, gains, sq, sk, sv, do,
        kb, vb, ka, va, flops=12 * HEADS * TOK * 3 * TOK * DH,
    )
    back_a = lax.ppermute(part_b, "t", down)
    back_b = lax.ppermute(part_a, "t", up)

    att, svg, cvg, dks, dkc, inner = call(
        gather_kernel, "gather", 1, [shape(TOK, BF16)] * 3 + [shape(TOK, F32)] * 2 + [shape(8, F32, TOK)],
        scal, gains, sq, sk, cq, ck, s_out, c_out, s_dq, c_dq, s_dk, s_dv, back_b, back_a, *c_back,
    )
    inner = lax.psum(inner, "head")
    g0, g1, g2, g3 = call(
        final_kernel, "final", 1, [shape(TOK, BF16)] * 4, scal, gains, sums, inner, sq, sk, cq, ck, s_dq, dks, c_dq, dkc
    )
    return att, g0, g1, svg, g2, g3, cvg


def solution(mesh):
    seq = mesh.shape["seq"]
    grid = Mesh(mesh.devices.reshape(4, seq // 4, mesh.shape["head"]), ("y", "t", "head"))
    block = P(("y", "t"), "head")
    return jax.shard_map(
        on_device,
        mesh=grid,
        in_specs=(block,) * 7 + (P(None, None, "head"), P()),
        out_specs=(block,) * 7,
        check_vma=False,
    )
```

time: 183 us -> 102 us (0.56)
  the two profiles are of different devices: /device:TPU:8 before, /device:TPU:400 now
where the time goes in v1:
time: 102 us; the launch traced here: 101 us
  starting transfers between devices  45.1 us (44%)
  blocking collectives  21.1 us (21%)
  waiting for transfers between devices  16.4 us (16%)
  Pallas kernels  11.1 us (11%)
  local copies, waits for them, and re-layouts  6.3 us (6%)
    psum x1, blocking collectives, on_device(): sums = lax.psum(sums, 'head')  13.2 us
    ppermute x6, starting transfers between devices, on_device(): c_in = [(lax.ppermute(ck, 'y', p), lax.ppermute(cv, 'y', p)) for p in pairs]  12.8 us
    pallas_call x5, Pallas kernels, call(): pl.pallas_call(kernel, name=name, out_shape=outs, in_specs=[SSPEC] * scal...  11.1 us
    ppermute x2, starting transfers between devices, on_device(): ka, va = (lax.ppermute(sk, 't', down), lax.ppermute(sv, 't', down))  9.84 us
    ppermute x3, starting transfers between devices, on_device(): c_back = [lax.ppermute(part, 'y', p) for part, p in zip(c_parts, pairs)]  9.42 us
    psum x1, blocking collectives, on_device(): inner = lax.psum(inner, 'head')  7.91 us
    ppermute x1, waiting for transfers between devices, on_device(): back_b = lax.ppermute(part_a, 't', up)  7.42 us
    ppermute x1, starting transfers between devices, on_device(): back_a = lax.ppermute(part_b, 't', down)  6.03 us
  transfers between devices with their start and end apart: 15, of which 4 were waited for; matrix products, arithmetic and copies ran while one was open for 0% of the time, Pallas kernels for 7%

profile of v1, /device:TPU:400, one launch (start us, length us, event | category | flops | bytes accessed | tf_op | source)
XLA Modules:
  0.0 101.1 jit_solution(879250661425176089)
XLA Ops:
  0.6 5.1 %collective-permute-start.1 = (bf16[256,384]{1,0:T(8,128)(2,1)}, bf16[256,384]{1,0:T(8,128)(2,1)S(1)}, u32[]{:S(2)}, u32[]{:S(2)}) collective-permute-start(bf16[256,384]{1,0:T(8,128)(2,1)} %sk.3), channel_id=1, source_target_pairs={{4,0},{8,4},{12,8},{16,12},{20,16},{24,20},{28,24},{32,28},{36,32}... | collective-permute-start | bytes 589832 | tf_op jit(solution)/shard_map/ppermute | solution.py:237
  5.7 1.9 %collective-permute-start = (bf16[256,384]{1,0:T(8,128)(2,1)}, bf16[256,384]{1,0:T(8,128)(2,1)S(1)}, u32[]{:S(2)}, u32[]{:S(2)}) collective-permute-start(bf16[256,384]{1,0:T(8,128)(2,1)} %sk.3), channel_id=1, source_target_pairs={{0,4},{4,8},{8,12},{12,16},{16,20},{20,24},{24,28},{28,32},{32,36}... | collective-permute-start | bytes 589832 | tf_op jit(solution)/shard_map/ppermute | solution.py:236
  7.6 3.2 %collective-permute-start.4 = (bf16[256,384]{1,0:T(8,128)(2,1)}, bf16[256,384]{1,0:T(8,128)(2,1)S(1)}, u32[]{:S(2)}, u32[]{:S(2)}) collective-permute-start(bf16[256,384]{1,0:T(8,128)(2,1)} %ck.3), channel_id=1, source_target_pairs={{384,256},{256,384},{385,257},{257,385},{386,258},{258,386},{387,2... | collective-permute-start | bytes 589832 | tf_op jit(solution)/shard_map/ppermute | solution.py:235
  10.8 0.7 collective-permute-start.3
  11.5 0.7 collective-permute-start.2
  12.2 0.7 copy-done.13
  12.9 0.7 collective-permute-start.7
  13.6 2.7 %collective-permute-done.refs_4_.kb_ref = bf16[256,384]{1,0:T(8,128)(2,1)S(1)} collective-permute-done((bf16[256,384]{1,0:T(8,128)(2,1)}, bf16[256,384]{1,0:T(8,128)(2,1)S(1)}, u32[]{:S(2)}, u32[]{:S(2)}) %collective-permute-start) | collective-permute-done | bytes 196640 | tf_op jit(solution)/shard_map/ppermute | solution.py:236
  16.3 6.9 %collective-permute-start.9 = (bf16[256,384]{1,0:T(8,128)(2,1)}, bf16[256,384]{1,0:T(8,128)(2,1)S(1)}, u32[]{:S(2)}, u32[]{:S(2)}) collective-permute-start(bf16[256,384]{1,0:T(8,128)(2,1)} %param.14), channel_id=1, source_target_pairs={{384,256},{256,384},{385,257},{257,385},{386,258},{258,386},{387,2... | collective-permute-start | bytes 589832 | tf_op jit(solution)/shard_map/ppermute | solution.py:235
  23.2 0.7 collective-permute-start.8
  24.2 3.2 %collective-permute-start.5 = (bf16[256,384]{1,0:T(8,128)(2,1)}, bf16[256,384]{1,0:T(8,128)(2,1)S(1)}, u32[]{:S(2)}, u32[]{:S(2)}) collective-permute-start(bf16[256,384]{1,0:T(8,128)(2,1)} %v_ref.1), channel_id=1, source_target_pairs={{0,4},{4,8},{8,12},{12,16},{16,20},{20,24},{24,28},{28,32},{32,36}... | collective-permute-start | bytes 589832 | tf_op jit(solution)/shard_map/ppermute | solution.py:236
  27.4 4.8 %collective-permute-start.6 = (bf16[256,384]{1,0:T(8,128)(2,1)}, bf16[256,384]{1,0:T(8,128)(2,1)S(1)}, u32[]{:S(2)}, u32[]{:S(2)}) collective-permute-start(bf16[256,384]{1,0:T(8,128)(2,1)} %v_ref.1), channel_id=1, source_target_pairs={{4,0},{8,4},{12,8},{16,12},{20,16},{24,20},{28,24},{32,28},{36,32}... | collective-permute-start | bytes 589832 | tf_op jit(solution)/shard_map/ppermute | solution.py:237
  32.2 0.9 copy-done
  33.2 0.9 copy-done.2
  34.1 0.9 copy-done.4
  35.0 0.9 copy-done.6
  36.4 13.2 %psum.14.sums = f32[16,256]{1,0:T(8,128)S(1)} all-reduce(f32[16,256]{1,0:T(8,128)S(1)} %squares.1), channel_id=1, replica_groups=mesh['y'=4,'t'=32,'head'=4] {'head'}, use_global_device_ids=true, to_apply=%region_0.0 | all-reduce | flops 4096 | bytes 32768 | tf_op jit(solution)/shard_map/psum | solution.py:242
  49.7 0.7 copy-done.11
  50.3 0.9 copy-done.12
  51.3 3.0 %cross.1 = (f32[256,384]{1,0:T(8,128)S(1)}, f32[256,384]{1,0:T(8,128)S(1)}, bf16[512,384]{1,0:T(8,128)(2,1)S(1)}, bf16[512,384]{1,0:T(8,128)(2,1)S(1)}, bf16[512,384]{1,0:T(8,128)(2,1)S(1)}) custom-call(s32[26]{0:T(128)S(1)} %pad_add_fusion.scal, f32[16,256]{1,0:T(8,128)S(1)} %psum.14.sums, f32[2,4,384]{2,1,0:T(4,128)S(1)} %copy-done.8, ...), custom_call_target="tpu_custom_call" | custom-call | flops 905969664 | bytes 3567720 | tf_op jit(solution)/shard_map/cross/pallas_call | solution.py:214
  54.3 0.7 collective-permute-start.12
  55.0 0.7 collective-permute-start.13
  55.7 8.0 %collective-permute-start.14 = (bf16[512,384]{1,0:T(8,128)(2,1)S(1)}, bf16[512,384]{1,0:T(8,128)(2,1)S(1)}, u32[]{:S(2)}, u32[]{:S(2)}) collective-permute-start(bf16[512,384]{1,0:T(8,128)(2,1)S(1)} %get-tuple-element.38), channel_id=1, source_target_pairs={{384,256},{256,384},{385,257},{257,385},{386,258},{258,386},{387,2... | collective-permute-start | bytes 1179656 | tf_op jit(solution)/shard_map/ppermute | solution.py:249
  63.8 4.1 %selfatt.1 = (f32[256,384]{1,0:T(8,128)S(1)}, f32[256,384]{1,0:T(8,128)S(1)}, f32[256,384]{1,0:T(8,128)S(1)}, f32[256,384]{1,0:T(8,128)S(1)}, bf16[512,384]{1,0:...) custom-call(s32[26]{0:T(128)S(1)} %pad_add_fusion.scal, f32[16,256]{1,0:T(8,128)S(1)} %psum.14.sums, f32[2,4,384]{2,1,0:T(4,128)S(1)} %copy-done.8, ...), custom_call_target="tpu_custom_call" | custom-call | flops 905969664 | bytes 3960936 | tf_op jit(solution)/shard_map/selfatt/pallas_call | solution.py:214
  67.9 1.9 %collective-permute-start.10 = (bf16[512,384]{1,0:T(8,128)(2,1)S(1)}, bf16[512,384]{1,0:T(8,128)(2,1)S(1)}, u32[]{:S(2)}, u32[]{:S(2)}) collective-permute-start(bf16[512,384]{1,0:T(8,128)(2,1)S(1)} %get-tuple-element.34), channel_id=1, source_target_pairs={{0,4},{4,8},{8,12},{12,16},{16,20},{20,24},{24,28},{28,32},{32,36}... | collective-permute-start | bytes 1179656 | tf_op jit(solution)/shard_map/ppermute | solution.py:255
  69.8 6.0 %collective-permute-start.11 = (bf16[512,384]{1,0:T(8,128)(2,1)S(1)}, bf16[512,384]{1,0:T(8,128)(2,1)S(1)}, u32[]{:S(2)}, u32[]{:S(2)}) collective-permute-start(bf16[512,384]{1,0:T(8,128)(2,1)S(1)} %get-tuple-element.35), channel_id=1, source_target_pairs={{4,0},{8,4},{12,8},{16,12},{20,16},{24,20},{28,24},{32,28},{36,32}... | collective-permute-start | bytes 1179656 | tf_op jit(solution)/shard_map/ppermute | solution.py:254
  75.9 2.2 %collective-permute-done.14.r2 = bf16[512,384]{1,0:T(8,128)(2,1)S(1)} collective-permute-done((bf16[512,384]{1,0:T(8,128)(2,1)S(1)}, bf16[512,384]{1,0:T(8,128)(2,1)S(1)}, u32[]{:S(2)}, u32[]{:S(2)}) %collective-permute-start.14) | collective-permute-done | bytes 393248 | tf_op jit(solution)/shard_map/ppermute | solution.py:249
  78.0 7.4 %collective-permute-done.10.rb = bf16[512,384]{1,0:T(8,128)(2,1)S(1)} collective-permute-done((bf16[512,384]{1,0:T(8,128)(2,1)S(1)}, bf16[512,384]{1,0:T(8,128)(2,1)S(1)}, u32[]{:S(2)}, u32[]{:S(2)}) %collective-permute-start.10) | collective-permute-done | bytes 393248 | tf_op jit(solution)/shard_map/ppermute | solution.py:255
  85.5 4.1 %collective-permute-done.11.ra = bf16[512,384]{1,0:T(8,128)(2,1)S(1)} collective-permute-done((bf16[512,384]{1,0:T(8,128)(2,1)S(1)}, bf16[512,384]{1,0:T(8,128)(2,1)S(1)}, u32[]{:S(2)}, u32[]{:S(2)}) %collective-permute-start.11) | collective-permute-done | bytes 393248 | tf_op jit(solution)/shard_map/ppermute | solution.py:254
  89.6 1.8 %gather.1 = (bf16[256,384]{1,0:T(8,128)(2,1)}, bf16[256,384]{1,0:T(8,128)(2,1)}, bf16[256,384]{1,0:T(8,128)(2,1)}, f32[256,384]{1,0:T(8,128)S(1)}, f32[256,384]{1,0:T(8,128)S(1)}, /*index=5*/f32[8,256]{1,0:T(8,128)S(1)}) custom-call(s32[26]{0:T(128)S(1)} %pad_add_fusion.scal, f32[2,4,384]{2,1,0:T(4,128)S(1)} %copy-done.8, bf16[256,384]{1,0:T(8,128)(2,1)S(1)} %copy-done.1, ...), custom_call_target="tpu_custom_call" | custom-call | bytes 6508648 | tf_op jit(solution)/shard_map/gather/pallas_call | solution.py:214
  91.4 7.9 %psum.15.inner = f32[8,256]{1,0:T(8,128)S(1)} all-reduce(f32[8,256]{1,0:T(8,128)S(1)} %get-tuple-element.40), channel_id=1, replica_groups=mesh['y'=4,'t'=32,'head'=4] {'head'}, use_global_device_ids=true, to_apply=%region_1.0 | all-reduce | flops 2048 | bytes 16384 | tf_op jit(solution)/shard_map/psum | solution.py:261
  99.3 1.8 %final.1 = (bf16[256,384]{1,0:T(8,128)(2,1)}, bf16[256,384]{1,0:T(8,128)(2,1)}, bf16[256,384]{1,0:T(8,128)(2,1)}, bf16[256,384]{1,0:T(8,128)(2,1)}) custom-call(s32[26]{0:T(128)S(1)} %pad_add_fusion.scal, f32[2,4,384]{2,1,0:T(4,128)S(1)} %copy-done.8, f32[16,256]{1,0:T(8,128)S(1)} %psum.14.sums, f32[8,256]{1,0:T(8,128)S(1)} %psum.15.inner, ...), custom_call_target="tpu_custom_call" | custom-call | bytes 3182696 | tf_op jit(solution)/shard_map/final/pallas_call | solution.py:214
  (38 shorter events, 0.9 us)
Async XLA Ops:
  0.6 12.3 %collective-permute-start.1 = (bf16[256,384]{1,0:T(8,128)(2,1)}, bf16[256,384]{1,0:T(8,128)(2,1)S(1)}, u32[]{:S(2)}, u32[]{:S(2)}) collective-permute-start(bf16[256,384]{1,0:T(8,128)(2,1)} %sk.3), channel_id=1, source_target_pairs={{4,0},{8,4},{12,8},{16,12},{20,16},{24,20},{28,24},{32,28},{36,32}... | collective-permute-start | bytes 589832 | tf_op jit(solution)/shard_map/ppermute | solution.py:237
  5.7 10.6 %collective-permute-start = (bf16[256,384]{1,0:T(8,128)(2,1)}, bf16[256,384]{1,0:T(8,128)(2,1)S(1)}, u32[]{:S(2)}, u32[]{:S(2)}) collective-permute-start(bf16[256,384]{1,0:T(8,128)(2,1)} %sk.3), channel_id=1, source_target_pairs={{0,4},{4,8},{8,12},{12,16},{16,20},{20,24},{24,28},{28,32},{32,36}... | collective-permute-start | bytes 589832 | tf_op jit(solution)/shard_map/ppermute | solution.py:236
  7.6 15.6 %collective-permute-start.4 = (bf16[256,384]{1,0:T(8,128)(2,1)}, bf16[256,384]{1,0:T(8,128)(2,1)S(1)}, u32[]{:S(2)}, u32[]{:S(2)}) collective-permute-start(bf16[256,384]{1,0:T(8,128)(2,1)} %ck.3), channel_id=1, source_target_pairs={{384,256},{256,384},{385,257},{257,385},{386,258},{258,386},{387,2... | collective-permute-start | bytes 589832 | tf_op jit(solution)/shard_map/ppermute | solution.py:235
  10.8 13.4 %collective-permute-start.3 = (bf16[256,384]{1,0:T(8,128)(2,1)}, bf16[256,384]{1,0:T(8,128)(2,1)S(1)}, u32[]{:S(2)}, u32[]{:S(2)}) collective-permute-start(bf16[256,384]{1,0:T(8,128)(2,1)} %ck.3), channel_id=1, source_target_pairs={{384,128},{128,384},{385,129},{129,385},{386,130},{130,386},{387,1... | collective-permute-start | bytes 589832 | tf_op jit(solution)/shard_map/ppermute | solution.py:235
  11.5 15.9 %collective-permute-start.2 = (bf16[256,384]{1,0:T(8,128)(2,1)}, bf16[256,384]{1,0:T(8,128)(2,1)S(1)}, u32[]{:S(2)}, u32[]{:S(2)}) collective-permute-start(bf16[256,384]{1,0:T(8,128)(2,1)} %ck.3), channel_id=1, source_target_pairs={{384,0},{0,384},{385,1},{1,385},{386,2},{2,386},{387,3},{3,387},{3... | collective-permute-start | bytes 589832 | tf_op jit(solution)/shard_map/ppermute | solution.py:235
  12.2 0.7 copy-start.13
  12.9 36.7 %collective-permute-start.7 = (bf16[256,384]{1,0:T(8,128)(2,1)}, bf16[256,384]{1,0:T(8,128)(2,1)S(1)}, u32[]{:S(2)}, u32[]{:S(2)}) collective-permute-start(bf16[256,384]{1,0:T(8,128)(2,1)} %param.14), channel_id=1, source_target_pairs={{384,0},{0,384},{385,1},{1,385},{386,2},{2,386},{387,3},{3,387},{3... | collective-permute-start | bytes 589832 | tf_op jit(solution)/shard_map/ppermute | solution.py:235
  16.3 33.4 %collective-permute-start.9 = (bf16[256,384]{1,0:T(8,128)(2,1)}, bf16[256,384]{1,0:T(8,128)(2,1)S(1)}, u32[]{:S(2)}, u32[]{:S(2)}) collective-permute-start(bf16[256,384]{1,0:T(8,128)(2,1)} %param.14), channel_id=1, source_target_pairs={{384,256},{256,384},{385,257},{257,385},{386,258},{258,386},{387,2... | collective-permute-start | bytes 589832 | tf_op jit(solution)/shard_map/ppermute | solution.py:235
  23.2 26.4 %collective-permute-start.8 = (bf16[256,384]{1,0:T(8,128)(2,1)}, bf16[256,384]{1,0:T(8,128)(2,1)S(1)}, u32[]{:S(2)}, u32[]{:S(2)}) collective-permute-start(bf16[256,384]{1,0:T(8,128)(2,1)} %param.14), channel_id=1, source_target_pairs={{384,128},{128,384},{385,129},{129,385},{386,130},{130,386},{387,1... | collective-permute-start | bytes 589832 | tf_op jit(solution)/shard_map/ppermute | solution.py:235
  24.2 39.5 %collective-permute-start.5 = (bf16[256,384]{1,0:T(8,128)(2,1)}, bf16[256,384]{1,0:T(8,128)(2,1)S(1)}, u32[]{:S(2)}, u32[]{:S(2)}) collective-permute-start(bf16[256,384]{1,0:T(8,128)(2,1)} %v_ref.1), channel_id=1, source_target_pairs={{0,4},{4,8},{8,12},{12,16},{16,20},{20,24},{24,28},{28,32},{32,36}... | collective-permute-start | bytes 589832 | tf_op jit(solution)/shard_map/ppermute | solution.py:236
  27.4 36.3 %collective-permute-start.6 = (bf16[256,384]{1,0:T(8,128)(2,1)}, bf16[256,384]{1,0:T(8,128)(2,1)S(1)}, u32[]{:S(2)}, u32[]{:S(2)}) collective-permute-start(bf16[256,384]{1,0:T(8,128)(2,1)} %v_ref.1), channel_id=1, source_target_pairs={{4,0},{8,4},{12,8},{16,12},{20,16},{24,20},{28,24},{32,28},{36,32}... | collective-permute-start | bytes 589832 | tf_op jit(solution)/shard_map/ppermute | solution.py:237
  32.2 0.9 copy-start
  33.2 0.9 copy-start.2
  34.1 0.9 copy-start.4
  35.0 0.9 copy-start.6
  36.0 14.4 %copy-start.5 = (bf16[256,384]{1,0:T(8,128)(2,1)S(1)}, bf16[256,384]{1,0:T(8,128)(2,1)}, u32[]{:S(2)}) copy-start(bf16[256,384]{1,0:T(8,128)(2,1)} %cq.3) | copy-start | bytes 589828
  36.0 14.4 %copy-start.10 = (bf16[256,384]{1,0:T(8,128)(2,1)S(1)}, bf16[256,384]{1,0:T(8,128)(2,1)}, u32[]{:S(2)}) copy-start(bf16[256,384]{1,0:T(8,128)(2,1)} %do_ref.3) | copy-start | bytes 589828
  36.4 13.9 %copy-start.8 = (f32[2,4,384]{2,1,0:T(4,128)S(1)}, f32[2,4,384]{2,1,0:T(4,128)}, u32[]{:S(2)}) copy-start(f32[2,4,384]{2,1,0:T(4,128)} %gains.7) | copy-start | bytes 36868
  49.6 14.1 %copy-start.1 = (bf16[256,384]{1,0:T(8,128)(2,1)S(1)}, bf16[256,384]{1,0:T(8,128)(2,1)}, u32[]{:S(2)}) copy-start(bf16[256,384]{1,0:T(8,128)(2,1)} %sq.3) | copy-start | bytes 589828
  49.6 14.1 %copy-start.3 = (bf16[256,384]{1,0:T(8,128)(2,1)S(1)}, bf16[256,384]{1,0:T(8,128)(2,1)}, u32[]{:S(2)}) copy-start(bf16[256,384]{1,0:T(8,128)(2,1)} %sk.3) | copy-start | bytes 589828
  49.6 14.1 %copy-start.9 = (bf16[256,384]{1,0:T(8,128)(2,1)S(1)}, bf16[256,384]{1,0:T(8,128)(2,1)}, u32[]{:S(2)}) copy-start(bf16[256,384]{1,0:T(8,128)(2,1)} %v_ref.1) | copy-start | bytes 589828
  49.6 0.7 copy-start.11
  50.3 0.9 copy-start.12
  54.3 21.6 %collective-permute-start.12 = (bf16[512,384]{1,0:T(8,128)(2,1)S(1)}, bf16[512,384]{1,0:T(8,128)(2,1)S(1)}, u32[]{:S(2)}, u32[]{:S(2)}) collective-permute-start(bf16[512,384]{1,0:T(8,128)(2,1)S(1)} %get-tuple-element.36), channel_id=1, source_target_pairs={{384,0},{0,384},{385,1},{1,385},{386,2},{2,386},{387,3},{3,387},{3... | collective-permute-start | bytes 1179656 | tf_op jit(solution)/shard_map/ppermute | solution.py:249
  55.0 20.9 %collective-permute-start.13 = (bf16[512,384]{1,0:T(8,128)(2,1)S(1)}, bf16[512,384]{1,0:T(8,128)(2,1)S(1)}, u32[]{:S(2)}, u32[]{:S(2)}) collective-permute-start(bf16[512,384]{1,0:T(8,128)(2,1)S(1)} %get-tuple-element.37), channel_id=1, source_target_pairs={{384,128},{128,384},{385,129},{129,385},{386,130},{130,386},{387,1... | collective-permute-start | bytes 1179656 | tf_op jit(solution)/shard_map/ppermute | solution.py:249
  55.6 33.9 %copy-start.7 = (bf16[256,384]{1,0:T(8,128)(2,1)S(1)}, bf16[256,384]{1,0:T(8,128)(2,1)}, u32[]{:S(2)}) copy-start(bf16[256,384]{1,0:T(8,128)(2,1)} %ck.3) | copy-start | bytes 589828
  55.7 22.4 %collective-permute-start.14 = (bf16[512,384]{1,0:T(8,128)(2,1)S(1)}, bf16[512,384]{1,0:T(8,128)(2,1)S(1)}, u32[]{:S(2)}, u32[]{:S(2)}) collective-permute-start(bf16[512,384]{1,0:T(8,128)(2,1)S(1)} %get-tuple-element.38), channel_id=1, source_target_pairs={{384,256},{256,384},{385,257},{257,385},{386,258},{258,386},{387,2... | collective-permute-start | bytes 1179656 | tf_op jit(solution)/shard_map/ppermute | solution.py:249
  67.9 17.6 %collective-permute-start.10 = (bf16[512,384]{1,0:T(8,128)(2,1)S(1)}, bf16[512,384]{1,0:T(8,128)(2,1)S(1)}, u32[]{:S(2)}, u32[]{:S(2)}) collective-permute-start(bf16[512,384]{1,0:T(8,128)(2,1)S(1)} %get-tuple-element.34), channel_id=1, source_target_pairs={{0,4},{4,8},{8,12},{12,16},{16,20},{20,24},{24,28},{28,32},{32,36}... | collective-permute-start | bytes 1179656 | tf_op jit(solution)/shard_map/ppermute | solution.py:255
  69.8 19.8 %collective-permute-start.11 = (bf16[512,384]{1,0:T(8,128)(2,1)S(1)}, bf16[512,384]{1,0:T(8,128)(2,1)S(1)}, u32[]{:S(2)}, u32[]{:S(2)}) collective-permute-start(bf16[512,384]{1,0:T(8,128)(2,1)S(1)} %get-tuple-element.35), channel_id=1, source_target_pairs={{4,0},{8,4},{12,8},{16,12},{20,16},{24,20},{28,24},{32,28},{36,32}... | collective-permute-start | bytes 1179656 | tf_op jit(solution)/shard_map/ppermute | solution.py:254

commit v2 on v1

--- a/solution.py
+++ b/solution.py
@@ -37,8 +37,18 @@
     ins, out = refs[:-1], refs[-1]
     out[...] = jnp.zeros(out.shape, F32)
     for i, ref in enumerate(ins):
-        wide = ref[...].astype(F32)
+        wide = ref[0:TOK, :].astype(F32)
         out[i : i + 1, :] = row_sums(wide * wide)
+
+
+def more_squares_kernel(own, *refs):
+    ins, out = refs[:-1], refs[-1]
+    out[0:8, :] = own[...]
+    out[8:16, :] = jnp.zeros((8, TOK), F32)
+    for i, ref in enumerate(ins):
+        wide = ref[0:TOK, :].astype(F32)
+        row = (8, 4, 6, 7, 5)[i]
+        out[row : row + 1, :] = row_sums(wide * wide)
 
 
 def attend(heads_q, heads_k, heads_v, heads_do, biases, masks):
@@ -71,8 +81,12 @@
     return out, dq, dks, dvs
 
 
+def over_heads(ref):
+    return ref[0] + ref[1] + ref[2] + ref[3]
+
+
 def inverse_rms(sums_ref):
-    return jnp.transpose(lax.rsqrt(sums_ref[...] * (1.0 / WIDTH) + EPSILON))
+    return jnp.transpose(lax.rsqrt(over_heads(sums_ref) * (1.0 / WIDTH) + EPSILON))
 
 
 def normed(raw, inv, gain):
@@ -80,7 +94,7 @@
 
 
 def self_kernel(
-    scal, sums, gains, q_ref, k_ref, v_ref, do_ref, kb_ref, vb_ref, ka_ref, va_ref,
+    scal, sums, gains, q_ref, k_ref, v_ref, do_ref, b_ref, a_ref,
     out_ref, dq_ref, dk_ref, dv_ref, pb_ref, pa_ref,
 ):
     group, slot = scal[0], scal[1]
@@ -96,10 +110,10 @@
         do = do_ref[:, c]
         kn = [
             normed(k_ref[:, c], inv[:, 1:2], gk),
-            normed(kb_ref[:, c], inv[:, 4:5], gk),
-            normed(ka_ref[:, c], inv[:, 5:6], gk),
+            normed(b_ref[0:TOK, c], inv[:, 4:5], gk),
+            normed(a_ref[0:TOK, c], inv[:, 5:6], gk),
         ]
-        vs = [v_ref[:, c], vb_ref[:, c], va_ref[:, c]]
+        vs = [v_ref[:, c], b_ref[TOK:, c], a_ref[TOK:, c]]
         out, dq, dks, dvs = attend(qn, kn, vs, do, [None, bias_b, bias_a], [None] * 3)
         out_ref[:, c] = out
         dq_ref[:, c] = dq
@@ -111,7 +125,7 @@
 
 
 def cross_kernel(
-    scal, sums, gains, q_ref, do_ref, k0, v0, k1, v1, k2, v2,
+    scal, sums, gains, q_ref, do_ref, i0, i1, i2, s_ref,
     out_ref, dq_ref, p0, p1, p2,
 ):
     group = scal[0]
@@ -137,10 +151,10 @@
             c = slice(h * DH, (h + 1) * DH)
             qn = normed(q_ref[:, c], inv[:, 2:3], gains[1, 2:3, c])
             do = do_ref[:, c]
-            kn = [normed(k[:, c], inv[:, 6 + j : 7 + j], gains[0, 3:4, c]) for j, k in enumerate((k0, k1, k2))]
-            vs = [v[:, c] for v in (v0, v1, v2)]
+            kn = [normed(r[0:TOK, c], inv[:, 6 + j : 7 + j], gains[0, 3:4, c]) for j, r in enumerate((i0, i1, i2))]
+            vs = [r[TOK:, c] for r in (i0, i1, i2)]
             out, dq, dks, dvs = attend(qn, kn, vs, do, [None] * 3, masks)
-            out_ref[:, c] = out
+            out_ref[:, c] = (out + s_ref[:, c]).astype(BF16)
             dq_ref[:, c] = dq
             for ref, dk, dv in zip((p0, p1, p2), dks, dvs):
                 ref[0:TOK, c] = dk.astype(BF16)
@@ -162,10 +176,10 @@
             c = slice(h * DH, (h + 1) * DH)
             qn = normed(q_ref[:, c], inv[:, 2:3], gains[0, 2:3, c])
             do = do_ref[:, c]
-            kn = normed(pick(k0[:, c], k1[:, c], k2[:, c]), inv_k, gains[1, 3:4, c])
-            v = pick(v0[:, c], v1[:, c], v2[:, c])
+            kn = normed(pick(i0[0:TOK, c], i1[0:TOK, c], i2[0:TOK, c]), inv_k, gains[1, 3:4, c])
+            v = pick(i0[TOK:, c], i1[TOK:, c], i2[TOK:, c])
             out, dq, dks, dvs = attend(qn, [kn], [v], do, [None], [mask])
-            out_ref[:, c] = out
+            out_ref[:, c] = (out + s_ref[:, c]).astype(BF16)
             dq_ref[:, c] = dq
             dk = dks[0].astype(BF16)
             dv = dvs[0].astype(BF16)
@@ -178,11 +192,10 @@
 
 
 def gather_kernel(
-    scal, gains, sq, sk, cq, ck, so, co, sdq, cdq, sdk, sdv, rb, ra, r0, r1, r2,
-    att, svg, cvg, dks_ref, dkc_ref, inner,
+    scal, gains, sq, sk, cq, ck, sdq, cdq, sdk, sdv, rb, r1, r0, r2, ra,
+    svg, cvg, dks_ref, dkc_ref, inner,
 ):
     tower = (scal[0] == 3).astype(jnp.int32)
-    att[...] = (so[...] + co[...]).astype(BF16)
     dks = sdk[...] + rb[0:TOK, :].astype(F32) + ra[0:TOK, :].astype(F32)
     svg[...] = (sdv[...] + rb[TOK:, :].astype(F32) + ra[TOK:, :].astype(F32)).astype(BF16)
     dkc = r0[0:TOK, :].astype(F32) + r1[0:TOK, :].astype(F32) + r2[0:TOK, :].astype(F32)
@@ -197,7 +210,7 @@
 def final_kernel(scal, gains, sums, inner, sq, sk, cq, ck, y0, y1, y2, y3, o0, o1, o2, o3):
     tower = (scal[0] == 3).astype(jnp.int32)
     inv = inverse_rms(sums)
-    mean = jnp.transpose(inner[...]) * (1.0 / WIDTH)
+    mean = jnp.transpose(over_heads(inner)) * (1.0 / WIDTH)
     for i, (x, y, o) in enumerate(zip((sq, sk, cq, ck), (y0, y1, y2, y3), (o0, o1, o2, o3))):
         r = inv[:, i : i + 1]
         o[...] = (
@@ -232,33 +245,37 @@
     spans = lax.dynamic_slice_in_dim(span.reshape(3, NSUB * slots, 2), slot * NSUB, NSUB, 1)
     scal = jnp.concatenate([jnp.stack([group, slot]).astype(jnp.int32), spans.reshape(-1)])
 
-    c_in = [(lax.ppermute(ck, "y", p), lax.ppermute(cv, "y", p)) for p in pairs]
-    kb, vb = lax.ppermute(sk, "t", up), lax.ppermute(sv, "t", up)
-    ka, va = lax.ppermute(sk, "t", down), lax.ppermute(sv, "t", down)
-
-    sums = call(
-        squares_kernel, "squares", 0, [shape(16, F32, TOK)], sq, sk, cq, ck, kb, ka, c_in[0][0], c_in[1][0], c_in[2][0]
-    )[0]
-    sums = lax.psum(sums, "head")
-
-    flat = [a for pair in c_in for a in pair]
-    c_out, c_dq, *c_parts = call(
-        cross_kernel, "cross", 1, [shape(TOK, F32)] * 2 + [shape(2 * TOK, BF16)] * 3, scal, sums, gains, cq, do, *flat,
-        flops=12 * HEADS * TOK * 3 * TOK * DH,
-    )
-    c_back = [lax.ppermute(part, "y", p) for part, p in zip(c_parts, pairs)]
+    s_kv, c_kv = jnp.concatenate([sk, sv]), jnp.concatenate([ck, cv])
+    own = call(squares_kernel, "squares", 0, [shape(8, F32, TOK)], sq, sk, cq, ck)[0]
+    c_in = [None] * 3
+    s_a = lax.ppermute(s_kv, "t", down)
+    c_in[1] = lax.ppermute(c_kv, "y", pairs[1])
+    c_in[0] = lax.ppermute(c_kv, "y", pairs[0])
+    s_later, s_a = lax.optimization_barrier((s_kv, s_a))
+    s_b = lax.ppermute(s_later, "t", up)
+    c_in[2] = lax.ppermute(c_kv, "y", pairs[2])
+    sums = call(more_squares_kernel, "more", 0, [shape(16, F32, TOK)], own, c_in[2], s_b, c_in[0], c_in[1], s_a)[0]
+    sums = lax.all_gather(sums, "head")
+
     s_out, s_dq, s_dk, s_dv, part_b, part_a = call(
-        self_kernel, "selfatt", 1, [shape(TOK, F32)] * 4 + [shape(2 * TOK, BF16)] * 2, scal, sums, gains, sq, sk, sv, do,
-        kb, vb, ka, va, flops=12 * HEADS * TOK * 3 * TOK * DH,
-    )
-    back_a = lax.ppermute(part_b, "t", down)
+        self_kernel, "selfatt", 1, [shape(TOK, F32)] + [shape(TOK, F32)] * 3 + [shape(2 * TOK, BF16)] * 2,
+        scal, sums, gains, sq, sk, sv, do, s_b, s_a, flops=12 * HEADS * TOK * 3 * TOK * DH,
+    )
+    att, c_dq, *c_parts = call(
+        cross_kernel, "cross", 1, [shape(TOK, BF16), shape(TOK, F32)] + [shape(2 * TOK, BF16)] * 3,
+        scal, sums, gains, cq, do, *c_in, s_out, flops=12 * HEADS * TOK * 3 * TOK * DH,
+    )
     back_b = lax.ppermute(part_a, "t", up)
-
-    att, svg, cvg, dks, dkc, inner = call(
-        gather_kernel, "gather", 1, [shape(TOK, BF16)] * 3 + [shape(TOK, F32)] * 2 + [shape(8, F32, TOK)],
-        scal, gains, sq, sk, cq, ck, s_out, c_out, s_dq, c_dq, s_dk, s_dv, back_b, back_a, *c_back,
-    )
-    inner = lax.psum(inner, "head")
+    part_later, back_b = lax.optimization_barrier((part_b, back_b))
+    c_back = [None] * 3
+    for j in (1, 0, 2):
+        c_back[j] = lax.ppermute(c_parts[j], "y", pairs[j])
+    back_a = lax.ppermute(part_later, "t", down)
+    svg, cvg, dks, dkc, inner = call(
+        gather_kernel, "gather", 1, [shape(TOK, BF16)] * 2 + [shape(TOK, F32)] * 2 + [shape(8, F32, TOK)],
+        scal, gains, sq, sk, cq, ck, s_dq, c_dq, s_dk, s_dv, back_b, c_back[1], c_back[0], c_back[2], back_a,
+    )
+    inner = lax.all_gather(inner, "head")
     g0, g1, g2, g3 = call(
         final_kernel, "final", 1, [shape(TOK, BF16)] * 4, scal, gains, sums, inner, sq, sk, cq, ck, s_dq, dks, c_dq, dkc
     )

time: 102 us -> 84 us (0.82)
  the two profiles are of different devices: /device:TPU:400 before, /device:TPU:127 now
where the time goes in v2:
time: 84 us; the launch traced here: 83.5 us
  waiting for transfers between devices  27.3 us (32%)
  starting transfers between devices  24.8 us (30%)
  blocking collectives  14 us (17%)
  Pallas kernels  13.1 us (16%)
  local copies, waits for them, and re-layouts  3.43 us (4%)
    ppermute x3, waiting for transfers between devices, on_device(): c_back[j] = lax.ppermute(c_parts[j], 'y', pairs[j])  15.2 us
    pallas_call x6, Pallas kernels, call(): pl.pallas_call(kernel, name=name, out_shape=outs, in_specs=[SSPEC] * scal...  13.1 us
    ppermute x1, waiting for transfers between devices, on_device(): c_in[0] = lax.ppermute(c_kv, 'y', pairs[0])  8.72 us
    all_gather x1, blocking collectives, on_device(): sums = lax.all_gather(sums, 'head')  7.07 us
    all_gather x1, blocking collectives, on_device(): inner = lax.all_gather(inner, 'head')  6.97 us
    ppermute x3, starting transfers between devices, on_device(): c_back[j] = lax.ppermute(c_parts[j], 'y', pairs[j])  5.75 us
    ppermute x1, starting transfers between devices, on_device(): back_b = lax.ppermute(part_a, 't', up)  4.98 us
    ppermute x1, waiting for transfers between devices, on_device(): s_a = lax.ppermute(s_kv, 't', down)  3.39 us
  transfers between devices with their start and end apart: 10, of which 4 were waited for; matrix products, arithmetic and copies ran while one was open for 2% of the time, Pallas kernels for 6%

profile of v2, /device:TPU:127, one launch (start us, length us, event | category | flops | bytes accessed | tf_op | source)
XLA Modules:
  0.0 83.5 jit_solution(17632778580680093824)
XLA Ops:
  0.6 1.0 %constant_dynamic-update-slice_fusion.3 = bf16[512,384]{1,0:T(8,128)(2,1)S(1)} fusion(bf16[256,384]{1,0:T(8,128)(2,1)} %sk.3), kind=kLoop, calls=%fused_computation.3 | loop fusion | bytes 393216
  1.6 0.0 copy-done.4
  1.7 2.6 %collective-permute-start.1 = (bf16[512,384]{1,0:T(8,128)(2,1)S(1)}, bf16[512,384]{1,0:T(8,128)(2,1)S(1)}, u32[]{:S(2)}, u32[]{:S(2)}) collective-permute-start(bf16[512,384]{1,0:T(8,128)(2,1)S(1)} %constant_dynamic-update-slice_fusion.2), channel_id=1, source_target_pairs={{4,0},{8,4},{12,8},{16,12},{20,16},{24,20},{28,24},{32,28},{36,32}... | collective-permute-start | bytes 1179656 | tf_op jit(solution)/shard_map/ppermute | solution.py:251
  4.3 0.7 constant_dynamic-update-slice_fusion.1
  5.0 0.7 constant_dynamic-update-slice_fusion
  5.7 2.9 %collective-permute-start.4 = (bf16[512,384]{1,0:T(8,128)(2,1)}, bf16[512,384]{1,0:T(8,128)(2,1)S(1)}, u32[]{:S(2)}, u32[]{:S(2)}) collective-permute-start(bf16[512,384]{1,0:T(8,128)(2,1)} %constant_dynamic-update-slice_fusion), channel_id=1, source_target_pairs={{384,128},{128,384},{385,129},{129,385},{386,130},{130,386},{387,1... | collective-permute-start | bytes 1179656 | tf_op jit(solution)/shard_map/ppermute | solution.py:252
  8.6 1.9 %collective-permute-start.3 = (bf16[512,384]{1,0:T(8,128)(2,1)}, bf16[512,384]{1,0:T(8,128)(2,1)S(1)}, u32[]{:S(2)}, u32[]{:S(2)}) collective-permute-start(bf16[512,384]{1,0:T(8,128)(2,1)} %constant_dynamic-update-slice_fusion), channel_id=1, source_target_pairs={{384,0},{0,384},{385,1},{1,385},{386,2},{2,386},{387,3},{3,387},{3... | collective-permute-start | bytes 1179656 | tf_op jit(solution)/shard_map/ppermute | solution.py:253
  10.5 1.9 %collective-permute-start = (bf16[512,384]{1,0:T(8,128)(2,1)}, bf16[512,384]{1,0:T(8,128)(2,1)S(1)}, u32[]{:S(2)}, u32[]{:S(2)}) collective-permute-start(bf16[512,384]{1,0:T(8,128)(2,1)} %constant_dynamic-update-slice_fusion), channel_id=1, source_target_pairs={{384,256},{256,384},{385,257},{257,385},{386,258},{258,386},{387,2... | collective-permute-start | bytes 1179656 | tf_op jit(solution)/shard_map/ppermute | solution.py:256
  12.4 3.4 %collective-permute-done.1.refs_4_.a_ref = bf16[512,384]{1,0:T(8,128)(2,1)S(1)} collective-permute-done((bf16[512,384]{1,0:T(8,128)(2,1)S(1)}, bf16[512,384]{1,0:T(8,128)(2,1)S(1)}, u32[]{:S(2)}, u32[]{:S(2)}) %collective-permute-start.1) | collective-permute-done | bytes 393248 | tf_op jit(solution)/shard_map/ppermute | solution.py:251
  15.8 2.9 %collective-permute-start.2 = (bf16[512,384]{1,0:T(8,128)(2,1)S(1)}, bf16[512,384]{1,0:T(8,128)(2,1)S(1)}, u32[]{:S(2)}, u32[]{:S(2)}) collective-permute-start(bf16[512,384]{1,0:T(8,128)(2,1)S(1)} %constant_dynamic-update-slice_fusion.2), channel_id=1, source_target_pairs={{0,4},{4,8},{8,12},{12,16},{16,20},{20,24},{24,28},{28,32},{32,36}... | collective-permute-start | bytes 1179656 | tf_op jit(solution)/shard_map/ppermute | solution.py:255
  18.7 0.0 copy-start.8
  18.8 0.7 copy-done.8
  19.4 0.1 constant_dynamic-slice_fusion
  19.5 0.1 copy.17
  19.6 0.1 reshape.21
  19.7 0.2 squares.1.own
  20.0 0.1 pad_add_fusion.scal
  20.1 8.7 %collective-permute-done.3.refs_2_.i0 = bf16[512,384]{1,0:T(8,128)(2,1)S(1)} collective-permute-done((bf16[512,384]{1,0:T(8,128)(2,1)}, bf16[512,384]{1,0:T(8,128)(2,1)S(1)}, u32[]{:S(2)}, u32[]{:S(2)}) %collective-permute-start.3) | collective-permute-done | bytes 393248 | tf_op jit(solution)/shard_map/ppermute | solution.py:253
  28.8 0.3 more.1
  29.1 7.1 %all-gather = f32[64,256]{1,0:T(8,128)S(1)} all-gather(f32[16,256]{1,0:T(8,128)S(1)} %more.1), channel_id=2, replica_groups=mesh['y'=4,'t'=32,'head'=4] {'head'}, dimensions={0}, use_global_device_ids=true | all-gather | bytes 81920 | tf_op jit(solution)/shard_map/all_gather | solution.py:258
  36.1 4.1 %selfatt.1 = (f32[256,384]{1,0:T(8,128)S(1)}, f32[256,384]{1,0:T(8,128)S(1)}, f32[256,384]{1,0:T(8,128)S(1)}, f32[256,384]{1,0:T(8,128)S(1)}, bf16[512,384]{1,0:...) custom-call(s32[26]{0:T(128)S(1)} %pad_add_fusion.scal, f32[4,16,256]{2,1,0:T(8,128)S(1)} %bitcast.6, ...), custom_call_target="tpu_custom_call" | custom-call | flops 905969664 | bytes 4010088 | tf_op jit(solution)/shard_map/selfatt/pallas_call | solution.py:227
  40.3 5.0 %collective-permute-start.5 = (bf16[512,384]{1,0:T(8,128)(2,1)S(1)}, bf16[512,384]{1,0:T(8,128)(2,1)S(1)}, u32[]{:S(2)}, u32[]{:S(2)}) collective-permute-start(bf16[512,384]{1,0:T(8,128)(2,1)S(1)} %get-tuple-element.40), channel_id=1, source_target_pairs={{0,4},{4,8},{8,12},{12,16},{16,20},{20,24},{24,28},{28,32},{32,36}... | collective-permute-start | bytes 1179656 | tf_op jit(solution)/shard_map/ppermute | solution.py:268
  45.3 4.9 %cross.1 = (bf16[256,384]{1,0:T(8,128)(2,1)}, f32[256,384]{1,0:T(8,128)S(1)}, bf16[512,384]{1,0:T(8,128)(2,1)S(1)}, bf16[512,384]{1,0:T(8,128)(2,1)S(1)}, bf16[512,384]{1,0:T(8,128)(2,1)S(1)}) custom-call(s32[26]{0:T(128)S(1)} %pad_add_fusion.scal, f32[4,16,256]{2,1,0:T(8,128)S(1)} %bitcast.7, f32[2,4,384]{2,1,0:T(4,128)S(1)} %copy-done.5, ...), custom_call_target="tpu_custom_call" | custom-call | flops 905969664 | bytes 3813480 | tf_op jit(solution)/shard_map/cross/pallas_call | solution.py:227
  50.1 1.9 %collective-permute-start.6 = (bf16[512,384]{1,0:T(8,128)(2,1)S(1)}, bf16[512,384]{1,0:T(8,128)(2,1)S(1)}, u32[]{:S(2)}, u32[]{:S(2)}) collective-permute-start(bf16[512,384]{1,0:T(8,128)(2,1)S(1)} %get-tuple-element.42), channel_id=1, source_target_pairs={{384,128},{128,384},{385,129},{129,385},{386,130},{130,386},{387,1... | collective-permute-start | bytes 1179656 | tf_op jit(solution)/shard_map/ppermute | solution.py:272
  52.0 1.9 %collective-permute-start.7 = (bf16[512,384]{1,0:T(8,128)(2,1)S(1)}, bf16[512,384]{1,0:T(8,128)(2,1)S(1)}, u32[]{:S(2)}, u32[]{:S(2)}) collective-permute-start(bf16[512,384]{1,0:T(8,128)(2,1)S(1)} %get-tuple-element.43), channel_id=1, source_target_pairs={{384,0},{0,384},{385,1},{1,385},{386,2},{2,386},{387,3},{3,387},{3... | collective-permute-start | bytes 1179656 | tf_op jit(solution)/shard_map/ppermute | solution.py:272
  54.0 1.9 %collective-permute-start.8 = (bf16[512,384]{1,0:T(8,128)(2,1)S(1)}, bf16[512,384]{1,0:T(8,128)(2,1)S(1)}, u32[]{:S(2)}, u32[]{:S(2)}) collective-permute-start(bf16[512,384]{1,0:T(8,128)(2,1)S(1)} %get-tuple-element.44), channel_id=1, source_target_pairs={{384,256},{256,384},{385,257},{257,385},{386,258},{258,386},{387,2... | collective-permute-start | bytes 1179656 | tf_op jit(solution)/shard_map/ppermute | solution.py:272
  55.9 1.9 %collective-permute-start.9 = (bf16[512,384]{1,0:T(8,128)(2,1)S(1)}, bf16[512,384]{1,0:T(8,128)(2,1)S(1)}, u32[]{:S(2)}, u32[]{:S(2)}) collective-permute-start(bf16[512,384]{1,0:T(8,128)(2,1)S(1)} %get-tuple-element.45), channel_id=1, source_target_pairs={{4,0},{8,4},{12,8},{16,12},{20,16},{24,20},{28,24},{32,28},{36,32}... | collective-permute-start | bytes 1179656 | tf_op jit(solution)/shard_map/ppermute | solution.py:273
  57.8 6.0 %collective-permute-done.6.r1 = bf16[512,384]{1,0:T(8,128)(2,1)S(1)} collective-permute-done((bf16[512,384]{1,0:T(8,128)(2,1)S(1)}, bf16[512,384]{1,0:T(8,128)(2,1)S(1)}, u32[]{:S(2)}, u32[]{:S(2)}) %collective-permute-start.6) | collective-permute-done | bytes 393248 | tf_op jit(solution)/shard_map/ppermute | solution.py:272
  63.8 9.2 %collective-permute-done.7.r0 = bf16[512,384]{1,0:T(8,128)(2,1)S(1)} collective-permute-done((bf16[512,384]{1,0:T(8,128)(2,1)S(1)}, bf16[512,384]{1,0:T(8,128)(2,1)S(1)}, u32[]{:S(2)}, u32[]{:S(2)}) %collective-permute-start.7) | collective-permute-done | bytes 393248 | tf_op jit(solution)/shard_map/ppermute | solution.py:272
  73.0 1.8 %gather.1 = (bf16[256,384]{1,0:T(8,128)(2,1)}, bf16[256,384]{1,0:T(8,128)(2,1)}, f32[256,384]{1,0:T(8,128)S(1)}, f32[256,384]{1,0:T(8,128)S(1)}, f32[8,256]{1,0:T(8,128)S(1)}) custom-call(s32[26]{0:T(128)S(1)} %pad_add_fusion.scal, f32[2,4,384]{2,1,0:T(4,128)S(1)} %copy-done.5, bf16[256,384]{1,0:T(8,128)(2,1)S(1)} %copy-done.2, ...), custom_call_target="tpu_custom_call" | custom-call | bytes 5525608 | tf_op jit(solution)/shard_map/gather/pallas_call | solution.py:227
  74.8 7.0 %all-gather.1 = f32[32,256]{1,0:T(8,128)S(1)} all-gather(f32[8,256]{1,0:T(8,128)S(1)} %get-tuple-element.46), channel_id=3, replica_groups=mesh['y'=4,'t'=32,'head'=4] {'head'}, dimensions={0}, use_global_device_ids=true | all-gather | bytes 40960 | tf_op jit(solution)/shard_map/all_gather | solution.py:278
  81.8 1.8 %final.1 = (bf16[256,384]{1,0:T(8,128)(2,1)}, bf16[256,384]{1,0:T(8,128)(2,1)}, bf16[256,384]{1,0:T(8,128)(2,1)}, bf16[256,384]{1,0:T(8,128)(2,1)}) custom-call(s32[26]{0:T(128)S(1)} %pad_add_fusion.scal, f32[2,4,384]{2,1,0:T(4,128)S(1)} %copy-done.5, f32[4,16,256]{2,1,0:T(8,128)S(1)} %bitcast.8, f32[4,8,256]{2,1,0:T(8,128)S(1)} %bitcast.9, ...), custom_call_target="tpu_custom_call" | custom-call | bytes 3256424 | tf_op jit(solution)/shard_map/final/pallas_call | solution.py:227
  (23 shorter events, 0.1 us)
Async XLA Ops:
  0.6 1.0 %copy-start.4 = (bf16[256,384]{1,0:T(8,128)(2,1)S(1)}, bf16[256,384]{1,0:T(8,128)(2,1)}, u32[]{:S(2)}) copy-start(bf16[256,384]{1,0:T(8,128)(2,1)} %v_ref.1) | copy-start | bytes 589828
  1.7 2.7 %copy-start.1 = (bf16[256,384]{1,0:T(8,128)(2,1)S(1)}, bf16[256,384]{1,0:T(8,128)(2,1)}, u32[]{:S(2)}) copy-start(bf16[256,384]{1,0:T(8,128)(2,1)} %ck.3) | copy-start | bytes 589828
  1.7 3.3 %copy-start.7 = (bf16[256,384]{1,0:T(8,128)(2,1)S(1)}, bf16[256,384]{1,0:T(8,128)(2,1)}, u32[]{:S(2)}) copy-start(bf16[256,384]{1,0:T(8,128)(2,1)} %param.14) | copy-start | bytes 589828
  1.7 14.1 %collective-permute-start.1 = (bf16[512,384]{1,0:T(8,128)(2,1)S(1)}, bf16[512,384]{1,0:T(8,128)(2,1)S(1)}, u32[]{:S(2)}, u32[]{:S(2)}) collective-permute-start(bf16[512,384]{1,0:T(8,128)(2,1)S(1)} %constant_dynamic-update-slice_fusion.2), channel_id=1, source_target_pairs={{4,0},{8,4},{12,8},{16,12},{20,16},{24,20},{28,24},{32,28},{36,32}... | collective-permute-start | bytes 1179656 | tf_op jit(solution)/shard_map/ppermute | solution.py:251
  4.3 15.4 %copy-start.3 = (bf16[256,384]{1,0:T(8,128)(2,1)S(1)}, bf16[256,384]{1,0:T(8,128)(2,1)}, u32[]{:S(2)}) copy-start(bf16[256,384]{1,0:T(8,128)(2,1)} %cq.3) | copy-start | bytes 589828
  5.0 14.7 %copy-start = (bf16[256,384]{1,0:T(8,128)(2,1)S(1)}, bf16[256,384]{1,0:T(8,128)(2,1)}, u32[]{:S(2)}) copy-start(bf16[256,384]{1,0:T(8,128)(2,1)} %sk.3) | copy-start | bytes 589828
  5.0 14.7 %copy-start.2 = (bf16[256,384]{1,0:T(8,128)(2,1)S(1)}, bf16[256,384]{1,0:T(8,128)(2,1)}, u32[]{:S(2)}) copy-start(bf16[256,384]{1,0:T(8,128)(2,1)} %sq.3) | copy-start | bytes 589828
  5.7 14.3 %collective-permute-start.4 = (bf16[512,384]{1,0:T(8,128)(2,1)}, bf16[512,384]{1,0:T(8,128)(2,1)S(1)}, u32[]{:S(2)}, u32[]{:S(2)}) collective-permute-start(bf16[512,384]{1,0:T(8,128)(2,1)} %constant_dynamic-update-slice_fusion), channel_id=1, source_target_pairs={{384,128},{128,384},{385,129},{129,385},{386,130},{130,386},{387,1... | collective-permute-start | bytes 1179656 | tf_op jit(solution)/shard_map/ppermute | solution.py:252
  8.6 20.2 %collective-permute-start.3 = (bf16[512,384]{1,0:T(8,128)(2,1)}, bf16[512,384]{1,0:T(8,128)(2,1)S(1)}, u32[]{:S(2)}, u32[]{:S(2)}) collective-permute-start(bf16[512,384]{1,0:T(8,128)(2,1)} %constant_dynamic-update-slice_fusion), channel_id=1, source_target_pairs={{384,0},{0,384},{385,1},{1,385},{386,2},{2,386},{387,3},{3,387},{3... | collective-permute-start | bytes 1179656 | tf_op jit(solution)/shard_map/ppermute | solution.py:253
  10.5 18.3 %collective-permute-start = (bf16[512,384]{1,0:T(8,128)(2,1)}, bf16[512,384]{1,0:T(8,128)(2,1)S(1)}, u32[]{:S(2)}, u32[]{:S(2)}) collective-permute-start(bf16[512,384]{1,0:T(8,128)(2,1)} %constant_dynamic-update-slice_fusion), channel_id=1, source_target_pairs={{384,256},{256,384},{385,257},{257,385},{386,258},{258,386},{387,2... | collective-permute-start | bytes 1179656 | tf_op jit(solution)/shard_map/ppermute | solution.py:256
  15.8 13.0 %collective-permute-start.2 = (bf16[512,384]{1,0:T(8,128)(2,1)S(1)}, bf16[512,384]{1,0:T(8,128)(2,1)S(1)}, u32[]{:S(2)}, u32[]{:S(2)}) collective-permute-start(bf16[512,384]{1,0:T(8,128)(2,1)S(1)} %constant_dynamic-update-slice_fusion.2), channel_id=1, source_target_pairs={{0,4},{4,8},{8,12},{12,16},{16,20},{20,24},{24,28},{28,32},{32,36}... | collective-permute-start | bytes 1179656 | tf_op jit(solution)/shard_map/ppermute | solution.py:255
  18.7 0.7 copy-start.8
  20.1 16.1 %copy-start.6 = (bf16[256,384]{1,0:T(8,128)(2,1)S(1)}, bf16[256,384]{1,0:T(8,128)(2,1)}, u32[]{:S(2)}) copy-start(bf16[256,384]{1,0:T(8,128)(2,1)} %do_ref.3) | copy-start | bytes 589828
  29.1 7.1 %copy-start.5 = (f32[2,4,384]{2,1,0:T(4,128)S(1)}, f32[2,4,384]{2,1,0:T(4,128)}, u32[]{:S(2)}) copy-start(f32[2,4,384]{2,1,0:T(4,128)} %gains.7) | copy-start | bytes 36868
  40.3 15.6 %collective-permute-start.5 = (bf16[512,384]{1,0:T(8,128)(2,1)S(1)}, bf16[512,384]{1,0:T(8,128)(2,1)S(1)}, u32[]{:S(2)}, u32[]{:S(2)}) collective-permute-start(bf16[512,384]{1,0:T(8,128)(2,1)S(1)} %get-tuple-element.40), channel_id=1, source_target_pairs={{0,4},{4,8},{8,12},{12,16},{16,20},{20,24},{24,28},{28,32},{32,36}... | collective-permute-start | bytes 1179656 | tf_op jit(solution)/shard_map/ppermute | solution.py:268
  50.1 13.7 %collective-permute-start.6 = (bf16[512,384]{1,0:T(8,128)(2,1)S(1)}, bf16[512,384]{1,0:T(8,128)(2,1)S(1)}, u32[]{:S(2)}, u32[]{:S(2)}) collective-permute-start(bf16[512,384]{1,0:T(8,128)(2,1)S(1)} %get-tuple-element.42), channel_id=1, source_target_pairs={{384,128},{128,384},{385,129},{129,385},{386,130},{130,386},{387,1... | collective-permute-start | bytes 1179656 | tf_op jit(solution)/shard_map/ppermute | solution.py:272
  52.0 20.9 %collective-permute-start.7 = (bf16[512,384]{1,0:T(8,128)(2,1)S(1)}, bf16[512,384]{1,0:T(8,128)(2,1)S(1)}, u32[]{:S(2)}, u32[]{:S(2)}) collective-permute-start(bf16[512,384]{1,0:T(8,128)(2,1)S(1)} %get-tuple-element.43), channel_id=1, source_target_pairs={{384,0},{0,384},{385,1},{1,385},{386,2},{2,386},{387,3},{3,387},{3... | collective-permute-start | bytes 1179656 | tf_op jit(solution)/shard_map/ppermute | solution.py:272
  54.0 19.0 %collective-permute-start.8 = (bf16[512,384]{1,0:T(8,128)(2,1)S(1)}, bf16[512,384]{1,0:T(8,128)(2,1)S(1)}, u32[]{:S(2)}, u32[]{:S(2)}) collective-permute-start(bf16[512,384]{1,0:T(8,128)(2,1)S(1)} %get-tuple-element.44), channel_id=1, source_target_pairs={{384,256},{256,384},{385,257},{257,385},{386,258},{258,386},{387,2... | collective-permute-start | bytes 1179656 | tf_op jit(solution)/shard_map/ppermute | solution.py:272
  55.9 17.1 %collective-permute-start.9 = (bf16[512,384]{1,0:T(8,128)(2,1)S(1)}, bf16[512,384]{1,0:T(8,128)(2,1)S(1)}, u32[]{:S(2)}, u32[]{:S(2)}) collective-permute-start(bf16[512,384]{1,0:T(8,128)(2,1)S(1)} %get-tuple-element.45), channel_id=1, source_target_pairs={{4,0},{8,4},{12,8},{16,12},{20,16},{24,20},{28,24},{32,28},{36,32}... | collective-permute-start | bytes 1179656 | tf_op jit(solution)/shard_map/ppermute | solution.py:273

commit v3 on v2

v3 whole, which is shorter than its diff:
```python
import functools

import jax
import jax.numpy as jnp
from jax import lax
from jax.experimental import pallas as pl
from jax.experimental.pallas import tpu as pltpu
from jax.sharding import Mesh, PartitionSpec as P

DH = 128
BLK = 64
WIDTH = 1536
NSUB = 4
HEADS = 3
TOK = 256
COLS = 384
COLUMNS = [slice(h * DH, (h + 1) * DH) for h in range(HEADS)]
EPSILON = 1e-06
SCALE = DH ** (-0.5)
MASKED = -1e30
LOG2E = 1.4426950408889634
F32 = jnp.float32
BF16 = jnp.bfloat16
VMEM = pltpu.VMEM
VSPEC = pl.BlockSpec(memory_space=pltpu.VMEM)
SSPEC = pl.BlockSpec(memory_space=pltpu.SMEM)


def dot(a, b, ca, cb):
    return lax.dot_general(a, b, (((ca,), (cb,)), ((), ())), preferred_element_type=F32)


def row_sums(product):
    folded = product[:, 0:128] + product[:, 128:256] + product[:, 256:384]
    return jnp.sum(jnp.transpose(folded), axis=0, keepdims=True)


def squares_kernel(*refs):
    ins, out = refs[:4], refs[-1]
    out[...] = jnp.zeros(out.shape, F32)
    for i, ref in enumerate(ins):
        wide = ref[0:TOK, :].astype(F32)
        out[i : i + 1, :] = row_sums(wide * wide)


def more_squares_kernel(own, *refs):
    ins, out = refs[:-1], refs[-1]
    out[0:8, :] = own[...]
    out[8:16, :] = jnp.zeros((8, TOK), F32)
    for i, ref in enumerate(ins):
        wide = ref[0:TOK, :].astype(F32)
        row = (8, 4, 6, 7, 5)[i]
        out[row : row + 1, :] = row_sums(wide * wide)


def attend(qs, kns, vs, dos, valid, masks, key_side=3):
    heads, blocks = range(len(qs)), range(len(kns[0]))
    scores = [[dot(kns[h][j], qs[h], 1, 1) for j in blocks] for h in heads]
    if masks is not None:
        scores = [[jnp.where(masks[j], scores[h][j], MASKED) for j in blocks] for h in heads]
    dprobs = [[dot(vs[h][j], dos[h], 1, 1) for j in blocks] for h in heads]
    tops = []
    for h in heads:
        peaks = [jnp.max(scores[h][j], axis=0, keepdims=True) for j in blocks]
        if valid is not None:
            peaks = [peaks[0]] + [jnp.where(ok, peak, MASKED) for ok, peak in zip(valid[1:], peaks[1:])]
        tops.append(functools.reduce(jnp.maximum, peaks))
    if valid is None:
        lifts = [[tops[h]] * len(blocks) for h in heads]
    else:
        lifts = [[tops[h]] + [jnp.where(ok, tops[h], -MASKED) for ok in valid[1:]] for h in heads]
    shifted = [[jnp.exp2((scores[h][j] - lifts[h][j]) * (SCALE * LOG2E)) for j in blocks] for h in heads]
    inverse = [1.0 / sum(jnp.sum(e, axis=0, keepdims=True) for e in shifted[h]) for h in heads]
    probs = [[e * inverse[h] for e in shifted[h]] for h in heads]
    weights = [[p.astype(BF16) for p in probs[h]] for h in heads]
    delta = [sum(jnp.sum(p * d, axis=0, keepdims=True) for p, d in zip(probs[h], dprobs[h])) for h in heads]
    dscores = [
        [(p * (d - delta[h]) * SCALE).astype(BF16) for p, d in zip(probs[h], dprobs[h])] for h in heads
    ]
    results = []
    for h in heads:
        out = sum(dot(w, v, 0, 0) for w, v in zip(weights[h], vs[h]))
        dq = sum(dot(ds, kn, 0, 0) for ds, kn in zip(dscores[h], kns[h]))
        dks = [dot(ds, qs[h], 1, 0) for ds in dscores[h][:key_side]]
        dvs = [dot(w, dos[h], 1, 0) for w in weights[h][:key_side]]
        results.append((out, dq, dks, dvs, (tops[h], inverse[h], delta[h])))
    return results


def over_heads(ref):
    return ref[0] + ref[1] + ref[2] + ref[3]


def inverse_rms(sums_ref):
    return jnp.transpose(lax.rsqrt(over_heads(sums_ref) * (1.0 / WIDTH) + EPSILON))


def normed(raw, inv, gain):
    return (raw.astype(F32) * inv * gain).astype(BF16)


def self_kernel(
    scal, sums, gains, q_ref, k_ref, v_ref, do_ref, x_ref, d_ref,
    out_ref, dq_ref, dk_ref, dv_ref, px_ref, stats,
):
    group, slot = scal[0], scal[1]
    tower = (group == 3).astype(jnp.int32)
    inv = inverse_rms(sums)
    qs, kns, vs, dos = [], [], [], []
    for c in COLUMNS:
        gk = gains[tower, 1:2, c]
        qs.append(normed(q_ref[:, c], inv[:, 0:1], gains[tower, 0:1, c]))
        kns.append(
            [
                normed(k_ref[:, c], inv[:, 1:2], gk),
                normed(x_ref[0:TOK, c], inv[:, 5:6], gk),
                normed(d_ref[0:TOK, c], inv[:, 4:5], gk),
            ]
        )
        vs.append([v_ref[:, c], x_ref[TOK:, c], d_ref[TOK:, c]])
        dos.append(do_ref[:, c])
    has_d = (slot > 0) & (slot < 31)
    results = attend(qs, kns, vs, dos, [True, True, has_d], None, key_side=2)
    stats[...] = jnp.zeros(stats.shape, F32)
    stats[9:10, :] = lax.rsqrt(over_heads(sums)[0:1, :] * (1.0 / WIDTH) + EPSILON)
    for h, (c, (out, dq, dks, dvs, rows)) in enumerate(zip(COLUMNS, results)):
        out_ref[:, c] = out
        dq_ref[:, c] = dq
        dk_ref[:, c] = dks[0]
        dv_ref[:, c] = dvs[0]
        px_ref[0:TOK, c] = dks[1].astype(BF16)
        px_ref[TOK:, c] = dvs[1].astype(BF16)
        for i, row in enumerate(rows):
            stats[3 * i + h : 3 * i + h + 1, :] = row


def key_side(tower, inv_k, gains, k_ref, v_ref, qdo_ref, stats):
    inv_q = jnp.transpose(stats[...])[:, 9:10]
    kns = [normed(k_ref[:, c], inv_k, gains[tower, 1:2, c]) for c in COLUMNS]
    qs = [normed(qdo_ref[0:TOK, c], inv_q, gains[tower, 0:1, c]) for c in COLUMNS]
    dos = [qdo_ref[TOK:, c] for c in COLUMNS]
    scores = [dot(kn, q, 1, 1) for kn, q in zip(kns, qs)]
    dprobs = [dot(v_ref[:, c], do, 1, 1) for c, do in zip(COLUMNS, dos)]
    dks, dvs = [], []
    for h in range(HEADS):
        top, inverse, delta = (stats[3 * i + h : 3 * i + h + 1, :] for i in range(3))
        p = jnp.exp2((scores[h] - top) * (SCALE * LOG2E)) * inverse
        ds = (p * (dprobs[h] - delta) * SCALE).astype(BF16)
        dks.append(dot(ds, qs[h], 1, 0))
        dvs.append(dot(p.astype(BF16), dos[h], 1, 0))
    return jnp.concatenate(dks, axis=1), jnp.concatenate(dvs, axis=1)


def cross_kernel(
    scal, sums, gains, q_ref, do_ref, i0, i1, i2,
    out_ref, dq_ref, p0, p1, p2,
):
    group = scal[0]
    audio = group == 3
    inv = inverse_rms(sums)
    sub_row = lax.broadcasted_iota(jnp.int32, (1, TOK), 1) // BLK
    sub_col = lax.broadcasted_iota(jnp.int32, (TOK, 1), 0) // BLK

    def spread(base, offset, sub):
        value = jnp.zeros(sub.shape, jnp.int32)
        for b in range(NSUB):
            value = jnp.where(sub == b, scal[base + 2 * b + offset], value)
        return value

    @pl.when(audio)
    def _():
        masks = []
        for j in range(3):
            lower = spread(2 + 8 * j, 0, sub_col)
            upper = spread(2 + 8 * j, 1, sub_col)
            masks.append((sub_row >= lower) & (sub_row < upper))
        qs = [normed(q_ref[:, c], inv[:, 2:3], gains[1, 2:3, c]) for c in COLUMNS]
        dos = [do_ref[:, c] for c in COLUMNS]
        kns = [
            [normed(r[0:TOK, c], inv[:, 6 + j : 7 + j], gains[0, 3:4, c]) for j, r in enumerate((i0, i1, i2))]
            for c in COLUMNS
        ]
        vs = [[r[TOK:, c] for r in (i0, i1, i2)] for c in COLUMNS]
        for c, (out, dq, dks, dvs, _) in zip(COLUMNS, attend(qs, kns, vs, dos, None, masks)):
            out_ref[:, c] = out
            dq_ref[:, c] = dq
            for ref, dk, dv in zip((p0, p1, p2), dks, dvs):
                ref[0:TOK, c] = dk.astype(BF16)
                ref[TOK:, c] = dv.astype(BF16)

    @pl.when(jnp.logical_not(audio))
    def _():
        base = 2 + 8 * group
        lower = spread(base, 0, sub_row)
        upper = spread(base, 1, sub_row)
        mask = (sub_col >= lower) & (sub_col < upper)
        first, second = group == 0, group == 1

        def pick(a, b, c):
            return jnp.where(first, a, jnp.where(second, b, c))

        inv_k = pick(inv[:, 6:7], inv[:, 7:8], inv[:, 8:9])
        qs = [normed(q_ref[:, c], inv[:, 2:3], gains[0, 2:3, c]) for c in COLUMNS]
        dos = [do_ref[:, c] for c in COLUMNS]
        kns = [
            [normed(pick(i0[0:TOK, c], i1[0:TOK, c], i2[0:TOK, c]), inv_k, gains[1, 3:4, c])] for c in COLUMNS
        ]
        vs = [[pick(i0[TOK:, c], i1[TOK:, c], i2[TOK:, c])] for c in COLUMNS]
        for c, (out, dq, dks, dvs, _) in zip(COLUMNS, attend(qs, kns, vs, dos, None, [mask])):
            out_ref[:, c] = out
            dq_ref[:, c] = dq
            dk = dks[0].astype(BF16)
            dv = dvs[0].astype(BF16)
            for ref in (p0, p1, p2):
                ref[0:TOK, c] = dk
                ref[TOK:, c] = dv


def gather_kernel(
    scal, sums, gains, sq, sk, sv, cq, ck, sdq, cdq, sdk, sdv, qdo, r1, r0, r2, stats, rx,
    svg, cvg, dks_ref, dkc_ref, inner,
):
    tower = (scal[0] == 3).astype(jnp.int32)
    dkc = r0[0:TOK, :].astype(F32) + r1[0:TOK, :].astype(F32) + r2[0:TOK, :].astype(F32)
    cvg[...] = (r0[TOK:, :].astype(F32) + r1[TOK:, :].astype(F32) + r2[TOK:, :].astype(F32)).astype(BF16)
    dk_d, dv_d = key_side(tower, inverse_rms(sums)[:, 1:2], gains, sk, sv, qdo, stats)
    dks = sdk[...] + dk_d + rx[0:TOK, :].astype(F32)
    svg[...] = (sdv[...] + dv_d + rx[TOK:, :].astype(F32)).astype(BF16)
    dks_ref[...] = dks
    dkc_ref[...] = dkc
    inner[...] = jnp.zeros(inner.shape, F32)
    for i, (x, y) in enumerate(((sq, sdq[...]), (sk, dks), (cq, cdq[...]), (ck, dkc))):
        inner[i : i + 1, :] = row_sums(gains[tower, i : i + 1, :] * y * x[...].astype(F32))


def final_kernel(scal, gains, sums, inner, sq, sk, cq, ck, y0, y1, y2, y3, o0, o1, o2, o3):
    tower = (scal[0] == 3).astype(jnp.int32)
    inv = inverse_rms(sums)
    mean = jnp.transpose(over_heads(inner)) * (1.0 / WIDTH)
    for i, (x, y, o) in enumerate(zip((sq, sk, cq, ck), (y0, y1, y2, y3), (o0, o1, o2, o3))):
        r = inv[:, i : i + 1]
        o[...] = (
            r * gains[tower, i : i + 1, :] * y[...] - x[...].astype(F32) * (r * r * r * mean[:, i : i + 1])
        ).astype(BF16)


def shape(rows, dtype, cols=COLS):
    return jax.ShapeDtypeStruct((rows, cols), dtype)


def call(kernel, name, scalars, outs, *args, flops=0):
    nbytes = sum(a.size * a.dtype.itemsize for a in args) + sum(o.size * o.dtype.itemsize for o in outs)
    return pl.pallas_call(
        kernel,
        name=name,
        out_shape=outs,
        in_specs=[SSPEC] * scalars + [VSPEC] * (len(args) - scalars),
        out_specs=[VSPEC] * len(outs),
        compiler_params=pltpu.CompilerParams(vmem_limit_bytes=40 * 1024 * 1024),
        cost_estimate=pl.CostEstimate(flops=flops, bytes_accessed=nbytes, transcendentals=0),
    )(*args)


def on_device(sq, sk, sv, cq, ck, cv, do, gains, span):
    group = lax.axis_index("y")
    slot = lax.axis_index("t")
    slots = lax.axis_size("t")
    x_pairs = [(i, i ^ 1) for i in range(slots)]
    d_pairs = [(i, i + 1) if i % 2 else (i, i - 1) for i in range(1, slots - 1)]
    pairs = [[(3, j), (j, 3)] for j in range(3)]
    spans = lax.dynamic_slice_in_dim(span.reshape(3, NSUB * slots, 2), slot * NSUB, NSUB, 1)
    scal = jnp.concatenate([jnp.stack([group, slot]).astype(jnp.int32), spans.reshape(-1)])

    s_kv, c_kv = jnp.concatenate([sk, sv]), jnp.concatenate([ck, cv])
    scal, sq = lax.optimization_barrier((scal, sq))
    own = call(squares_kernel, "squares", 0, [shape(8, F32, TOK)], sq, sk, cq, ck, do, sv, gains)[0]
    c_in = [None] * 3
    s_x = lax.ppermute(s_kv, "t", x_pairs)
    c_in[1] = lax.ppermute(c_kv, "y", pairs[1])
    c_in[0] = lax.ppermute(c_kv, "y", pairs[0])
    s_later, s_x = lax.optimization_barrier((s_kv, s_x))
    s_d = lax.ppermute(s_later, "t", d_pairs)
    c_in[2] = lax.ppermute(c_kv, "y", pairs[2])
    qdo, own = lax.optimization_barrier((jnp.concatenate([sq, do]), own))
    sums = call(
        more_squares_kernel, "more", 0, [shape(16, F32, TOK)], own, c_in[2], s_d, c_in[0], c_in[1], s_x
    )[0]
    sums = lax.all_gather(sums, "head")

    qdo, sums = lax.optimization_barrier((qdo, sums))
    d_qdo = lax.ppermute(qdo, "t", d_pairs)
    c_out, c_dq, *c_parts = call(
        cross_kernel, "cross", 1, [shape(TOK, F32)] * 2 + [shape(2 * TOK, BF16)] * 3,
        scal, sums, gains, cq, do, *c_in, flops=12 * HEADS * TOK * 3 * TOK * DH,
    )
    c_back = [None] * 3
    for j in (1, 0, 2):
        c_back[j] = lax.ppermute(c_parts[j], "y", pairs[j])
    sq_later, d_qdo, c_out = lax.optimization_barrier((sq, d_qdo, c_out))
    s_out, s_dq, s_dk, s_dv, part_x, stats = call(
        self_kernel, "selfatt", 1, [shape(TOK, F32)] * 4 + [shape(2 * TOK, BF16), shape(16, F32, TOK)],
        scal, sums, gains, sq_later, sk, sv, do, s_x, s_d, flops=12 * HEADS * TOK * 3 * TOK * DH,
    )
    d_stats = lax.ppermute(stats, "t", d_pairs)
    back_x = lax.ppermute(part_x, "t", x_pairs)
    att = (s_out + c_out).astype(BF16)
    svg, cvg, dks, dkc, inner = call(
        gather_kernel, "gather", 1, [shape(TOK, BF16)] * 2 + [shape(TOK, F32)] * 2 + [shape(8, F32, TOK)],
        scal, sums, gains, sq, sk, sv, cq, ck, s_dq, c_dq, s_dk, s_dv, d_qdo, c_back[1], c_back[0], c_back[2], d_stats, back_x,
        flops=8 * HEADS * TOK * TOK * DH,
    )
    inner = lax.all_gather(inner, "head")
    g0, g1, g2, g3 = call(
        final_kernel, "final", 1, [shape(TOK, BF16)] * 4, scal, gains, sums, inner, sq, sk, cq, ck, s_dq, dks, c_dq, dkc
    )
    return att, g0, g1, svg, g2, g3, cvg


def solution(mesh):
    seq = mesh.shape["seq"]
    grid = Mesh(mesh.devices.reshape(4, seq // 4, mesh.shape["head"]), ("y", "t", "head"))
    block = P(("y", "t"), "head")
    return jax.shard_map(
        on_device,
        mesh=grid,
        in_specs=(block,) * 7 + (P(None, None, "head"), P()),
        out_specs=(block,) * 7,
        check_vma=False,
    )
```

time: 84 us -> 81 us (0.964)
  the two profiles are of different devices: /device:TPU:127 before, /device:TPU:227 now
where the time goes in v3:
time: 81 us; the launch traced here: 80.5 us
  starting transfers between devices  36 us (44%)
  blocking collectives  16.2 us (20%)
  Pallas kernels  10.2 us (13%)
  waiting for transfers between devices  9.24 us (11%)
  local copies, waits for them, and re-layouts  7.16 us (9%)
  between operations  0.86 us (1%)
  other arithmetic  0.83 us (1%)
    pallas_call x6, Pallas kernels, call(): pl.pallas_call(kernel, name=name, out_shape=outs, in_specs=[SSPEC] * scal...  10.2 us
    ppermute x3, starting transfers between devices, on_device(): c_back[j] = lax.ppermute(c_parts[j], 'y', pairs[j])  8.74 us
    all_gather x1, blocking collectives, on_device(): inner = lax.all_gather(inner, 'head')  8.12 us
    all_gather x1, blocking collectives, on_device(): sums = lax.all_gather(sums, 'head')  8.04 us
    ppermute x1, starting transfers between devices, on_device(): c_in[0] = lax.ppermute(c_kv, 'y', pairs[0])  6.82 us
    ppermute x1, starting transfers between devices, on_device(): s_d = lax.ppermute(s_later, 't', d_pairs)  5.63 us
    ppermute x1, starting transfers between devices, on_device(): d_qdo = lax.ppermute(qdo, 't', d_pairs)  5.46 us
    ppermute x3, waiting for transfers between devices, on_device(): c_back[j] = lax.ppermute(c_parts[j], 'y', pairs[j])  5.05 us
  transfers between devices with their start and end apart: 11, of which 4 were waited for; matrix products, arithmetic and copies ran while one was open for 7% of the time, Pallas kernels for 7%

profile of v3, /device:TPU:227, one launch (start us, length us, event | category | flops | bytes accessed | tf_op | source)
XLA Modules:
  0.0 80.5 jit_solution(10423149108898516356)
XLA Ops:
  0.6 1.0 %constant_dynamic-update-slice_fusion.3 = bf16[512,384]{1,0:T(8,128)(2,1)S(1)} fusion(bf16[256,384]{1,0:T(8,128)(2,1)} %sk.3), kind=kLoop, calls=%fused_computation.5 | loop fusion | bytes 393216
  1.7 2.3 %collective-permute-start.1 = (bf16[512,384]{1,0:T(8,128)(2,1)S(1)}, bf16[512,384]{1,0:T(8,128)(2,1)S(1)}, u32[]{:S(2)}, u32[]{:S(2)}) collective-permute-start(bf16[512,384]{1,0:T(8,128)(2,1)S(1)} %constant_dynamic-update-slice_fusion.2), channel_id=1, source_target_pairs={{0,4},{4,0},{8,12},{12,8},{16,20},{20,16},{24,28},{28,24},{32,36},... | collective-permute-start | bytes 1179656 | tf_op jit(solution)/shard_map/ppermute | solution.py:278
  4.0 0.7 constant_dynamic-update-slice_fusion.1
  4.8 0.7 constant_dynamic-update-slice_fusion
  5.4 0.7 collective-permute-start.4
  6.1 6.8 %collective-permute-start.3 = (bf16[512,384]{1,0:T(8,128)(2,1)}, bf16[512,384]{1,0:T(8,128)(2,1)S(1)}, u32[]{:S(2)}, u32[]{:S(2)}) collective-permute-start(bf16[512,384]{1,0:T(8,128)(2,1)} %constant_dynamic-update-slice_fusion), channel_id=1, source_target_pairs={{384,0},{0,384},{385,1},{1,385},{386,2},{2,386},{387,3},{3,387},{3... | collective-permute-start | bytes 1179656 | tf_op jit(solution)/shard_map/ppermute | solution.py:280
  13.0 0.7 collective-permute-start
  13.7 5.6 %collective-permute-start.2 = (bf16[512,384]{1,0:T(8,128)(2,1)S(1)}, bf16[512,384]{1,0:T(8,128)(2,1)S(1)}, u32[]{:S(2)}, u32[]{:S(2)}) collective-permute-start(bf16[512,384]{1,0:T(8,128)(2,1)S(1)} %constant_dynamic-update-slice_fusion.2), channel_id=1, source_target_pairs={{4,8},{8,4},{12,16},{16,12},{20,24},{24,20},{28,32},{32,28},{36,40... | collective-permute-start | bytes 1179656 | tf_op jit(solution)/shard_map/ppermute | solution.py:282
  19.4 0.7 copy-done.8
  20.1 0.7 constant_dynamic-slice_fusion
  20.7 1.4 %copy.17 = s32[3,4,2]{2,1,0:T(4,128)} copy(s32[3,4,2]{1,0,2:T(4,128)} %constant_dynamic-slice_fusion) | data formatting | bytes 192 | tf_op jit(solution)/shard_map/dynamic_slice | solution.py:271
  22.1 1.3 %reshape.21 = s32[24]{0:T(128)} reshape(s32[3,4,2]{2,1,0:T(4,128)} %copy.17) | data formatting | bytes 192 | tf_op jit(solution)/shard_map/reshape | solution.py:272
  23.4 0.7 copy-done.9
  24.1 0.1 pad_add_fusion.scal
  24.2 0.2 squares.1.own
  24.5 3.5 %collective-permute-done.3.refs_2_.i0 = bf16[512,384]{1,0:T(8,128)(2,1)S(1)} collective-permute-done((bf16[512,384]{1,0:T(8,128)(2,1)}, bf16[512,384]{1,0:T(8,128)(2,1)S(1)}, u32[]{:S(2)}, u32[]{:S(2)}) %collective-permute-start.3) | collective-permute-done | bytes 393248 | tf_op jit(solution)/shard_map/ppermute | solution.py:280
  27.9 0.3 more.1
  28.2 8.0 %all-gather = f32[64,256]{1,0:T(8,128)S(1)} all-gather(f32[16,256]{1,0:T(8,128)S(1)} %more.1), channel_id=2, replica_groups=mesh['y'=4,'t'=32,'head'=4] {'head'}, dimensions={0}, use_global_device_ids=true | all-gather | bytes 81920 | tf_op jit(solution)/shard_map/all_gather | solution.py:288
  36.3 5.5 %collective-permute-start.5 = (bf16[512,384]{1,0:T(8,128)(2,1)S(1)}, bf16[512,384]{1,0:T(8,128)(2,1)S(1)}, u32[]{:S(2)}, u32[]{:S(2)}) collective-permute-start(bf16[512,384]{1,0:T(8,128)(2,1)S(1)} %pad_maximum_fusion), channel_id=1, source_target_pairs={{4,8},{8,4},{12,16},{16,12},{20,24},{24,20},{28,32},{32,28},{36,40... | collective-permute-start | bytes 1179656 | tf_op jit(solution)/shard_map/ppermute | solution.py:291
  41.7 2.1 %cross.1 = (f32[256,384]{1,0:T(8,128)S(1)}, f32[256,384]{1,0:T(8,128)S(1)}, bf16[512,384]{1,0:T(8,128)(2,1)S(1)}, bf16[512,384]{1,0:T(8,128)(2,1)S(1)}, bf16[512,384]{1,0:T(8,128)(2,1)S(1)}) custom-call(s32[26]{0:T(128)S(1)} %pad_add_fusion.scal, f32[4,16,256]{2,1,0:T(8,128)S(1)} %bitcast.6, f32[2,4,384]{2,1,0:T(4,128)S(1)} %copy-done.6, ...), custom_call_target="tpu_custom_call" | custom-call | flops 905969664 | bytes 3616872 | tf_op jit(solution)/shard_map/cross/pallas_call | solution.py:253
  43.8 0.7 collective-permute-start.6
  44.5 7.4 %collective-permute-start.7 = (bf16[512,384]{1,0:T(8,128)(2,1)S(1)}, bf16[512,384]{1,0:T(8,128)(2,1)S(1)}, u32[]{:S(2)}, u32[]{:S(2)}) collective-permute-start(bf16[512,384]{1,0:T(8,128)(2,1)S(1)} %get-tuple-element.56), channel_id=1, source_target_pairs={{384,0},{0,384},{385,1},{1,385},{386,2},{2,386},{387,3},{3,387},{3... | collective-permute-start | bytes 1179656 | tf_op jit(solution)/shard_map/ppermute | solution.py:298
  51.9 0.7 collective-permute-start.8
  52.6 3.4 %selfatt.1 = (f32[256,384]{1,0:T(8,128)S(1)}, f32[256,384]{1,0:T(8,128)S(1)}, f32[256,384]{1,0:T(8,128)S(1)}, f32[256,384]{1,0:T(8,128)S(1)}, bf16[512,384]{1,0:T(8,128)(2,1)S(1)}, /*index=5*/f32[16,256]{1,0:T(8,128)S(1)}) custom-call(s32[26]{0:T(128)S(1)} %pad_add_fusion.scal, f32[4,16,256]{2,1,0:T(8,128)S(1)} %bitcast.7, f32[2,4,384]{2,1,0:T(4,128)S(1)} %copy-done.6, ...), custom_call_target="tpu_custom_call" | custom-call | flops 905969664 | bytes 3633256 | tf_op jit(solution)/shard_map/selfatt/pallas_call | solution.py:253
  56.0 1.9 %collective-permute-start.10 = (bf16[512,384]{1,0:T(8,128)(2,1)S(1)}, bf16[512,384]{1,0:T(8,128)(2,1)S(1)}, u32[]{:S(2)}, u32[]{:S(2)}) collective-permute-start(bf16[512,384]{1,0:T(8,128)(2,1)S(1)} %get-tuple-element.59), channel_id=1, source_target_pairs={{0,4},{4,0},{8,12},{12,8},{16,20},{20,16},{24,28},{28,24},{32,36},... | collective-permute-start | bytes 1179656 | tf_op jit(solution)/shard_map/ppermute | solution.py:305
  57.9 3.8 %collective-permute-start.9 = (f32[16,256]{1,0:T(8,128)S(1)}, f32[16,256]{1,0:T(8,128)S(1)}, u32[]{:S(2)}, u32[]{:S(2)}) collective-permute-start(f32[16,256]{1,0:T(8,128)S(1)} %get-tuple-element.58), channel_id=1, source_target_pairs={{4,8},{8,4},{12,16},{16,12},{20,24},{24,20},{28,32},{32,28},{36,40... | collective-permute-start | bytes 49160 | tf_op jit(solution)/shard_map/ppermute | solution.py:304
  61.7 0.7 add_convert_fusion
  62.5 5.0 %collective-permute-done.7.r0 = bf16[512,384]{1,0:T(8,128)(2,1)S(1)} collective-permute-done((bf16[512,384]{1,0:T(8,128)(2,1)S(1)}, bf16[512,384]{1,0:T(8,128)(2,1)S(1)}, u32[]{:S(2)}, u32[]{:S(2)}) %collective-permute-start.7) | collective-permute-done | bytes 393248 | tf_op jit(solution)/shard_map/ppermute | solution.py:298
  67.5 0.6 collective-permute-done.10.rx
  68.1 2.5 %gather.1 = (bf16[256,384]{1,0:T(8,128)(2,1)}, bf16[256,384]{1,0:T(8,128)(2,1)}, f32[256,384]{1,0:T(8,128)S(1)}, f32[256,384]{1,0:T(8,128)S(1)}, f32[8,256]{1,0:T(8,128)S(1)}) custom-call(s32[26]{0:T(128)S(1)} %pad_add_fusion.scal, f32[4,16,256]{2,1,0:T(8,128)S(1)} %bitcast.8, f32[2,4,384]{2,1,0:T(4,128)S(1)} %copy-done.6, bf16[256,384]{1,0:T(8,128)(2,1)S(1)} %copy-done.2, ...), custom_call_target="tpu_custom_call" | custom-call | flops 201326592 | bytes 5804136 | tf_op jit(solution)/shard_map/gather/pallas_call | solution.py:253
  70.6 8.1 %all-gather.1 = f32[32,256]{1,0:T(8,128)S(1)} all-gather(f32[8,256]{1,0:T(8,128)S(1)} %get-tuple-element.60), channel_id=3, replica_groups=mesh['y'=4,'t'=32,'head'=4] {'head'}, dimensions={0}, use_global_device_ids=true | all-gather | bytes 40960 | tf_op jit(solution)/shard_map/all_gather | solution.py:312
  78.7 1.8 %final.1 = (bf16[256,384]{1,0:T(8,128)(2,1)}, bf16[256,384]{1,0:T(8,128)(2,1)}, bf16[256,384]{1,0:T(8,128)(2,1)}, bf16[256,384]{1,0:T(8,128)(2,1)}) custom-call(s32[26]{0:T(128)S(1)} %pad_add_fusion.scal, f32[2,4,384]{2,1,0:T(4,128)S(1)} %copy-done.6, f32[4,16,256]{2,1,0:T(8,128)S(1)} %bitcast.9, f32[4,8,256]{2,1,0:T(8,128)S(1)} %bitcast.10, ...), custom_call_target="tpu_custom_call" | custom-call | bytes 3256424 | tf_op jit(solution)/shard_map/final/pallas_call | solution.py:253
  (29 shorter events, 0.2 us)
Async XLA Ops:
  0.6 1.0 %copy-start.3 = (bf16[256,384]{1,0:T(8,128)(2,1)S(1)}, bf16[256,384]{1,0:T(8,128)(2,1)}, u32[]{:S(2)}) copy-start(bf16[256,384]{1,0:T(8,128)(2,1)} %sv.1) | copy-start | bytes 589828
  1.7 2.4 %copy-start.1 = (bf16[256,384]{1,0:T(8,128)(2,1)S(1)}, bf16[256,384]{1,0:T(8,128)(2,1)}, u32[]{:S(2)}) copy-start(bf16[256,384]{1,0:T(8,128)(2,1)} %ck.3) | copy-start | bytes 589828
  1.7 3.1 %copy-start.7 = (bf16[256,384]{1,0:T(8,128)(2,1)S(1)}, bf16[256,384]{1,0:T(8,128)(2,1)}, u32[]{:S(2)}) copy-start(bf16[256,384]{1,0:T(8,128)(2,1)} %param.14) | copy-start | bytes 589828
  1.7 12.0 %collective-permute-start.1 = (bf16[512,384]{1,0:T(8,128)(2,1)S(1)}, bf16[512,384]{1,0:T(8,128)(2,1)S(1)}, u32[]{:S(2)}, u32[]{:S(2)}) collective-permute-start(bf16[512,384]{1,0:T(8,128)(2,1)S(1)} %constant_dynamic-update-slice_fusion.2), channel_id=1, source_target_pairs={{0,4},{4,0},{8,12},{12,8},{16,20},{20,16},{24,28},{28,24},{32,36},... | collective-permute-start | bytes 1179656 | tf_op jit(solution)/shard_map/ppermute | solution.py:278
  4.0 20.1 %copy-start.4 = (bf16[256,384]{1,0:T(8,128)(2,1)S(1)}, bf16[256,384]{1,0:T(8,128)(2,1)}, u32[]{:S(2)}) copy-start(bf16[256,384]{1,0:T(8,128)(2,1)} %cq.3) | copy-start | bytes 589828
  4.0 20.1 %copy-start.5 = (bf16[256,384]{1,0:T(8,128)(2,1)S(1)}, bf16[256,384]{1,0:T(8,128)(2,1)}, u32[]{:S(2)}) copy-start(bf16[256,384]{1,0:T(8,128)(2,1)} %do_ref.3) | copy-start | bytes 589828
  4.7 19.4 %copy-start = (bf16[256,384]{1,0:T(8,128)(2,1)S(1)}, bf16[256,384]{1,0:T(8,128)(2,1)}, u32[]{:S(2)}) copy-start(bf16[256,384]{1,0:T(8,128)(2,1)} %sk.3) | copy-start | bytes 589828
  4.8 19.4 %copy-start.2 = (bf16[256,384]{1,0:T(8,128)(2,1)S(1)}, bf16[256,384]{1,0:T(8,128)(2,1)}, u32[]{:S(2)}) copy-start(bf16[256,384]{1,0:T(8,128)(2,1)} %sq.1) | copy-start | bytes 589828
  5.4 19.0 %collective-permute-start.4 = (bf16[512,384]{1,0:T(8,128)(2,1)}, bf16[512,384]{1,0:T(8,128)(2,1)S(1)}, u32[]{:S(2)}, u32[]{:S(2)}) collective-permute-start(bf16[512,384]{1,0:T(8,128)(2,1)} %constant_dynamic-update-slice_fusion), channel_id=1, source_target_pairs={{384,128},{128,384},{385,129},{129,385},{386,130},{130,386},{387,1... | collective-permute-start | bytes 1179656 | tf_op jit(solution)/shard_map/ppermute | solution.py:279
  6.1 21.8 %collective-permute-start.3 = (bf16[512,384]{1,0:T(8,128)(2,1)}, bf16[512,384]{1,0:T(8,128)(2,1)S(1)}, u32[]{:S(2)}, u32[]{:S(2)}) collective-permute-start(bf16[512,384]{1,0:T(8,128)(2,1)} %constant_dynamic-update-slice_fusion), channel_id=1, source_target_pairs={{384,0},{0,384},{385,1},{1,385},{386,2},{2,386},{387,3},{3,387},{3... | collective-permute-start | bytes 1179656 | tf_op jit(solution)/shard_map/ppermute | solution.py:280
  13.0 15.0 %collective-permute-start = (bf16[512,384]{1,0:T(8,128)(2,1)}, bf16[512,384]{1,0:T(8,128)(2,1)S(1)}, u32[]{:S(2)}, u32[]{:S(2)}) collective-permute-start(bf16[512,384]{1,0:T(8,128)(2,1)} %constant_dynamic-update-slice_fusion), channel_id=1, source_target_pairs={{384,256},{256,384},{385,257},{257,385},{386,258},{258,386},{387,2... | collective-permute-start | bytes 1179656 | tf_op jit(solution)/shard_map/ppermute | solution.py:283
  13.7 14.2 %collective-permute-start.2 = (bf16[512,384]{1,0:T(8,128)(2,1)S(1)}, bf16[512,384]{1,0:T(8,128)(2,1)S(1)}, u32[]{:S(2)}, u32[]{:S(2)}) collective-permute-start(bf16[512,384]{1,0:T(8,128)(2,1)S(1)} %constant_dynamic-update-slice_fusion.2), channel_id=1, source_target_pairs={{4,8},{8,4},{12,16},{16,12},{20,24},{24,20},{28,32},{32,28},{36,40... | collective-permute-start | bytes 1179656 | tf_op jit(solution)/shard_map/ppermute | solution.py:282
  19.4 0.7 copy-start.8
  20.7 3.4 %copy-start.6 = (f32[2,4,384]{2,1,0:T(4,128)S(1)}, f32[2,4,384]{2,1,0:T(4,128)}, u32[]{:S(2)}) copy-start(f32[2,4,384]{2,1,0:T(4,128)} %gains.7) | copy-start | bytes 36868
  23.4 0.7 copy-start.9
  36.3 16.3 %collective-permute-start.5 = (bf16[512,384]{1,0:T(8,128)(2,1)S(1)}, bf16[512,384]{1,0:T(8,128)(2,1)S(1)}, u32[]{:S(2)}, u32[]{:S(2)}) collective-permute-start(bf16[512,384]{1,0:T(8,128)(2,1)S(1)} %pad_maximum_fusion), channel_id=1, source_target_pairs={{4,8},{8,4},{12,16},{16,12},{20,24},{24,20},{28,32},{32,28},{36,40... | collective-permute-start | bytes 1179656 | tf_op jit(solution)/shard_map/ppermute | solution.py:291
  43.8 18.6 %collective-permute-start.6 = (bf16[512,384]{1,0:T(8,128)(2,1)S(1)}, bf16[512,384]{1,0:T(8,128)(2,1)S(1)}, u32[]{:S(2)}, u32[]{:S(2)}) collective-permute-start(bf16[512,384]{1,0:T(8,128)(2,1)S(1)} %get-tuple-element.55), channel_id=1, source_target_pairs={{384,128},{128,384},{385,129},{129,385},{386,130},{130,386},{387,1... | collective-permute-start | bytes 1179656 | tf_op jit(solution)/shard_map/ppermute | solution.py:298
  44.5 23.0 %collective-permute-start.7 = (bf16[512,384]{1,0:T(8,128)(2,1)S(1)}, bf16[512,384]{1,0:T(8,128)(2,1)S(1)}, u32[]{:S(2)}, u32[]{:S(2)}) collective-permute-start(bf16[512,384]{1,0:T(8,128)(2,1)S(1)} %get-tuple-element.56), channel_id=1, source_target_pairs={{384,0},{0,384},{385,1},{1,385},{386,2},{2,386},{387,3},{3,387},{3... | collective-permute-start | bytes 1179656 | tf_op jit(solution)/shard_map/ppermute | solution.py:298
  51.9 15.6 %collective-permute-start.8 = (bf16[512,384]{1,0:T(8,128)(2,1)S(1)}, bf16[512,384]{1,0:T(8,128)(2,1)S(1)}, u32[]{:S(2)}, u32[]{:S(2)}) collective-permute-start(bf16[512,384]{1,0:T(8,128)(2,1)S(1)} %get-tuple-element.57), channel_id=1, source_target_pairs={{384,256},{256,384},{385,257},{257,385},{386,258},{258,386},{387,2... | collective-permute-start | bytes 1179656 | tf_op jit(solution)/shard_map/ppermute | solution.py:298
  56.0 12.2 %collective-permute-start.10 = (bf16[512,384]{1,0:T(8,128)(2,1)S(1)}, bf16[512,384]{1,0:T(8,128)(2,1)S(1)}, u32[]{:S(2)}, u32[]{:S(2)}) collective-permute-start(bf16[512,384]{1,0:T(8,128)(2,1)S(1)} %get-tuple-element.59), channel_id=1, source_target_pairs={{0,4},{4,0},{8,12},{12,8},{16,20},{20,16},{24,28},{28,24},{32,36},... | collective-permute-start | bytes 1179656 | tf_op jit(solution)/shard_map/ppermute | solution.py:305
  57.9 9.6 %collective-permute-start.9 = (f32[16,256]{1,0:T(8,128)S(1)}, f32[16,256]{1,0:T(8,128)S(1)}, u32[]{:S(2)}, u32[]{:S(2)}) collective-permute-start(f32[16,256]{1,0:T(8,128)S(1)} %get-tuple-element.58), channel_id=1, source_target_pairs={{4,8},{8,4},{12,16},{16,12},{20,24},{24,20},{28,32},{32,28},{36,40... | collective-permute-start | bytes 49160 | tf_op jit(solution)/shard_map/ppermute | solution.py:304

commit v4 on v3

--- a/solution.py
+++ b/solution.py
@@ -49,7 +49,7 @@
     out[8:16, :] = jnp.zeros((8, TOK), F32)
     for i, ref in enumerate(ins):
         wide = ref[0:TOK, :].astype(F32)
-        row = (8, 4, 6, 7, 5)[i]
+        row = (8, 4, 7, 6, 5)[i]
         out[row : row + 1, :] = row_sums(wide * wide)
 
 
@@ -134,21 +134,21 @@
             stats[3 * i + h : 3 * i + h + 1, :] = row
 
 
-def key_side(tower, inv_k, gains, k_ref, v_ref, qdo_ref, stats):
+def key_side_kernel(scal, sums, gains, k_ref, v_ref, qdo_ref, stats, dk_in, dv_in, dk_ref, dv_ref):
+    tower = (scal[0] == 3).astype(jnp.int32)
+    inv_k = inverse_rms(sums)[:, 1:2]
     inv_q = jnp.transpose(stats[...])[:, 9:10]
     kns = [normed(k_ref[:, c], inv_k, gains[tower, 1:2, c]) for c in COLUMNS]
     qs = [normed(qdo_ref[0:TOK, c], inv_q, gains[tower, 0:1, c]) for c in COLUMNS]
     dos = [qdo_ref[TOK:, c] for c in COLUMNS]
     scores = [dot(kn, q, 1, 1) for kn, q in zip(kns, qs)]
     dprobs = [dot(v_ref[:, c], do, 1, 1) for c, do in zip(COLUMNS, dos)]
-    dks, dvs = [], []
-    for h in range(HEADS):
+    for h, c in enumerate(COLUMNS):
         top, inverse, delta = (stats[3 * i + h : 3 * i + h + 1, :] for i in range(3))
         p = jnp.exp2((scores[h] - top) * (SCALE * LOG2E)) * inverse
         ds = (p * (dprobs[h] - delta) * SCALE).astype(BF16)
-        dks.append(dot(ds, qs[h], 1, 0))
-        dvs.append(dot(p.astype(BF16), dos[h], 1, 0))
-    return jnp.concatenate(dks, axis=1), jnp.concatenate(dvs, axis=1)
+        dk_ref[:, c] = dk_in[:, c] + dot(ds, qs[h], 1, 0)
+        dv_ref[:, c] = dv_in[:, c] + dot(p.astype(BF16), dos[h], 1, 0)
 
 
 def cross_kernel(
@@ -217,15 +217,14 @@
 
 
 def gather_kernel(
-    scal, sums, gains, sq, sk, sv, cq, ck, sdq, cdq, sdk, sdv, qdo, r1, r0, r2, stats, rx,
+    scal, gains, sq, sk, cq, ck, sdq, cdq, sdk, sdv, r0, r1, r2, rx,
     svg, cvg, dks_ref, dkc_ref, inner,
 ):
     tower = (scal[0] == 3).astype(jnp.int32)
     dkc = r0[0:TOK, :].astype(F32) + r1[0:TOK, :].astype(F32) + r2[0:TOK, :].astype(F32)
     cvg[...] = (r0[TOK:, :].astype(F32) + r1[TOK:, :].astype(F32) + r2[TOK:, :].astype(F32)).astype(BF16)
-    dk_d, dv_d = key_side(tower, inverse_rms(sums)[:, 1:2], gains, sk, sv, qdo, stats)
-    dks = sdk[...] + dk_d + rx[0:TOK, :].astype(F32)
-    svg[...] = (sdv[...] + dv_d + rx[TOK:, :].astype(F32)).astype(BF16)
+    dks = sdk[...] + rx[0:TOK, :].astype(F32)
+    svg[...] = (sdv[...] + rx[TOK:, :].astype(F32)).astype(BF16)
     dks_ref[...] = dks
     dkc_ref[...] = dkc
     inner[...] = jnp.zeros(inner.shape, F32)
@@ -283,7 +282,7 @@
     c_in[2] = lax.ppermute(c_kv, "y", pairs[2])
     qdo, own = lax.optimization_barrier((jnp.concatenate([sq, do]), own))
     sums = call(
-        more_squares_kernel, "more", 0, [shape(16, F32, TOK)], own, c_in[2], s_d, c_in[0], c_in[1], s_x
+        more_squares_kernel, "more", 0, [shape(16, F32, TOK)], own, c_in[2], s_d, c_in[1], c_in[0], s_x
     )[0]
     sums = lax.all_gather(sums, "head")
 
@@ -303,11 +302,14 @@
     )
     d_stats = lax.ppermute(stats, "t", d_pairs)
     back_x = lax.ppermute(part_x, "t", x_pairs)
+    s_dk, s_dv = call(
+        key_side_kernel, "keyside", 1, [shape(TOK, F32)] * 2,
+        scal, sums, gains, sk, sv, d_qdo, d_stats, s_dk, s_dv, flops=8 * HEADS * TOK * TOK * DH,
+    )
     att = (s_out + c_out).astype(BF16)
     svg, cvg, dks, dkc, inner = call(
         gather_kernel, "gather", 1, [shape(TOK, BF16)] * 2 + [shape(TOK, F32)] * 2 + [shape(8, F32, TOK)],
-        scal, sums, gains, sq, sk, sv, cq, ck, s_dq, c_dq, s_dk, s_dv, d_qdo, c_back[1], c_back[0], c_back[2], d_stats, back_x,
-        flops=8 * HEADS * TOK * TOK * DH,
+        scal, gains, sq, sk, cq, ck, s_dq, c_dq, s_dk, s_dv, c_back[0], c_back[1], c_back[2], back_x,
     )
     inner = lax.all_gather(inner, "head")
     g0, g1, g2, g3 = call(

time: 81 us -> 79.4 us (0.980)
  the two profiles are of different devices: /device:TPU:227 before, /device:TPU:119 now
where the time goes in v4:
time: 79.4 us; the launch traced here: 78.9 us
  starting transfers between devices  34.5 us (43%)
  blocking collectives  16.4 us (21%)
  Pallas kernels  10.8 us (14%)
  waiting for transfers between devices  8.25 us (10%)
  local copies, waits for them, and re-layouts  7.15 us (9%)
  between operations  0.88 us (1%)
  other arithmetic  0.83 us (1%)
    pallas_call x7, Pallas kernels, call(): pl.pallas_call(kernel, name=name, out_shape=outs, in_specs=[SSPEC] * scal...  10.8 us
    all_gather x1, blocking collectives, on_device(): sums = lax.all_gather(sums, 'head')  8.36 us
    ppermute x3, starting transfers between devices, on_device(): c_back[j] = lax.ppermute(c_parts[j], 'y', pairs[j])  8.15 us
    all_gather x1, blocking collectives, on_device(): inner = lax.all_gather(inner, 'head')  8.08 us
    ppermute x1, starting transfers between devices, on_device(): d_qdo = lax.ppermute(qdo, 't', d_pairs)  5.38 us
    ppermute x1, starting transfers between devices, on_device(): c_in[2] = lax.ppermute(c_kv, 'y', pairs[2])  5.38 us
    ppermute x1, starting transfers between devices, on_device(): s_d = lax.ppermute(s_later, 't', d_pairs)  5.01 us
    ppermute x1, starting transfers between devices, on_device(): d_stats = lax.ppermute(stats, 't', d_pairs)  4.71 us
  transfers between devices with their start and end apart: 11, of which 4 were waited for; matrix products, arithmetic and copies ran while one was open for 7% of the time, Pallas kernels for 9%

profile of v4, /device:TPU:119, one launch (start us, length us, event | category | flops | bytes accessed | tf_op | source)
XLA Modules:
  0.0 78.9 jit_solution(17936275477642507027)
XLA Ops:
  0.6 1.0 %constant_dynamic-update-slice_fusion.3 = bf16[512,384]{1,0:T(8,128)(2,1)S(1)} fusion(bf16[256,384]{1,0:T(8,128)(2,1)} %sk.3), kind=kLoop, calls=%fused_computation.5 | loop fusion | bytes 393216
  1.7 2.6 %collective-permute-start.1 = (bf16[512,384]{1,0:T(8,128)(2,1)S(1)}, bf16[512,384]{1,0:T(8,128)(2,1)S(1)}, u32[]{:S(2)}, u32[]{:S(2)}) collective-permute-start(bf16[512,384]{1,0:T(8,128)(2,1)S(1)} %constant_dynamic-update-slice_fusion.2), channel_id=1, source_target_pairs={{0,4},{4,0},{8,12},{12,8},{16,20},{20,16},{24,28},{28,24},{32,36},... | collective-permute-start | bytes 1179656 | tf_op jit(solution)/shard_map/ppermute | solution.py:277
  4.3 0.7 constant_dynamic-update-slice_fusion.1
  5.0 0.7 constant_dynamic-update-slice_fusion
  5.7 0.7 collective-permute-start.4
  6.4 0.7 collective-permute-start.3
  7.1 5.4 %collective-permute-start = (bf16[512,384]{1,0:T(8,128)(2,1)}, bf16[512,384]{1,0:T(8,128)(2,1)S(1)}, u32[]{:S(2)}, u32[]{:S(2)}) collective-permute-start(bf16[512,384]{1,0:T(8,128)(2,1)} %constant_dynamic-update-slice_fusion), channel_id=1, source_target_pairs={{384,256},{256,384},{385,257},{257,385},{386,258},{258,386},{387,2... | collective-permute-start | bytes 1179656 | tf_op jit(solution)/shard_map/ppermute | solution.py:282
  12.5 1.2 %collective-permute-done.1.refs_4_.x_ref = bf16[512,384]{1,0:T(8,128)(2,1)S(1)} collective-permute-done((bf16[512,384]{1,0:T(8,128)(2,1)S(1)}, bf16[512,384]{1,0:T(8,128)(2,1)S(1)}, u32[]{:S(2)}, u32[]{:S(2)}) %collective-permute-start.1) | collective-permute-done | bytes 393248 | tf_op jit(solution)/shard_map/ppermute | solution.py:277
  13.7 5.0 %collective-permute-start.2 = (bf16[512,384]{1,0:T(8,128)(2,1)S(1)}, bf16[512,384]{1,0:T(8,128)(2,1)S(1)}, u32[]{:S(2)}, u32[]{:S(2)}) collective-permute-start(bf16[512,384]{1,0:T(8,128)(2,1)S(1)} %constant_dynamic-update-slice_fusion.2), channel_id=1, source_target_pairs={{4,8},{8,4},{12,16},{16,12},{20,24},{24,20},{28,32},{32,28},{36,40... | collective-permute-start | bytes 1179656 | tf_op jit(solution)/shard_map/ppermute | solution.py:281
  18.8 0.7 copy-done.8
  19.4 0.7 constant_dynamic-slice_fusion
  20.1 1.4 %copy.17 = s32[3,4,2]{2,1,0:T(4,128)} copy(s32[3,4,2]{1,0,2:T(4,128)} %constant_dynamic-slice_fusion) | data formatting | bytes 192 | tf_op jit(solution)/shard_map/dynamic_slice | solution.py:270
  21.5 1.3 %reshape.21 = s32[24]{0:T(128)} reshape(s32[3,4,2]{2,1,0:T(4,128)} %copy.17) | data formatting | bytes 192 | tf_op jit(solution)/shard_map/reshape | solution.py:271
  22.8 0.7 copy-done.9
  23.8 3.6 %collective-permute-done.refs_0_.i2 = bf16[512,384]{1,0:T(8,128)(2,1)S(1)} collective-permute-done((bf16[512,384]{1,0:T(8,128)(2,1)}, bf16[512,384]{1,0:T(8,128)(2,1)S(1)}, u32[]{:S(2)}, u32[]{:S(2)}) %collective-permute-start) | collective-permute-done | bytes 393248 | tf_op jit(solution)/shard_map/ppermute | solution.py:282
  27.5 0.3 more.1
  27.7 8.4 %all-gather = f32[64,256]{1,0:T(8,128)S(1)} all-gather(f32[16,256]{1,0:T(8,128)S(1)} %more.1), channel_id=2, replica_groups=mesh['y'=4,'t'=32,'head'=4] {'head'}, dimensions={0}, use_global_device_ids=true | all-gather | bytes 81920 | tf_op jit(solution)/shard_map/all_gather | solution.py:287
  36.1 5.4 %collective-permute-start.5 = (bf16[512,384]{1,0:T(8,128)(2,1)S(1)}, bf16[512,384]{1,0:T(8,128)(2,1)S(1)}, u32[]{:S(2)}, u32[]{:S(2)}) collective-permute-start(bf16[512,384]{1,0:T(8,128)(2,1)S(1)} %pad_maximum_fusion), channel_id=1, source_target_pairs={{4,8},{8,4},{12,16},{16,12},{20,24},{24,20},{28,32},{32,28},{36,40... | collective-permute-start | bytes 1179656 | tf_op jit(solution)/shard_map/ppermute | solution.py:290
  41.5 2.1 %cross.1 = (f32[256,384]{1,0:T(8,128)S(1)}, f32[256,384]{1,0:T(8,128)S(1)}, bf16[512,384]{1,0:T(8,128)(2,1)S(1)}, bf16[512,384]{1,0:T(8,128)(2,1)S(1)}, bf16[512,384]{1,0:T(8,128)(2,1)S(1)}) custom-call(s32[26]{0:T(128)S(1)} %pad_add_fusion.scal, f32[4,16,256]{2,1,0:T(8,128)S(1)} %bitcast.6, f32[2,4,384]{2,1,0:T(4,128)S(1)} %copy-done.6, ...), custom_call_target="tpu_custom_call" | custom-call | flops 905969664 | bytes 3616872 | tf_op jit(solution)/shard_map/cross/pallas_call | solution.py:252
  43.6 0.7 collective-permute-start.7
  44.3 0.7 collective-permute-start.8
  45.0 6.8 %collective-permute-start.9 = (bf16[512,384]{1,0:T(8,128)(2,1)S(1)}, bf16[512,384]{1,0:T(8,128)(2,1)S(1)}, u32[]{:S(2)}, u32[]{:S(2)}) collective-permute-start(bf16[512,384]{1,0:T(8,128)(2,1)S(1)} %get-tuple-element.62), channel_id=1, source_target_pairs={{384,256},{256,384},{385,257},{257,385},{386,258},{258,386},{387,2... | collective-permute-start | bytes 1179656 | tf_op jit(solution)/shard_map/ppermute | solution.py:297
  51.8 3.4 %selfatt.1 = (f32[256,384]{1,0:T(8,128)S(1)}, f32[256,384]{1,0:T(8,128)S(1)}, f32[256,384]{1,0:T(8,128)S(1)}, f32[256,384]{1,0:T(8,128)S(1)}, bf16[512,384]{1,0:T(8,128)(2,1)S(1)}, /*index=5*/f32[16,256]{1,0:T(8,128)S(1)}) custom-call(s32[26]{0:T(128)S(1)} %pad_add_fusion.scal, f32[4,16,256]{2,1,0:T(8,128)S(1)} %bitcast.7, f32[2,4,384]{2,1,0:T(4,128)S(1)} %copy-done.6, ...), custom_call_target="tpu_custom_call" | custom-call | flops 905969664 | bytes 3633256 | tf_op jit(solution)/shard_map/selfatt/pallas_call | solution.py:252
  55.2 1.9 %collective-permute-start.10 = (bf16[512,384]{1,0:T(8,128)(2,1)S(1)}, bf16[512,384]{1,0:T(8,128)(2,1)S(1)}, u32[]{:S(2)}, u32[]{:S(2)}) collective-permute-start(bf16[512,384]{1,0:T(8,128)(2,1)S(1)} %get-tuple-element.63), channel_id=1, source_target_pairs={{0,4},{4,0},{8,12},{12,8},{16,20},{20,16},{24,28},{28,24},{32,36},... | collective-permute-start | bytes 1179656 | tf_op jit(solution)/shard_map/ppermute | solution.py:304
  57.1 4.7 %collective-permute-start.6 = (f32[16,256]{1,0:T(8,128)S(1)}, f32[16,256]{1,0:T(8,128)S(1)}, u32[]{:S(2)}, u32[]{:S(2)}) collective-permute-start(f32[16,256]{1,0:T(8,128)S(1)} %get-tuple-element.55), channel_id=1, source_target_pairs={{4,8},{8,4},{12,16},{16,12},{20,24},{24,20},{28,32},{32,28},{36,40... | collective-permute-start | bytes 49160 | tf_op jit(solution)/shard_map/ppermute | solution.py:303
  61.8 0.7 add_convert_fusion
  62.5 1.3 %collective-permute-done.6.stats = f32[16,256]{1,0:T(8,128)S(1)} collective-permute-done((f32[16,256]{1,0:T(8,128)S(1)}, f32[16,256]{1,0:T(8,128)S(1)}, u32[]{:S(2)}, u32[]{:S(2)}) %collective-permute-start.6) | collective-permute-done | bytes 16416 | tf_op jit(solution)/shard_map/ppermute | solution.py:303
  63.8 1.4 %keyside.1 = (f32[256,384]{1,0:T(8,128)S(1)}, f32[256,384]{1,0:T(8,128)S(1)}) custom-call(s32[26]{0:T(128)S(1)} %pad_add_fusion.scal, f32[4,16,256]{2,1,0:T(8,128)S(1)} %bitcast.8, f32[2,4,384]{2,1,0:T(4,128)S(1)} %copy-done.6, bf16[256,384]{1,0:T(8,128)(2,1)S(1)} %copy-done, bf16[256,384]{1,0:T(8,128)(2,1)S(1)} %copy-done.3, ...), custom_call_target="tpu_custom_call" | custom-call | flops 201326592 | bytes 2453608 | tf_op jit(solution)/shard_map/keyside/pallas_call | solution.py:252
  65.2 2.1 %collective-permute-done.9.r2 = bf16[512,384]{1,0:T(8,128)(2,1)S(1)} collective-permute-done((bf16[512,384]{1,0:T(8,128)(2,1)S(1)}, bf16[512,384]{1,0:T(8,128)(2,1)S(1)}, u32[]{:S(2)}, u32[]{:S(2)}) %collective-permute-start.9) | collective-permute-done | bytes 393248 | tf_op jit(solution)/shard_map/ppermute | solution.py:297
  67.3 1.7 %gather.1 = (bf16[256,384]{1,0:T(8,128)(2,1)}, bf16[256,384]{1,0:T(8,128)(2,1)}, f32[256,384]{1,0:T(8,128)S(1)}, f32[256,384]{1,0:T(8,128)S(1)}, f32[8,256]{1,0:T(8,128)S(1)}) custom-call(s32[26]{0:T(128)S(1)} %pad_add_fusion.scal, f32[2,4,384]{2,1,0:T(4,128)S(1)} %copy-done.6, bf16[256,384]{1,0:T(8,128)(2,1)S(1)} %copy-done.2, ...), custom_call_target="tpu_custom_call" | custom-call | bytes 5132392 | tf_op jit(solution)/shard_map/gather/pallas_call | solution.py:252
  69.0 8.1 %all-gather.1 = f32[32,256]{1,0:T(8,128)S(1)} all-gather(f32[8,256]{1,0:T(8,128)S(1)} %get-tuple-element.64), channel_id=3, replica_groups=mesh['y'=4,'t'=32,'head'=4] {'head'}, dimensions={0}, use_global_device_ids=true | all-gather | bytes 40960 | tf_op jit(solution)/shard_map/all_gather | solution.py:314
  77.1 1.8 %final.1 = (bf16[256,384]{1,0:T(8,128)(2,1)}, bf16[256,384]{1,0:T(8,128)(2,1)}, bf16[256,384]{1,0:T(8,128)(2,1)}, bf16[256,384]{1,0:T(8,128)(2,1)}) custom-call(s32[26]{0:T(128)S(1)} %pad_add_fusion.scal, f32[2,4,384]{2,1,0:T(4,128)S(1)} %copy-done.6, f32[4,16,256]{2,1,0:T(8,128)S(1)} %bitcast.9, f32[4,8,256]{2,1,0:T(8,128)S(1)} %bitcast.10, ...), custom_call_target="tpu_custom_call" | custom-call | bytes 3256424 | tf_op jit(solution)/shard_map/final/pallas_call | solution.py:252
  (30 shorter events, 0.5 us)
Async XLA Ops:
  0.6 1.0 %copy-start.3 = (bf16[256,384]{1,0:T(8,128)(2,1)S(1)}, bf16[256,384]{1,0:T(8,128)(2,1)}, u32[]{:S(2)}) copy-start(bf16[256,384]{1,0:T(8,128)(2,1)} %v_ref.3) | copy-start | bytes 589828
  1.7 2.7 %copy-start.1 = (bf16[256,384]{1,0:T(8,128)(2,1)S(1)}, bf16[256,384]{1,0:T(8,128)(2,1)}, u32[]{:S(2)}) copy-start(bf16[256,384]{1,0:T(8,128)(2,1)} %ck.3) | copy-start | bytes 589828
  1.7 3.4 %copy-start.7 = (bf16[256,384]{1,0:T(8,128)(2,1)S(1)}, bf16[256,384]{1,0:T(8,128)(2,1)}, u32[]{:S(2)}) copy-start(bf16[256,384]{1,0:T(8,128)(2,1)} %param.14) | copy-start | bytes 589828
  1.7 12.0 %collective-permute-start.1 = (bf16[512,384]{1,0:T(8,128)(2,1)S(1)}, bf16[512,384]{1,0:T(8,128)(2,1)S(1)}, u32[]{:S(2)}, u32[]{:S(2)}) collective-permute-start(bf16[512,384]{1,0:T(8,128)(2,1)S(1)} %constant_dynamic-update-slice_fusion.2), channel_id=1, source_target_pairs={{0,4},{4,0},{8,12},{12,8},{16,20},{20,16},{24,28},{28,24},{32,36},... | collective-permute-start | bytes 1179656 | tf_op jit(solution)/shard_map/ppermute | solution.py:277
  4.3 19.2 %copy-start.4 = (bf16[256,384]{1,0:T(8,128)(2,1)S(1)}, bf16[256,384]{1,0:T(8,128)(2,1)}, u32[]{:S(2)}) copy-start(bf16[256,384]{1,0:T(8,128)(2,1)} %cq.3) | copy-start | bytes 589828
  4.3 19.2 %copy-start.5 = (bf16[256,384]{1,0:T(8,128)(2,1)S(1)}, bf16[256,384]{1,0:T(8,128)(2,1)}, u32[]{:S(2)}) copy-start(bf16[256,384]{1,0:T(8,128)(2,1)} %do_ref.3) | copy-start | bytes 589828
  5.0 18.5 %copy-start = (bf16[256,384]{1,0:T(8,128)(2,1)S(1)}, bf16[256,384]{1,0:T(8,128)(2,1)}, u32[]{:S(2)}) copy-start(bf16[256,384]{1,0:T(8,128)(2,1)} %sk.3) | copy-start | bytes 589828
  5.0 18.5 %copy-start.2 = (bf16[256,384]{1,0:T(8,128)(2,1)S(1)}, bf16[256,384]{1,0:T(8,128)(2,1)}, u32[]{:S(2)}) copy-start(bf16[256,384]{1,0:T(8,128)(2,1)} %sq.1) | copy-start | bytes 589828
  5.7 18.1 %collective-permute-start.4 = (bf16[512,384]{1,0:T(8,128)(2,1)}, bf16[512,384]{1,0:T(8,128)(2,1)S(1)}, u32[]{:S(2)}, u32[]{:S(2)}) collective-permute-start(bf16[512,384]{1,0:T(8,128)(2,1)} %constant_dynamic-update-slice_fusion), channel_id=1, source_target_pairs={{384,0},{0,384},{385,1},{1,385},{386,2},{2,386},{387,3},{3,387},{3... | collective-permute-start | bytes 1179656 | tf_op jit(solution)/shard_map/ppermute | solution.py:279
  6.4 17.4 %collective-permute-start.3 = (bf16[512,384]{1,0:T(8,128)(2,1)}, bf16[512,384]{1,0:T(8,128)(2,1)S(1)}, u32[]{:S(2)}, u32[]{:S(2)}) collective-permute-start(bf16[512,384]{1,0:T(8,128)(2,1)} %constant_dynamic-update-slice_fusion), channel_id=1, source_target_pairs={{384,128},{128,384},{385,129},{129,385},{386,130},{130,386},{387,1... | collective-permute-start | bytes 1179656 | tf_op jit(solution)/shard_map/ppermute | solution.py:278
  7.1 20.4 %collective-permute-start = (bf16[512,384]{1,0:T(8,128)(2,1)}, bf16[512,384]{1,0:T(8,128)(2,1)S(1)}, u32[]{:S(2)}, u32[]{:S(2)}) collective-permute-start(bf16[512,384]{1,0:T(8,128)(2,1)} %constant_dynamic-update-slice_fusion), channel_id=1, source_target_pairs={{384,256},{256,384},{385,257},{257,385},{386,258},{258,386},{387,2... | collective-permute-start | bytes 1179656 | tf_op jit(solution)/shard_map/ppermute | solution.py:282
  13.7 13.8 %collective-permute-start.2 = (bf16[512,384]{1,0:T(8,128)(2,1)S(1)}, bf16[512,384]{1,0:T(8,128)(2,1)S(1)}, u32[]{:S(2)}, u32[]{:S(2)}) collective-permute-start(bf16[512,384]{1,0:T(8,128)(2,1)S(1)} %constant_dynamic-update-slice_fusion.2), channel_id=1, source_target_pairs={{4,8},{8,4},{12,16},{16,12},{20,24},{24,20},{28,32},{32,28},{36,40... | collective-permute-start | bytes 1179656 | tf_op jit(solution)/shard_map/ppermute | solution.py:281
  18.7 0.7 copy-start.8
  20.1 3.4 %copy-start.6 = (f32[2,4,384]{2,1,0:T(4,128)S(1)}, f32[2,4,384]{2,1,0:T(4,128)}, u32[]{:S(2)}) copy-start(f32[2,4,384]{2,1,0:T(4,128)} %gains.9) | copy-start | bytes 36868
  22.8 0.7 copy-start.9
  36.1 15.7 %collective-permute-start.5 = (bf16[512,384]{1,0:T(8,128)(2,1)S(1)}, bf16[512,384]{1,0:T(8,128)(2,1)S(1)}, u32[]{:S(2)}, u32[]{:S(2)}) collective-permute-start(bf16[512,384]{1,0:T(8,128)(2,1)S(1)} %pad_maximum_fusion), channel_id=1, source_target_pairs={{4,8},{8,4},{12,16},{16,12},{20,24},{24,20},{28,32},{32,28},{36,40... | collective-permute-start | bytes 1179656 | tf_op jit(solution)/shard_map/ppermute | solution.py:290
  43.6 21.6 %collective-permute-start.7 = (bf16[512,384]{1,0:T(8,128)(2,1)S(1)}, bf16[512,384]{1,0:T(8,128)(2,1)S(1)}, u32[]{:S(2)}, u32[]{:S(2)}) collective-permute-start(bf16[512,384]{1,0:T(8,128)(2,1)S(1)} %get-tuple-element.60), channel_id=1, source_target_pairs={{384,0},{0,384},{385,1},{1,385},{386,2},{2,386},{387,3},{3,387},{3... | collective-permute-start | bytes 1179656 | tf_op jit(solution)/shard_map/ppermute | solution.py:297
  44.3 20.9 %collective-permute-start.8 = (bf16[512,384]{1,0:T(8,128)(2,1)S(1)}, bf16[512,384]{1,0:T(8,128)(2,1)S(1)}, u32[]{:S(2)}, u32[]{:S(2)}) collective-permute-start(bf16[512,384]{1,0:T(8,128)(2,1)S(1)} %get-tuple-element.61), channel_id=1, source_target_pairs={{384,128},{128,384},{385,129},{129,385},{386,130},{130,386},{387,1... | collective-permute-start | bytes 1179656 | tf_op jit(solution)/shard_map/ppermute | solution.py:297
  45.0 22.4 %collective-permute-start.9 = (bf16[512,384]{1,0:T(8,128)(2,1)S(1)}, bf16[512,384]{1,0:T(8,128)(2,1)S(1)}, u32[]{:S(2)}, u32[]{:S(2)}) collective-permute-start(bf16[512,384]{1,0:T(8,128)(2,1)S(1)} %get-tuple-element.62), channel_id=1, source_target_pairs={{384,256},{256,384},{385,257},{257,385},{386,258},{258,386},{387,2... | collective-permute-start | bytes 1179656 | tf_op jit(solution)/shard_map/ppermute | solution.py:297
  55.2 12.2 %collective-permute-start.10 = (bf16[512,384]{1,0:T(8,128)(2,1)S(1)}, bf16[512,384]{1,0:T(8,128)(2,1)S(1)}, u32[]{:S(2)}, u32[]{:S(2)}) collective-permute-start(bf16[512,384]{1,0:T(8,128)(2,1)S(1)} %get-tuple-element.63), channel_id=1, source_target_pairs={{0,4},{4,0},{8,12},{12,8},{16,20},{20,16},{24,28},{28,24},{32,36},... | collective-permute-start | bytes 1179656 | tf_op jit(solution)/shard_map/ppermute | solution.py:304
  57.1 6.7 %collective-permute-start.6 = (f32[16,256]{1,0:T(8,128)S(1)}, f32[16,256]{1,0:T(8,128)S(1)}, u32[]{:S(2)}, u32[]{:S(2)}) collective-permute-start(f32[16,256]{1,0:T(8,128)S(1)} %get-tuple-element.55), channel_id=1, source_target_pairs={{4,8},{8,4},{12,16},{16,12},{20,24},{24,20},{28,32},{32,28},{36,40... | collective-permute-start | bytes 49160 | tf_op jit(solution)/shard_map/ppermute | solution.py:303

commit v5 on v4

--- a/solution.py
+++ b/solution.py
@@ -286,8 +286,6 @@
     )[0]
     sums = lax.all_gather(sums, "head")
 
-    qdo, sums = lax.optimization_barrier((qdo, sums))
-    d_qdo = lax.ppermute(qdo, "t", d_pairs)
     c_out, c_dq, *c_parts = call(
         cross_kernel, "cross", 1, [shape(TOK, F32)] * 2 + [shape(2 * TOK, BF16)] * 3,
         scal, sums, gains, cq, do, *c_in, flops=12 * HEADS * TOK * 3 * TOK * DH,
@@ -295,11 +293,13 @@
     c_back = [None] * 3
     for j in (1, 0, 2):
         c_back[j] = lax.ppermute(c_parts[j], "y", pairs[j])
-    sq_later, d_qdo, c_out = lax.optimization_barrier((sq, d_qdo, c_out))
+    sq_later, qdo, c_out = lax.optimization_barrier((sq, qdo, c_out))
+    d_qdo = lax.ppermute(qdo, "t", d_pairs)
     s_out, s_dq, s_dk, s_dv, part_x, stats = call(
         self_kernel, "selfatt", 1, [shape(TOK, F32)] * 4 + [shape(2 * TOK, BF16), shape(16, F32, TOK)],
         scal, sums, gains, sq_later, sk, sv, do, s_x, s_d, flops=12 * HEADS * TOK * 3 * TOK * DH,
     )
+    stats, d_qdo = lax.optimization_barrier((stats, d_qdo))
     d_stats = lax.ppermute(stats, "t", d_pairs)
     back_x = lax.ppermute(part_x, "t", x_pairs)
     s_dk, s_dv = call(

time: 79.4 us -> 79.4 us (level)
  the two profiles are of different devices: /device:TPU:119 before, /device:TPU:243 now
where the time goes in v5:
time: 79.4 us; the launch traced here: 78.9 us
  starting transfers between devices  33 us (42%)
  blocking collectives  16.7 us (21%)
  waiting for transfers between devices  10.8 us (14%)
  Pallas kernels  10.8 us (14%)
  local copies, waits for them, and re-layouts  5.86 us (7%)
  between operations  0.88 us (1%)
  other arithmetic  0.83 us (1%)
    pallas_call x7, Pallas kernels, call(): pl.pallas_call(kernel, name=name, out_shape=outs, in_specs=[SSPEC] * scal...  10.8 us
    all_gather x1, blocking collectives, on_device(): sums = lax.all_gather(sums, 'head')  8.64 us
    ppermute x3, starting transfers between devices, on_device(): c_back[j] = lax.ppermute(c_parts[j], 'y', pairs[j])  8.16 us
    all_gather x1, blocking collectives, on_device(): inner = lax.all_gather(inner, 'head')  8.03 us
    ppermute x1, starting transfers between devices, on_device(): d_qdo = lax.ppermute(qdo, 't', d_pairs)  5.41 us
    ppermute x1, starting transfers between devices, on_device(): c_in[2] = lax.ppermute(c_kv, 'y', pairs[2])  5.38 us
    ppermute x1, waiting for transfers between devices, on_device(): c_in[2] = lax.ppermute(c_kv, 'y', pairs[2])  4.9 us
    ppermute x1, starting transfers between devices, on_device(): s_d = lax.ppermute(s_later, 't', d_pairs)  4.72 us
  transfers between devices with their start and end apart: 11, of which 4 were waited for; matrix products, arithmetic and copies ran while one was open for 5% of the time, Pallas kernels for 6%

profile of v5, /device:TPU:243, one launch (start us, length us, event | category | flops | bytes accessed | tf_op | source)
XLA Modules:
  0.0 78.9 jit_solution(16908311530701205600)
XLA Ops:
  0.6 1.0 %constant_dynamic-update-slice_fusion.3 = bf16[512,384]{1,0:T(8,128)(2,1)S(1)} fusion(bf16[256,384]{1,0:T(8,128)(2,1)} %sk.3), kind=kLoop, calls=%fused_computation.5 | loop fusion | bytes 393216
  1.7 2.3 %collective-permute-start.1 = (bf16[512,384]{1,0:T(8,128)(2,1)S(1)}, bf16[512,384]{1,0:T(8,128)(2,1)S(1)}, u32[]{:S(2)}, u32[]{:S(2)}) collective-permute-start(bf16[512,384]{1,0:T(8,128)(2,1)S(1)} %constant_dynamic-update-slice_fusion.2), channel_id=1, source_target_pairs={{0,4},{4,0},{8,12},{12,8},{16,20},{20,16},{24,28},{28,24},{32,36},... | collective-permute-start | bytes 1179656 | tf_op jit(solution)/shard_map/ppermute | solution.py:277
  4.0 0.7 constant_dynamic-update-slice_fusion.1
  4.7 0.7 constant_dynamic-update-slice_fusion
  5.4 0.7 collective-permute-start.4
  6.1 0.7 collective-permute-start.3
  6.8 5.4 %collective-permute-start = (bf16[512,384]{1,0:T(8,128)(2,1)}, bf16[512,384]{1,0:T(8,128)(2,1)S(1)}, u32[]{:S(2)}, u32[]{:S(2)}) collective-permute-start(bf16[512,384]{1,0:T(8,128)(2,1)} %constant_dynamic-update-slice_fusion), channel_id=1, source_target_pairs={{384,256},{256,384},{385,257},{257,385},{386,258},{258,386},{387,2... | collective-permute-start | bytes 1179656 | tf_op jit(solution)/shard_map/ppermute | solution.py:282
  12.2 1.5 %collective-permute-done.1.refs_4_.x_ref = bf16[512,384]{1,0:T(8,128)(2,1)S(1)} collective-permute-done((bf16[512,384]{1,0:T(8,128)(2,1)S(1)}, bf16[512,384]{1,0:T(8,128)(2,1)S(1)}, u32[]{:S(2)}, u32[]{:S(2)}) %collective-permute-start.1) | collective-permute-done | bytes 393248 | tf_op jit(solution)/shard_map/ppermute | solution.py:277
  13.7 4.7 %collective-permute-start.2 = (bf16[512,384]{1,0:T(8,128)(2,1)S(1)}, bf16[512,384]{1,0:T(8,128)(2,1)S(1)}, u32[]{:S(2)}, u32[]{:S(2)}) collective-permute-start(bf16[512,384]{1,0:T(8,128)(2,1)S(1)} %constant_dynamic-update-slice_fusion.2), channel_id=1, source_target_pairs={{4,8},{8,4},{12,16},{16,12},{20,24},{24,20},{28,32},{32,28},{36,40... | collective-permute-start | bytes 1179656 | tf_op jit(solution)/shard_map/ppermute | solution.py:281
  18.5 0.7 copy-done.8
  19.2 0.7 copy.17
  19.9 1.3 %reshape.21 = s32[24]{0:T(128)} reshape(s32[3,4,2]{2,1,0:T(4,128)} %copy.17) | data formatting | bytes 192 | tf_op jit(solution)/shard_map/reshape | solution.py:271
  21.2 0.7 copy-done.9
  22.0 0.2 squares.1.own
  22.3 4.9 %collective-permute-done.refs_0_.i2 = bf16[512,384]{1,0:T(8,128)(2,1)S(1)} collective-permute-done((bf16[512,384]{1,0:T(8,128)(2,1)}, bf16[512,384]{1,0:T(8,128)(2,1)S(1)}, u32[]{:S(2)}, u32[]{:S(2)}) %collective-permute-start) | collective-permute-done | bytes 393248 | tf_op jit(solution)/shard_map/ppermute | solution.py:282
  27.2 0.3 more.1
  27.4 8.6 %all-gather = f32[64,256]{1,0:T(8,128)S(1)} all-gather(f32[16,256]{1,0:T(8,128)S(1)} %more.1), channel_id=2, replica_groups=mesh['y'=4,'t'=32,'head'=4] {'head'}, dimensions={0}, use_global_device_ids=true | all-gather | bytes 81920 | tf_op jit(solution)/shard_map/all_gather | solution.py:287
  36.1 2.1 %cross.1 = (f32[256,384]{1,0:T(8,128)S(1)}, f32[256,384]{1,0:T(8,128)S(1)}, bf16[512,384]{1,0:T(8,128)(2,1)S(1)}, bf16[512,384]{1,0:T(8,128)(2,1)S(1)}, bf16[512,384]{1,0:T(8,128)(2,1)S(1)}) custom-call(s32[26]{0:T(128)S(1)} %pad_add_fusion.scal, f32[4,16,256]{2,1,0:T(8,128)S(1)} %bitcast.6, f32[2,4,384]{2,1,0:T(4,128)S(1)} %copy-done.6, ...), custom_call_target="tpu_custom_call" | custom-call | flops 905969664 | bytes 3616872 | tf_op jit(solution)/shard_map/cross/pallas_call | solution.py:252
  38.2 5.4 %collective-permute-start.5 = (bf16[512,384]{1,0:T(8,128)(2,1)S(1)}, bf16[512,384]{1,0:T(8,128)(2,1)S(1)}, u32[]{:S(2)}, u32[]{:S(2)}) collective-permute-start(bf16[512,384]{1,0:T(8,128)(2,1)S(1)} %pad_maximum_fusion), channel_id=1, source_target_pairs={{4,8},{8,4},{12,16},{16,12},{20,24},{24,20},{28,32},{32,28},{36,40... | collective-permute-start | bytes 1179656 | tf_op jit(solution)/shard_map/ppermute | solution.py:297
  43.6 0.7 collective-permute-start.7
  44.3 0.7 collective-permute-start.8
  45.0 6.8 %collective-permute-start.9 = (bf16[512,384]{1,0:T(8,128)(2,1)S(1)}, bf16[512,384]{1,0:T(8,128)(2,1)S(1)}, u32[]{:S(2)}, u32[]{:S(2)}) collective-permute-start(bf16[512,384]{1,0:T(8,128)(2,1)S(1)} %get-tuple-element.62), channel_id=1, source_target_pairs={{384,256},{256,384},{385,257},{257,385},{386,258},{258,386},{387,2... | collective-permute-start | bytes 1179656 | tf_op jit(solution)/shard_map/ppermute | solution.py:295
  51.8 3.3 %selfatt.1 = (f32[256,384]{1,0:T(8,128)S(1)}, f32[256,384]{1,0:T(8,128)S(1)}, f32[256,384]{1,0:T(8,128)S(1)}, f32[256,384]{1,0:T(8,128)S(1)}, bf16[512,384]{1,0:T(8,128)(2,1)S(1)}, /*index=5*/f32[16,256]{1,0:T(8,128)S(1)}) custom-call(s32[26]{0:T(128)S(1)} %pad_add_fusion.scal, f32[4,16,256]{2,1,0:T(8,128)S(1)} %bitcast.7, f32[2,4,384]{2,1,0:T(4,128)S(1)} %copy-done.6, ...), custom_call_target="tpu_custom_call" | custom-call | flops 905969664 | bytes 3633256 | tf_op jit(solution)/shard_map/selfatt/pallas_call | solution.py:252
  55.1 1.9 %collective-permute-start.10 = (bf16[512,384]{1,0:T(8,128)(2,1)S(1)}, bf16[512,384]{1,0:T(8,128)(2,1)S(1)}, u32[]{:S(2)}, u32[]{:S(2)}) collective-permute-start(bf16[512,384]{1,0:T(8,128)(2,1)S(1)} %get-tuple-element.63), channel_id=1, source_target_pairs={{0,4},{4,0},{8,12},{12,8},{16,20},{20,16},{24,28},{28,24},{32,36},... | collective-permute-start | bytes 1179656 | tf_op jit(solution)/shard_map/ppermute | solution.py:304
  57.1 3.8 %collective-permute-start.6 = (f32[16,256]{1,0:T(8,128)S(1)}, f32[16,256]{1,0:T(8,128)S(1)}, u32[]{:S(2)}, u32[]{:S(2)}) collective-permute-start(f32[16,256]{1,0:T(8,128)S(1)} %get-tuple-element.55), channel_id=1, source_target_pairs={{4,8},{8,4},{12,16},{16,12},{20,24},{24,20},{28,32},{32,28},{36,40... | collective-permute-start | bytes 49160 | tf_op jit(solution)/shard_map/ppermute | solution.py:303
  60.9 0.7 add_convert_fusion
  61.6 2.2 %collective-permute-done.6.stats = f32[16,256]{1,0:T(8,128)S(1)} collective-permute-done((f32[16,256]{1,0:T(8,128)S(1)}, f32[16,256]{1,0:T(8,128)S(1)}, u32[]{:S(2)}, u32[]{:S(2)}) %collective-permute-start.6) | collective-permute-done | bytes 16416 | tf_op jit(solution)/shard_map/ppermute | solution.py:303
  63.8 1.4 %keyside.1 = (f32[256,384]{1,0:T(8,128)S(1)}, f32[256,384]{1,0:T(8,128)S(1)}) custom-call(s32[26]{0:T(128)S(1)} %pad_add_fusion.scal, f32[4,16,256]{2,1,0:T(8,128)S(1)} %bitcast.8, f32[2,4,384]{2,1,0:T(4,128)S(1)} %copy-done.6, bf16[256,384]{1,0:T(8,128)(2,1)S(1)} %copy-done, bf16[256,384]{1,0:T(8,128)(2,1)S(1)} %copy-done.3, ...), custom_call_target="tpu_custom_call" | custom-call | flops 201326592 | bytes 2453608 | tf_op jit(solution)/shard_map/keyside/pallas_call | solution.py:252
  65.2 2.2 %collective-permute-done.9.r2 = bf16[512,384]{1,0:T(8,128)(2,1)S(1)} collective-permute-done((bf16[512,384]{1,0:T(8,128)(2,1)S(1)}, bf16[512,384]{1,0:T(8,128)(2,1)S(1)}, u32[]{:S(2)}, u32[]{:S(2)}) %collective-permute-start.9) | collective-permute-done | bytes 393248 | tf_op jit(solution)/shard_map/ppermute | solution.py:295
  67.4 1.7 %gather.1 = (bf16[256,384]{1,0:T(8,128)(2,1)}, bf16[256,384]{1,0:T(8,128)(2,1)}, f32[256,384]{1,0:T(8,128)S(1)}, f32[256,384]{1,0:T(8,128)S(1)}, f32[8,256]{1,0:T(8,128)S(1)}) custom-call(s32[26]{0:T(128)S(1)} %pad_add_fusion.scal, f32[2,4,384]{2,1,0:T(4,128)S(1)} %copy-done.6, bf16[256,384]{1,0:T(8,128)(2,1)S(1)} %copy-done.2, ...), custom_call_target="tpu_custom_call" | custom-call | bytes 5132392 | tf_op jit(solution)/shard_map/gather/pallas_call | solution.py:252
  69.1 8.0 %all-gather.1 = f32[32,256]{1,0:T(8,128)S(1)} all-gather(f32[8,256]{1,0:T(8,128)S(1)} %get-tuple-element.64), channel_id=3, replica_groups=mesh['y'=4,'t'=32,'head'=4] {'head'}, dimensions={0}, use_global_device_ids=true | all-gather | bytes 40960 | tf_op jit(solution)/shard_map/all_gather | solution.py:314
  77.1 1.8 %final.1 = (bf16[256,384]{1,0:T(8,128)(2,1)}, bf16[256,384]{1,0:T(8,128)(2,1)}, bf16[256,384]{1,0:T(8,128)(2,1)}, bf16[256,384]{1,0:T(8,128)(2,1)}) custom-call(s32[26]{0:T(128)S(1)} %pad_add_fusion.scal, f32[2,4,384]{2,1,0:T(4,128)S(1)} %copy-done.6, f32[4,16,256]{2,1,0:T(8,128)S(1)} %bitcast.9, f32[4,8,256]{2,1,0:T(8,128)S(1)} %bitcast.10, ...), custom_call_target="tpu_custom_call" | custom-call | bytes 3256424 | tf_op jit(solution)/shard_map/final/pallas_call | solution.py:252
  (30 shorter events, 0.3 us)
Async XLA Ops:
  0.6 1.0 %copy-start.3 = (bf16[256,384]{1,0:T(8,128)(2,1)S(1)}, bf16[256,384]{1,0:T(8,128)(2,1)}, u32[]{:S(2)}) copy-start(bf16[256,384]{1,0:T(8,128)(2,1)} %v_ref.3) | copy-start | bytes 589828
  1.7 2.4 %copy-start.1 = (bf16[256,384]{1,0:T(8,128)(2,1)S(1)}, bf16[256,384]{1,0:T(8,128)(2,1)}, u32[]{:S(2)}) copy-start(bf16[256,384]{1,0:T(8,128)(2,1)} %ck.3) | copy-start | bytes 589828
  1.7 3.1 %copy-start.7 = (bf16[256,384]{1,0:T(8,128)(2,1)S(1)}, bf16[256,384]{1,0:T(8,128)(2,1)}, u32[]{:S(2)}) copy-start(bf16[256,384]{1,0:T(8,128)(2,1)} %param.14) | copy-start | bytes 589828
  1.7 12.0 %collective-permute-start.1 = (bf16[512,384]{1,0:T(8,128)(2,1)S(1)}, bf16[512,384]{1,0:T(8,128)(2,1)S(1)}, u32[]{:S(2)}, u32[]{:S(2)}) collective-permute-start(bf16[512,384]{1,0:T(8,128)(2,1)S(1)} %constant_dynamic-update-slice_fusion.2), channel_id=1, source_target_pairs={{0,4},{4,0},{8,12},{12,8},{16,20},{20,16},{24,28},{28,24},{32,36},... | collective-permute-start | bytes 1179656 | tf_op jit(solution)/shard_map/ppermute | solution.py:277
  4.0 17.9 %copy-start.4 = (bf16[256,384]{1,0:T(8,128)(2,1)S(1)}, bf16[256,384]{1,0:T(8,128)(2,1)}, u32[]{:S(2)}) copy-start(bf16[256,384]{1,0:T(8,128)(2,1)} %cq.3) | copy-start | bytes 589828
  4.0 17.9 %copy-start.5 = (bf16[256,384]{1,0:T(8,128)(2,1)S(1)}, bf16[256,384]{1,0:T(8,128)(2,1)}, u32[]{:S(2)}) copy-start(bf16[256,384]{1,0:T(8,128)(2,1)} %do_ref.3) | copy-start | bytes 589828
  4.7 17.2 %copy-start = (bf16[256,384]{1,0:T(8,128)(2,1)S(1)}, bf16[256,384]{1,0:T(8,128)(2,1)}, u32[]{:S(2)}) copy-start(bf16[256,384]{1,0:T(8,128)(2,1)} %sk.3) | copy-start | bytes 589828
  4.7 17.2 %copy-start.2 = (bf16[256,384]{1,0:T(8,128)(2,1)S(1)}, bf16[256,384]{1,0:T(8,128)(2,1)}, u32[]{:S(2)}) copy-start(bf16[256,384]{1,0:T(8,128)(2,1)} %sq.1) | copy-start | bytes 589828
  5.4 16.8 %collective-permute-start.4 = (bf16[512,384]{1,0:T(8,128)(2,1)}, bf16[512,384]{1,0:T(8,128)(2,1)S(1)}, u32[]{:S(2)}, u32[]{:S(2)}) collective-permute-start(bf16[512,384]{1,0:T(8,128)(2,1)} %constant_dynamic-update-slice_fusion), channel_id=1, source_target_pairs={{384,0},{0,384},{385,1},{1,385},{386,2},{2,386},{387,3},{3,387},{3... | collective-permute-start | bytes 1179656 | tf_op jit(solution)/shard_map/ppermute | solution.py:279
  6.1 16.1 %collective-permute-start.3 = (bf16[512,384]{1,0:T(8,128)(2,1)}, bf16[512,384]{1,0:T(8,128)(2,1)S(1)}, u32[]{:S(2)}, u32[]{:S(2)}) collective-permute-start(bf16[512,384]{1,0:T(8,128)(2,1)} %constant_dynamic-update-slice_fusion), channel_id=1, source_target_pairs={{384,128},{128,384},{385,129},{129,385},{386,130},{130,386},{387,1... | collective-permute-start | bytes 1179656 | tf_op jit(solution)/shard_map/ppermute | solution.py:278
  6.8 20.4 %collective-permute-start = (bf16[512,384]{1,0:T(8,128)(2,1)}, bf16[512,384]{1,0:T(8,128)(2,1)S(1)}, u32[]{:S(2)}, u32[]{:S(2)}) collective-permute-start(bf16[512,384]{1,0:T(8,128)(2,1)} %constant_dynamic-update-slice_fusion), channel_id=1, source_target_pairs={{384,256},{256,384},{385,257},{257,385},{386,258},{258,386},{387,2... | collective-permute-start | bytes 1179656 | tf_op jit(solution)/shard_map/ppermute | solution.py:282
  13.7 13.5 %collective-permute-start.2 = (bf16[512,384]{1,0:T(8,128)(2,1)S(1)}, bf16[512,384]{1,0:T(8,128)(2,1)S(1)}, u32[]{:S(2)}, u32[]{:S(2)}) collective-permute-start(bf16[512,384]{1,0:T(8,128)(2,1)S(1)} %constant_dynamic-update-slice_fusion.2), channel_id=1, source_target_pairs={{4,8},{8,4},{12,16},{16,12},{20,24},{24,20},{28,32},{32,28},{36,40... | collective-permute-start | bytes 1179656 | tf_op jit(solution)/shard_map/ppermute | solution.py:281
  18.4 0.7 copy-start.8
  19.2 2.7 %copy-start.6 = (f32[2,4,384]{2,1,0:T(4,128)S(1)}, f32[2,4,384]{2,1,0:T(4,128)}, u32[]{:S(2)}) copy-start(f32[2,4,384]{2,1,0:T(4,128)} %gains.9) | copy-start | bytes 36868
  21.2 0.7 copy-start.9
  38.2 18.9 %collective-permute-start.5 = (bf16[512,384]{1,0:T(8,128)(2,1)S(1)}, bf16[512,384]{1,0:T(8,128)(2,1)S(1)}, u32[]{:S(2)}, u32[]{:S(2)}) collective-permute-start(bf16[512,384]{1,0:T(8,128)(2,1)S(1)} %pad_maximum_fusion), channel_id=1, source_target_pairs={{4,8},{8,4},{12,16},{16,12},{20,24},{24,20},{28,32},{32,28},{36,40... | collective-permute-start | bytes 1179656 | tf_op jit(solution)/shard_map/ppermute | solution.py:297
  43.6 21.6 %collective-permute-start.7 = (bf16[512,384]{1,0:T(8,128)(2,1)S(1)}, bf16[512,384]{1,0:T(8,128)(2,1)S(1)}, u32[]{:S(2)}, u32[]{:S(2)}) collective-permute-start(bf16[512,384]{1,0:T(8,128)(2,1)S(1)} %get-tuple-element.60), channel_id=1, source_target_pairs={{384,0},{0,384},{385,1},{1,385},{386,2},{2,386},{387,3},{3,387},{3... | collective-permute-start | bytes 1179656 | tf_op jit(solution)/shard_map/ppermute | solution.py:295
  44.3 20.9 %collective-permute-start.8 = (bf16[512,384]{1,0:T(8,128)(2,1)S(1)}, bf16[512,384]{1,0:T(8,128)(2,1)S(1)}, u32[]{:S(2)}, u32[]{:S(2)}) collective-permute-start(bf16[512,384]{1,0:T(8,128)(2,1)S(1)} %get-tuple-element.61), channel_id=1, source_target_pairs={{384,128},{128,384},{385,129},{129,385},{386,130},{130,386},{387,1... | collective-permute-start | bytes 1179656 | tf_op jit(solution)/shard_map/ppermute | solution.py:295
  45.0 22.4 %collective-permute-start.9 = (bf16[512,384]{1,0:T(8,128)(2,1)S(1)}, bf16[512,384]{1,0:T(8,128)(2,1)S(1)}, u32[]{:S(2)}, u32[]{:S(2)}) collective-permute-start(bf16[512,384]{1,0:T(8,128)(2,1)S(1)} %get-tuple-element.62), channel_id=1, source_target_pairs={{384,256},{256,384},{385,257},{257,385},{386,258},{258,386},{387,2... | collective-permute-start | bytes 1179656 | tf_op jit(solution)/shard_map/ppermute | solution.py:295
  55.1 12.2 %collective-permute-start.10 = (bf16[512,384]{1,0:T(8,128)(2,1)S(1)}, bf16[512,384]{1,0:T(8,128)(2,1)S(1)}, u32[]{:S(2)}, u32[]{:S(2)}) collective-permute-start(bf16[512,384]{1,0:T(8,128)(2,1)S(1)} %get-tuple-element.63), channel_id=1, source_target_pairs={{0,4},{4,0},{8,12},{12,8},{16,20},{20,16},{24,28},{28,24},{32,36},... | collective-permute-start | bytes 1179656 | tf_op jit(solution)/shard_map/ppermute | solution.py:304
  57.1 6.7 %collective-permute-start.6 = (f32[16,256]{1,0:T(8,128)S(1)}, f32[16,256]{1,0:T(8,128)S(1)}, u32[]{:S(2)}, u32[]{:S(2)}) collective-permute-start(f32[16,256]{1,0:T(8,128)S(1)} %get-tuple-element.55), channel_id=1, source_target_pairs={{4,8},{8,4},{12,16},{16,12},{20,24},{24,20},{28,32},{32,28},{36,40... | collective-permute-start | bytes 49160 | tf_op jit(solution)/shard_map/ppermute | solution.py:303

commit v6 on v5

--- a/solution.py
+++ b/solution.py
@@ -217,7 +217,7 @@
 
 
 def gather_kernel(
-    scal, gains, sq, sk, cq, ck, sdq, cdq, sdk, sdv, r0, r1, r2, rx,
+    scal, gains, sq, sk, cq, ck, sdq, cdq, sdk, sdv, r1, r0, r2, rx,
     svg, cvg, dks_ref, dkc_ref, inner,
 ):
     tower = (scal[0] == 3).astype(jnp.int32)
@@ -309,7 +309,7 @@
     att = (s_out + c_out).astype(BF16)
     svg, cvg, dks, dkc, inner = call(
         gather_kernel, "gather", 1, [shape(TOK, BF16)] * 2 + [shape(TOK, F32)] * 2 + [shape(8, F32, TOK)],
-        scal, gains, sq, sk, cq, ck, s_dq, c_dq, s_dk, s_dv, c_back[0], c_back[1], c_back[2], back_x,
+        scal, gains, sq, sk, cq, ck, s_dq, c_dq, s_dk, s_dv, c_back[1], c_back[0], c_back[2], back_x,
     )
     inner = lax.all_gather(inner, "head")
     g0, g1, g2, g3 = call(

time: 79.4 us -> 79.9 us (level)
  the two profiles are of different devices: /device:TPU:243 before, /device:TPU:227 now
where the time goes in v6:
time: 79.9 us; the launch traced here: 79.4 us
  starting transfers between devices  32.8 us (41%)
  blocking collectives  17.1 us (21%)
  waiting for transfers between devices  11.1 us (14%)
  Pallas kernels  10.8 us (14%)
  local copies, waits for them, and re-layouts  5.86 us (7%)
  between operations  0.86 us (1%)
  other arithmetic  0.83 us (1%)
    pallas_call x7, Pallas kernels, call(): pl.pallas_call(kernel, name=name, out_shape=outs, in_specs=[SSPEC] * scal...  10.8 us
    ppermute x3, starting transfers between devices, on_device(): c_back[j] = lax.ppermute(c_parts[j], 'y', pairs[j])  9.34 us
    all_gather x1, blocking collectives, on_device(): sums = lax.all_gather(sums, 'head')  9.05 us
    all_gather x1, blocking collectives, on_device(): inner = lax.all_gather(inner, 'head')  8.09 us
    ppermute x1, starting transfers between devices, on_device(): d_qdo = lax.ppermute(qdo, 't', d_pairs)  4.73 us
    ppermute x1, starting transfers between devices, on_device(): s_d = lax.ppermute(s_later, 't', d_pairs)  4.72 us
    ppermute x1, starting transfers between devices, on_device(): c_in[0] = lax.ppermute(c_kv, 'y', pairs[0])  4.63 us
    ppermute x1, waiting for transfers between devices, on_device(): c_in[0] = lax.ppermute(c_kv, 'y', pairs[0])  4.01 us
  transfers between devices with their start and end apart: 11, of which 6 were waited for; matrix products, arithmetic and copies ran while one was open for 5% of the time, Pallas kernels for 6%

profile of v6, /device:TPU:227, one launch (start us, length us, event | category | flops | bytes accessed | tf_op | source)
XLA Modules:
  0.0 79.4 jit_solution(6009093941504425940)
XLA Ops:
  0.6 1.0 %constant_dynamic-update-slice_fusion.3 = bf16[512,384]{1,0:T(8,128)(2,1)S(1)} fusion(bf16[256,384]{1,0:T(8,128)(2,1)} %sk.3), kind=kLoop, calls=%fused_computation.5 | loop fusion | bytes 393216
  1.7 2.3 %collective-permute-start.1 = (bf16[512,384]{1,0:T(8,128)(2,1)S(1)}, bf16[512,384]{1,0:T(8,128)(2,1)S(1)}, u32[]{:S(2)}, u32[]{:S(2)}) collective-permute-start(bf16[512,384]{1,0:T(8,128)(2,1)S(1)} %constant_dynamic-update-slice_fusion.2), channel_id=1, source_target_pairs={{0,4},{4,0},{8,12},{12,8},{16,20},{20,16},{24,28},{28,24},{32,36},... | collective-permute-start | bytes 1179656 | tf_op jit(solution)/shard_map/ppermute | solution.py:277
  4.0 0.7 constant_dynamic-update-slice_fusion.1
  4.7 0.7 constant_dynamic-update-slice_fusion
  5.4 4.6 %collective-permute-start.4 = (bf16[512,384]{1,0:T(8,128)(2,1)}, bf16[512,384]{1,0:T(8,128)(2,1)S(1)}, u32[]{:S(2)}, u32[]{:S(2)}) collective-permute-start(bf16[512,384]{1,0:T(8,128)(2,1)} %constant_dynamic-update-slice_fusion), channel_id=1, source_target_pairs={{384,0},{0,384},{385,1},{1,385},{386,2},{2,386},{387,3},{3,387},{3... | collective-permute-start | bytes 1179656 | tf_op jit(solution)/shard_map/ppermute | solution.py:279
  10.1 0.7 collective-permute-start.3
  10.8 0.7 collective-permute-start
  11.5 2.3 %collective-permute-done.1.refs_4_.x_ref = bf16[512,384]{1,0:T(8,128)(2,1)S(1)} collective-permute-done((bf16[512,384]{1,0:T(8,128)(2,1)S(1)}, bf16[512,384]{1,0:T(8,128)(2,1)S(1)}, u32[]{:S(2)}, u32[]{:S(2)}) %collective-permute-start.1) | collective-permute-done | bytes 393248 | tf_op jit(solution)/shard_map/ppermute | solution.py:277
  13.7 4.7 %collective-permute-start.2 = (bf16[512,384]{1,0:T(8,128)(2,1)S(1)}, bf16[512,384]{1,0:T(8,128)(2,1)S(1)}, u32[]{:S(2)}, u32[]{:S(2)}) collective-permute-start(bf16[512,384]{1,0:T(8,128)(2,1)S(1)} %constant_dynamic-update-slice_fusion.2), channel_id=1, source_target_pairs={{4,8},{8,4},{12,16},{16,12},{20,24},{24,20},{28,32},{32,28},{36,40... | collective-permute-start | bytes 1179656 | tf_op jit(solution)/shard_map/ppermute | solution.py:281
  18.5 0.7 copy-done.8
  19.2 0.7 copy.17
  19.9 1.3 %reshape.21 = s32[24]{0:T(128)} reshape(s32[3,4,2]{2,1,0:T(4,128)} %copy.17) | data formatting | bytes 192 | tf_op jit(solution)/shard_map/reshape | solution.py:271
  21.2 0.7 copy-done.9
  22.3 4.0 %collective-permute-done.4.refs_3_.i0 = bf16[512,384]{1,0:T(8,128)(2,1)S(1)} collective-permute-done((bf16[512,384]{1,0:T(8,128)(2,1)}, bf16[512,384]{1,0:T(8,128)(2,1)S(1)}, u32[]{:S(2)}, u32[]{:S(2)}) %collective-permute-start.4) | collective-permute-done | bytes 393248 | tf_op jit(solution)/shard_map/ppermute | solution.py:279
  26.3 0.5 collective-permute-done.2.refs_1_.d_ref
  27.0 9.0 %all-gather = f32[64,256]{1,0:T(8,128)S(1)} all-gather(f32[16,256]{1,0:T(8,128)S(1)} %more.1), channel_id=2, replica_groups=mesh['y'=4,'t'=32,'head'=4] {'head'}, dimensions={0}, use_global_device_ids=true | all-gather | bytes 81920 | tf_op jit(solution)/shard_map/all_gather | solution.py:287
  36.1 2.1 %cross.1 = (f32[256,384]{1,0:T(8,128)S(1)}, f32[256,384]{1,0:T(8,128)S(1)}, bf16[512,384]{1,0:T(8,128)(2,1)S(1)}, bf16[512,384]{1,0:T(8,128)(2,1)S(1)}, bf16[512,384]{1,0:T(8,128)(2,1)S(1)}) custom-call(s32[26]{0:T(128)S(1)} %pad_add_fusion.scal, f32[4,16,256]{2,1,0:T(8,128)S(1)} %bitcast.6, f32[2,4,384]{2,1,0:T(4,128)S(1)} %copy-done.6, ...), custom_call_target="tpu_custom_call" | custom-call | flops 905969664 | bytes 3616872 | tf_op jit(solution)/shard_map/cross/pallas_call | solution.py:252
  38.2 4.7 %collective-permute-start.5 = (bf16[512,384]{1,0:T(8,128)(2,1)S(1)}, bf16[512,384]{1,0:T(8,128)(2,1)S(1)}, u32[]{:S(2)}, u32[]{:S(2)}) collective-permute-start(bf16[512,384]{1,0:T(8,128)(2,1)S(1)} %pad_maximum_fusion), channel_id=1, source_target_pairs={{4,8},{8,4},{12,16},{16,12},{20,24},{24,20},{28,32},{32,28},{36,40... | collective-permute-start | bytes 1179656 | tf_op jit(solution)/shard_map/ppermute | solution.py:297
  42.9 0.7 collective-permute-start.7
  43.6 8.0 %collective-permute-start.8 = (bf16[512,384]{1,0:T(8,128)(2,1)S(1)}, bf16[512,384]{1,0:T(8,128)(2,1)S(1)}, u32[]{:S(2)}, u32[]{:S(2)}) collective-permute-start(bf16[512,384]{1,0:T(8,128)(2,1)S(1)} %get-tuple-element.61), channel_id=1, source_target_pairs={{384,0},{0,384},{385,1},{1,385},{386,2},{2,386},{387,3},{3,387},{3... | collective-permute-start | bytes 1179656 | tf_op jit(solution)/shard_map/ppermute | solution.py:295
  51.6 0.7 collective-permute-start.9
  52.3 3.3 %selfatt.1 = (f32[256,384]{1,0:T(8,128)S(1)}, f32[256,384]{1,0:T(8,128)S(1)}, f32[256,384]{1,0:T(8,128)S(1)}, f32[256,384]{1,0:T(8,128)S(1)}, bf16[512,384]{1,0:T(8,128)(2,1)S(1)}, /*index=5*/f32[16,256]{1,0:T(8,128)S(1)}) custom-call(s32[26]{0:T(128)S(1)} %pad_add_fusion.scal, f32[4,16,256]{2,1,0:T(8,128)S(1)} %bitcast.7, f32[2,4,384]{2,1,0:T(4,128)S(1)} %copy-done.6, ...), custom_call_target="tpu_custom_call" | custom-call | flops 905969664 | bytes 3633256 | tf_op jit(solution)/shard_map/selfatt/pallas_call | solution.py:252
  55.6 1.9 %collective-permute-start.10 = (bf16[512,384]{1,0:T(8,128)(2,1)S(1)}, bf16[512,384]{1,0:T(8,128)(2,1)S(1)}, u32[]{:S(2)}, u32[]{:S(2)}) collective-permute-start(bf16[512,384]{1,0:T(8,128)(2,1)S(1)} %get-tuple-element.63), channel_id=1, source_target_pairs={{0,4},{4,0},{8,12},{12,8},{16,20},{20,16},{24,28},{28,24},{32,36},... | collective-permute-start | bytes 1179656 | tf_op jit(solution)/shard_map/ppermute | solution.py:304
  57.6 3.8 %collective-permute-start.6 = (f32[16,256]{1,0:T(8,128)S(1)}, f32[16,256]{1,0:T(8,128)S(1)}, u32[]{:S(2)}, u32[]{:S(2)}) collective-permute-start(f32[16,256]{1,0:T(8,128)S(1)} %get-tuple-element.55), channel_id=1, source_target_pairs={{4,8},{8,4},{12,16},{16,12},{20,24},{24,20},{28,32},{32,28},{36,40... | collective-permute-start | bytes 49160 | tf_op jit(solution)/shard_map/ppermute | solution.py:303
  61.4 0.7 add_convert_fusion
  62.1 2.2 %collective-permute-done.6.stats = f32[16,256]{1,0:T(8,128)S(1)} collective-permute-done((f32[16,256]{1,0:T(8,128)S(1)}, f32[16,256]{1,0:T(8,128)S(1)}, u32[]{:S(2)}, u32[]{:S(2)}) %collective-permute-start.6) | collective-permute-done | bytes 16416 | tf_op jit(solution)/shard_map/ppermute | solution.py:303
  64.3 1.4 %keyside.1 = (f32[256,384]{1,0:T(8,128)S(1)}, f32[256,384]{1,0:T(8,128)S(1)}) custom-call(s32[26]{0:T(128)S(1)} %pad_add_fusion.scal, f32[4,16,256]{2,1,0:T(8,128)S(1)} %bitcast.8, f32[2,4,384]{2,1,0:T(4,128)S(1)} %copy-done.6, bf16[256,384]{1,0:T(8,128)(2,1)S(1)} %copy-done, bf16[256,384]{1,0:T(8,128)(2,1)S(1)} %copy-done.3, ...), custom_call_target="tpu_custom_call" | custom-call | flops 201326592 | bytes 2453608 | tf_op jit(solution)/shard_map/keyside/pallas_call | solution.py:252
  65.7 1.5 %collective-permute-done.8.r0 = bf16[512,384]{1,0:T(8,128)(2,1)S(1)} collective-permute-done((bf16[512,384]{1,0:T(8,128)(2,1)S(1)}, bf16[512,384]{1,0:T(8,128)(2,1)S(1)}, u32[]{:S(2)}, u32[]{:S(2)}) %collective-permute-start.8) | collective-permute-done | bytes 393248 | tf_op jit(solution)/shard_map/ppermute | solution.py:295
  67.2 0.6 collective-permute-done.10.rx
  67.8 1.7 %gather.1 = (bf16[256,384]{1,0:T(8,128)(2,1)}, bf16[256,384]{1,0:T(8,128)(2,1)}, f32[256,384]{1,0:T(8,128)S(1)}, f32[256,384]{1,0:T(8,128)S(1)}, f32[8,256]{1,0:T(8,128)S(1)}) custom-call(s32[26]{0:T(128)S(1)} %pad_add_fusion.scal, f32[2,4,384]{2,1,0:T(4,128)S(1)} %copy-done.6, bf16[256,384]{1,0:T(8,128)(2,1)S(1)} %copy-done.2, ...), custom_call_target="tpu_custom_call" | custom-call | bytes 5132392 | tf_op jit(solution)/shard_map/gather/pallas_call | solution.py:252
  69.5 8.1 %all-gather.1 = f32[32,256]{1,0:T(8,128)S(1)} all-gather(f32[8,256]{1,0:T(8,128)S(1)} %get-tuple-element.64), channel_id=3, replica_groups=mesh['y'=4,'t'=32,'head'=4] {'head'}, dimensions={0}, use_global_device_ids=true | all-gather | bytes 40960 | tf_op jit(solution)/shard_map/all_gather | solution.py:314
  77.6 1.8 %final.1 = (bf16[256,384]{1,0:T(8,128)(2,1)}, bf16[256,384]{1,0:T(8,128)(2,1)}, bf16[256,384]{1,0:T(8,128)(2,1)}, bf16[256,384]{1,0:T(8,128)(2,1)}) custom-call(s32[26]{0:T(128)S(1)} %pad_add_fusion.scal, f32[2,4,384]{2,1,0:T(4,128)S(1)} %copy-done.6, f32[4,16,256]{2,1,0:T(8,128)S(1)} %bitcast.9, f32[4,8,256]{2,1,0:T(8,128)S(1)} %bitcast.10, ...), custom_call_target="tpu_custom_call" | custom-call | bytes 3256424 | tf_op jit(solution)/shard_map/final/pallas_call | solution.py:252
  (30 shorter events, 0.8 us)
Async XLA Ops:
  0.6 1.0 %copy-start.3 = (bf16[256,384]{1,0:T(8,128)(2,1)S(1)}, bf16[256,384]{1,0:T(8,128)(2,1)}, u32[]{:S(2)}) copy-start(bf16[256,384]{1,0:T(8,128)(2,1)} %v_ref.3) | copy-start | bytes 589828
  1.7 2.4 %copy-start.1 = (bf16[256,384]{1,0:T(8,128)(2,1)S(1)}, bf16[256,384]{1,0:T(8,128)(2,1)}, u32[]{:S(2)}) copy-start(bf16[256,384]{1,0:T(8,128)(2,1)} %ck.3) | copy-start | bytes 589828
  1.7 3.1 %copy-start.7 = (bf16[256,384]{1,0:T(8,128)(2,1)S(1)}, bf16[256,384]{1,0:T(8,128)(2,1)}, u32[]{:S(2)}) copy-start(bf16[256,384]{1,0:T(8,128)(2,1)} %param.14) | copy-start | bytes 589828
  1.7 12.0 %collective-permute-start.1 = (bf16[512,384]{1,0:T(8,128)(2,1)S(1)}, bf16[512,384]{1,0:T(8,128)(2,1)S(1)}, u32[]{:S(2)}, u32[]{:S(2)}) collective-permute-start(bf16[512,384]{1,0:T(8,128)(2,1)S(1)} %constant_dynamic-update-slice_fusion.2), channel_id=1, source_target_pairs={{0,4},{4,0},{8,12},{12,8},{16,20},{20,16},{24,28},{28,24},{32,36},... | collective-permute-start | bytes 1179656 | tf_op jit(solution)/shard_map/ppermute | solution.py:277
  4.0 17.9 %copy-start.4 = (bf16[256,384]{1,0:T(8,128)(2,1)S(1)}, bf16[256,384]{1,0:T(8,128)(2,1)}, u32[]{:S(2)}) copy-start(bf16[256,384]{1,0:T(8,128)(2,1)} %cq.3) | copy-start | bytes 589828
  4.0 17.9 %copy-start.5 = (bf16[256,384]{1,0:T(8,128)(2,1)S(1)}, bf16[256,384]{1,0:T(8,128)(2,1)}, u32[]{:S(2)}) copy-start(bf16[256,384]{1,0:T(8,128)(2,1)} %do_ref.3) | copy-start | bytes 589828
  4.7 17.2 %copy-start = (bf16[256,384]{1,0:T(8,128)(2,1)S(1)}, bf16[256,384]{1,0:T(8,128)(2,1)}, u32[]{:S(2)}) copy-start(bf16[256,384]{1,0:T(8,128)(2,1)} %sk.3) | copy-start | bytes 589828
  4.7 17.2 %copy-start.2 = (bf16[256,384]{1,0:T(8,128)(2,1)S(1)}, bf16[256,384]{1,0:T(8,128)(2,1)}, u32[]{:S(2)}) copy-start(bf16[256,384]{1,0:T(8,128)(2,1)} %sq.1) | copy-start | bytes 589828
  5.4 20.8 %collective-permute-start.4 = (bf16[512,384]{1,0:T(8,128)(2,1)}, bf16[512,384]{1,0:T(8,128)(2,1)S(1)}, u32[]{:S(2)}, u32[]{:S(2)}) collective-permute-start(bf16[512,384]{1,0:T(8,128)(2,1)} %constant_dynamic-update-slice_fusion), channel_id=1, source_target_pairs={{384,0},{0,384},{385,1},{1,385},{386,2},{2,386},{387,3},{3,387},{3... | collective-permute-start | bytes 1179656 | tf_op jit(solution)/shard_map/ppermute | solution.py:279
  10.1 16.2 %collective-permute-start.3 = (bf16[512,384]{1,0:T(8,128)(2,1)}, bf16[512,384]{1,0:T(8,128)(2,1)S(1)}, u32[]{:S(2)}, u32[]{:S(2)}) collective-permute-start(bf16[512,384]{1,0:T(8,128)(2,1)} %constant_dynamic-update-slice_fusion), channel_id=1, source_target_pairs={{384,128},{128,384},{385,129},{129,385},{386,130},{130,386},{387,1... | collective-permute-start | bytes 1179656 | tf_op jit(solution)/shard_map/ppermute | solution.py:278
  10.8 15.5 %collective-permute-start = (bf16[512,384]{1,0:T(8,128)(2,1)}, bf16[512,384]{1,0:T(8,128)(2,1)S(1)}, u32[]{:S(2)}, u32[]{:S(2)}) collective-permute-start(bf16[512,384]{1,0:T(8,128)(2,1)} %constant_dynamic-update-slice_fusion), channel_id=1, source_target_pairs={{384,256},{256,384},{385,257},{257,385},{386,258},{258,386},{387,2... | collective-permute-start | bytes 1179656 | tf_op jit(solution)/shard_map/ppermute | solution.py:282
  13.7 13.1 %collective-permute-start.2 = (bf16[512,384]{1,0:T(8,128)(2,1)S(1)}, bf16[512,384]{1,0:T(8,128)(2,1)S(1)}, u32[]{:S(2)}, u32[]{:S(2)}) collective-permute-start(bf16[512,384]{1,0:T(8,128)(2,1)S(1)} %constant_dynamic-update-slice_fusion.2), channel_id=1, source_target_pairs={{4,8},{8,4},{12,16},{16,12},{20,24},{24,20},{28,32},{32,28},{36,40... | collective-permute-start | bytes 1179656 | tf_op jit(solution)/shard_map/ppermute | solution.py:281
  18.4 0.7 copy-start.8
  19.2 2.7 %copy-start.6 = (f32[2,4,384]{2,1,0:T(4,128)S(1)}, f32[2,4,384]{2,1,0:T(4,128)}, u32[]{:S(2)}) copy-start(f32[2,4,384]{2,1,0:T(4,128)} %gains.9) | copy-start | bytes 36868
  21.2 0.7 copy-start.9
  38.2 19.4 %collective-permute-start.5 = (bf16[512,384]{1,0:T(8,128)(2,1)S(1)}, bf16[512,384]{1,0:T(8,128)(2,1)S(1)}, u32[]{:S(2)}, u32[]{:S(2)}) collective-permute-start(bf16[512,384]{1,0:T(8,128)(2,1)S(1)} %pad_maximum_fusion), channel_id=1, source_target_pairs={{4,8},{8,4},{12,16},{16,12},{20,24},{24,20},{28,32},{32,28},{36,40... | collective-permute-start | bytes 1179656 | tf_op jit(solution)/shard_map/ppermute | solution.py:297
  42.9 22.8 %collective-permute-start.7 = (bf16[512,384]{1,0:T(8,128)(2,1)S(1)}, bf16[512,384]{1,0:T(8,128)(2,1)S(1)}, u32[]{:S(2)}, u32[]{:S(2)}) collective-permute-start(bf16[512,384]{1,0:T(8,128)(2,1)S(1)} %get-tuple-element.60), channel_id=1, source_target_pairs={{384,128},{128,384},{385,129},{129,385},{386,130},{130,386},{387,1... | collective-permute-start | bytes 1179656 | tf_op jit(solution)/shard_map/ppermute | solution.py:295
  43.6 23.6 %collective-permute-start.8 = (bf16[512,384]{1,0:T(8,128)(2,1)S(1)}, bf16[512,384]{1,0:T(8,128)(2,1)S(1)}, u32[]{:S(2)}, u32[]{:S(2)}) collective-permute-start(bf16[512,384]{1,0:T(8,128)(2,1)S(1)} %get-tuple-element.61), channel_id=1, source_target_pairs={{384,0},{0,384},{385,1},{1,385},{386,2},{2,386},{387,3},{3,387},{3... | collective-permute-start | bytes 1179656 | tf_op jit(solution)/shard_map/ppermute | solution.py:295
  51.6 15.6 %collective-permute-start.9 = (bf16[512,384]{1,0:T(8,128)(2,1)S(1)}, bf16[512,384]{1,0:T(8,128)(2,1)S(1)}, u32[]{:S(2)}, u32[]{:S(2)}) collective-permute-start(bf16[512,384]{1,0:T(8,128)(2,1)S(1)} %get-tuple-element.62), channel_id=1, source_target_pairs={{384,256},{256,384},{385,257},{257,385},{386,258},{258,386},{387,2... | collective-permute-start | bytes 1179656 | tf_op jit(solution)/shard_map/ppermute | solution.py:295
  55.6 12.2 %collective-permute-start.10 = (bf16[512,384]{1,0:T(8,128)(2,1)S(1)}, bf16[512,384]{1,0:T(8,128)(2,1)S(1)}, u32[]{:S(2)}, u32[]{:S(2)}) collective-permute-start(bf16[512,384]{1,0:T(8,128)(2,1)S(1)} %get-tuple-element.63), channel_id=1, source_target_pairs={{0,4},{4,0},{8,12},{12,8},{16,20},{20,16},{24,28},{28,24},{32,36},... | collective-permute-start | bytes 1179656 | tf_op jit(solution)/shard_map/ppermute | solution.py:304
  57.6 6.7 %collective-permute-start.6 = (f32[16,256]{1,0:T(8,128)S(1)}, f32[16,256]{1,0:T(8,128)S(1)}, u32[]{:S(2)}, u32[]{:S(2)}) collective-permute-start(f32[16,256]{1,0:T(8,128)S(1)} %get-tuple-element.55), channel_id=1, source_target_pairs={{4,8},{8,4},{12,16},{16,12},{20,24},{24,20},{28,32},{32,28},{36,40... | collective-permute-start | bytes 49160 | tf_op jit(solution)/shard_map/ppermute | solution.py:303
